TPU v7x, 512 devices: a whole 4x8x8 slice. The times are simulated.
512 devices in a mesh: dp: 128 (over z_lo, y, x, core), mp: 4 (over z_hi).
Axes of the slice: x: 4, y: 8, z: 8 (z_hi: 4, z_lo: 2; z = z_hi * 2 + z_lo), core: 2. Of those that a mesh axis runs over, the one named last changes fastest.
Arguments:
- tokens: bfloat16 [4096, 4096], P('mp'), may hold values from -6 to 6
- gate_pre: bfloat16 [4096, 16384], P('mp', 'dp'), may hold values from -8 to 8
- up_value: bfloat16 [4096, 16384], P('mp', 'dp'), may hold values from -6 to 6
- grad_hidden: bfloat16 [4096, 16384], P('mp', 'dp'), may hold values from -6 to 6
- gate_weight: bfloat16 [4096, 16384], P('mp', 'dp'), may hold values from -0.1875 to 0.1875
Outputs:
- grad_tokens: bfloat16 [4096, 4096], P('mp', 'dp')
- grad_gate_weight: bfloat16 [4096, 16384], P('mp', 'dp')
All inputs are finite; a program needn't handle non-finite values.
Results may differ from a plain program's by a relative error of at most 0.0049.
Values may be sent and summed in bfloat16 or wider, within the bound.
No kernel may reach another device: no remote copies, remote signals or barrier semaphores. Data moves between devices by JAX's collectives and lax.ppermute only.
A program may use at most 128 MiB of HBM per device.

v0:
```python
import jax
import jax.numpy as jnp
from jax import lax
from jax.sharding import PartitionSpec as P


def body(tokens, gate_pre, up_value, grad_hidden, gate_weight):
    gate = gate_pre.astype(jnp.float32)
    sigma = jax.nn.sigmoid(gate)
    grad_gate = (
        grad_hidden.astype(jnp.float32)
        * up_value.astype(jnp.float32)
        * sigma
        * (1.0 + gate * (1.0 - sigma))
    ).astype(jnp.bfloat16)
    total_tokens = tokens.shape[0] * lax.axis_size("mp")
    norm_factor = float(total_tokens) ** (-0.5)
    partial_sums = lax.dot_general(
        grad_gate,
        lax.all_gather(gate_weight, "mp", axis=0, tiled=True),
        (((1,), (1,)), ((), ())),
        preferred_element_type=jnp.float32,
    )
    grad_tokens = lax.psum_scatter(partial_sums, "dp", scatter_dimension=1, tiled=True).astype(
        jnp.bfloat16
    )
    summed = lax.psum_scatter(
        lax.dot_general(
            tokens, grad_gate, (((0,), (0,)), ((), ())), preferred_element_type=jnp.float32
        ),
        "mp",
        scatter_dimension=0,
        tiled=True,
    )
    grad_gate_weight = (summed * norm_factor).astype(jnp.bfloat16)
    return (grad_tokens, grad_gate_weight)


def solution(mesh):
    in_specs = (P("mp", None), P("mp", "dp"), P("mp", "dp"), P("mp", "dp"), P("mp", "dp"))
    out_specs = (P("mp", "dp"), P("mp", "dp"))
    return jax.shard_map(body, mesh=mesh, in_specs=in_specs, out_specs=out_specs, check_vma=False)
```

profile of v0, /device:TPU:128, one launch (start us, length us, event | category | flops | bytes accessed | tf_op | source)
XLA Modules:
  0.0 710.0 jit_solution(8973049107877025127)
XLA Ops:
  7.2 0.0 all-gather.2.cloned.1.call-start
  7.2 0.7 all-gather.2.cloned.1.call-update
  7.9 0.0 copy-start
  7.9 0.0 copy-start.1
  7.9 0.0 copy-start.2
  7.9 0.0 reduce-scatter.5.cloned.1.call-start
  8.0 6.5 convolution_bitcast_fusion
  14.5 0.0 reduce-scatter.5.cloned.1.call-update
  14.5 0.0 reduce-scatter.3.cloned.1.call-start
  14.6 36.0 %all-gather.2.cloned.1.call-done = bf16[4096,128]{1,0:T(8,128)(2,1)} async-done(((bf16[1024,128]{1,0:T(8,128)(2,1)}), bf16[4096,128]{1,0:T(8,128)(2,1)}) %all-gather.2.cloned.1.call-update) | async-done | bytes 1048592 | tf_op jit(solution)/shard_map/all_gather | solution.py:20
  50.6 0.0 copy-done
  50.6 0.0 copy-done.1
  50.6 0.0 copy-done.2
  50.6 9.4 %fusion.7 = f32[1024,4096]{0,1:T(8,128)} fusion(bf16[4096,128]{1,0:T(8,128)(2,1)} %all-gather.2.cloned.1.call-done, bf16[1024,128]{1,0:T(8,128)(2,1)S(1)} %copy-done, bf16[1024,128]{1,0:T(8,128)(2,1)S(1)} %copy-done.1, bf16[1024,128]{1,0:T(8,128)(2,1)S(1)} %copy-done.2), kind=kOutput, calls=%fused_computation.10 | convolution fusion | flops 1075445760 | bytes 18612224 | tf_op jit(solution)/shard_map/dot_general | solution.py:18
  60.0 0.0 reduce-scatter.3.cloned.1.call-update
  60.0 45.7 %reduce-scatter.5.cloned.1.call-done = f32[1024,128]{0,1:T(8,128)} async-done(((f32[4096,128]{0,1:T(8,128)}), f32[1024,128]{0,1:T(8,128)}) %reduce-scatter.5.cloned.1.call-update) | async-done | bytes 524304 | tf_op jit(solution)/shard_map/reduce_scatter | solution.py:27
  105.7 1.1 multiply_convert_fusion
  106.8 0.8 copy.7
  107.6 594.3 %reduce-scatter.3.cloned.1.call-done = f32[1024,32]{0,1:T(8,128)} async-done(((f32[1024,4096]{0,1:T(8,128)}), f32[1024,32]{0,1:T(8,128)}) %reduce-scatter.3.cloned.1.call-update) | async-done | bytes 131088 | tf_op jit(solution)/shard_map/reduce_scatter | solution.py:24
  701.9 1.5 convert_element_type.22
Async XLA Ops:
  7.2 43.4 %all-gather.2.cloned.1.call-start = ((), (), s32[]{:S(2)}) async-start(), calls=%async_computation.2 | async-start | bytes 1310720 | tf_op jit(solution)/shard_map/all_gather | solution.py:20
  7.9 42.7 %copy-start = (bf16[1024,128]{1,0:T(8,128)(2,1)S(1)}, bf16[1024,128]{1,0:T(8,128)(2,1)}, u32[]{:S(2)}) copy-start(bf16[1024,128]{1,0:T(8,128)(2,1)} %param.6) | copy-start | bytes 786436
  7.9 42.7 %copy-start.1 = (bf16[1024,128]{1,0:T(8,128)(2,1)S(1)}, bf16[1024,128]{1,0:T(8,128)(2,1)}, u32[]{:S(2)}) copy-start(bf16[1024,128]{1,0:T(8,128)(2,1)} %param.7) | copy-start | bytes 786436
  7.9 42.6 %copy-start.2 = (bf16[1024,128]{1,0:T(8,128)(2,1)S(1)}, bf16[1024,128]{1,0:T(8,128)(2,1)}, u32[]{:S(2)}) copy-start(bf16[1024,128]{1,0:T(8,128)(2,1)} %param.8) | copy-start | bytes 786436
  7.9 97.8 %reduce-scatter.5.cloned.1.call-start = ((), (), s32[]{:S(2)}) async-start(), calls=%async_computation.4 | async-start | bytes 2621440 | tf_op jit(solution)/shard_map/reduce_scatter | solution.py:27
  14.5 687.4 %reduce-scatter.3.cloned.1.call-start = ((), (), s32[]{:S(2)}) async-start(), calls=%async_computation.3 | async-start | bytes 16908288 | tf_op jit(solution)/shard_map/reduce_scatter | solution.py:24
Sparse Core Ops, SparseCore 0:
  10.1 40.4 all-gather.1
  53.4 52.2 reduce-scatter.4
  108.8 593.0 reduce-scatter.2
where the time goes:
time: 710 us
  waiting for transfers between devices  677 us (95%)
  matrix products  15.9 us (2%)
  between operations  13.8 us (2%)
    reduce_scatter x1, waiting for transfers between devices, body(): lax.psum_scatter(partial_sums, 'dp', scatter_dimension=1, tiled=True)  594 us
    reduce_scatter x1, waiting for transfers between devices, body(): lax.psum_scatter(lax.dot_general(tokens, grad_gate, (((0,), (0,)), ((), (...  45.7 us
    all_gather x1, waiting for transfers between devices, body(): lax.all_gather(gate_weight, 'mp', axis=0, tiled=True)  36 us
  transfers between devices with their start and end apart: 3, of which 3 were waited for; matrix products, arithmetic and copies ran while one was open for 3% of the time, Pallas kernels for 0%

commit v1 on v0

v1 whole, which is shorter than its diff:
```python
import jax
import jax.numpy as jnp
from jax import lax
from jax.experimental import pallas as pl
from jax.experimental.pallas import tpu as pltpu
from jax.sharding import Mesh, PartitionSpec as P

AXES = ("zl", "y", "x", "c", "mp")
STEP = 256


def shift(array, axis, size, by):
    return lax.ppermute(array, axis, [((i + by) % size, i) for i in range(size)])


def partial_kernel(order, rows_ref, *refs):
    gates, out_ref, rows, block = refs[:8], refs[8], refs[9], refs[10]

    @pl.when(pl.program_id(0) == 0)
    def _():
        for k in range(8):
            for m in range(4):
                rows[m * 128 : (m + 1) * 128, k * 128 : (k + 1) * 128] = rows_ref[m, order[k]]

    for k in range(8):
        block[:, k * 128 : (k + 1) * 128] = gates[k][...]
    out_ref[...] = lax.dot_general(
        rows[...], block[...], (((1,), (1,)), ((), ())), preferred_element_type=jnp.float32
    ).astype(jnp.bfloat16)


def partial_product(order, rows, gates):
    return pl.pallas_call(
        partial_kernel,
        grid_spec=pltpu.PrefetchScalarGridSpec(
            num_scalar_prefetch=1,
            grid=(1024 // STEP,),
            in_specs=[pl.BlockSpec((4, 8, 128, 128), lambda t, order: (0, 0, 0, 0))]
            + [pl.BlockSpec((STEP, 128), lambda t, order: (t, 0))] * 8,
            out_specs=pl.BlockSpec((512, STEP), lambda t, order: (0, t)),
            scratch_shapes=[
                pltpu.VMEM((512, 1024), jnp.bfloat16),
                pltpu.VMEM((STEP, 1024), jnp.bfloat16),
            ],
        ),
        out_shape=jax.ShapeDtypeStruct((512, 1024), jnp.bfloat16),
        compiler_params=pltpu.CompilerParams(vmem_limit_bytes=16 << 20),
        cost_estimate=pl.CostEstimate(flops=1 << 30, bytes_accessed=4 << 20, transcendentals=0),
    )(order, rows, *gates)


def sum_kernel(pieces_ref, out_ref):
    out_ref[...] = jnp.sum(pieces_ref[...].astype(jnp.float32), axis=0).astype(jnp.bfloat16)


def sum_pieces(pieces):
    return pl.pallas_call(
        sum_kernel,
        out_shape=jax.ShapeDtypeStruct(pieces.shape[1:], jnp.bfloat16),
        in_specs=[pl.BlockSpec(memory_space=pltpu.VMEM)],
        out_specs=pl.BlockSpec(memory_space=pltpu.VMEM),
    )(pieces)


def body(tokens, gate_pre, up_value, grad_hidden, gate_weight):
    rows = gate_weight.reshape(4, 8, 32, 128).swapaxes(0, 1).reshape(1, 8, 128, 128)
    rows = jnp.broadcast_to(rows, (4, 8, 128, 128)).reshape(32, 128, 128)
    rows = lax.all_to_all(rows, ("mp", "x", "c"), 0, 0, tiled=True).reshape(4, 8, 128, 128)

    gate = gate_pre.astype(jnp.float32)
    sigma = jax.nn.sigmoid(gate)
    grad_gate = (
        grad_hidden.astype(jnp.float32)
        * up_value.astype(jnp.float32)
        * sigma
        * (1.0 + gate * (1.0 - sigma))
    ).astype(jnp.bfloat16)
    total_tokens = tokens.shape[0] * lax.axis_size("mp")
    norm_factor = float(total_tokens) ** (-0.5)

    mine = [grad_gate] + [shift(grad_gate, "x", 4, k) for k in (1, 3, 2)]
    other = [shift(block, "c", 2, 1) for block in mine]
    x, c = lax.axis_index("x"), lax.axis_index("c")
    order = jnp.stack(
        [((x + k) & 3) * 2 + c for k in (0, 1, 3, 2)] + [((x + k) & 3) * 2 + 1 - c for k in (0, 1, 3, 2)]
    ).astype(jnp.int32)
    partial_sums = partial_product(order, rows, mine + other)
    pieces = lax.all_to_all(partial_sums.reshape(16, 32, 1024), ("zl", "y"), 0, 0, tiled=True)
    grad_tokens = sum_pieces(pieces).T

    share = lax.dot_general(
        grad_gate, tokens, (((0,), (0,)), ((), ())), preferred_element_type=jnp.float32
    )
    m = lax.axis_index("mp")
    summed = lax.dynamic_slice_in_dim(share, m * 1024, 1024, axis=1)
    for k in (1, 3, 2):
        away = lax.dynamic_slice_in_dim(share, ((m + k) & 3) * 1024, 1024, axis=1).astype(jnp.bfloat16)
        summed = summed + shift(away, "mp", 4, -k).astype(jnp.float32)
    grad_gate_weight = (summed * norm_factor).astype(jnp.bfloat16).T
    return (grad_tokens, grad_gate_weight)


def solution(mesh):
    fine = Mesh(mesh.devices.reshape(2, 8, 4, 2, 4), AXES)
    dp = ("zl", "y", "x", "c")
    in_specs = (P("mp", None), P("mp", dp), P("mp", dp), P("mp", dp), P("mp", dp))
    out_specs = (P("mp", dp), P("mp", dp))
    return jax.shard_map(body, mesh=fine, in_specs=in_specs, out_specs=out_specs, check_vma=False)
```

time: 710 us -> 112 us (0.16)
  the two profiles are of different devices: /device:TPU:128 before, /device:TPU:8 now
where the time goes in v1:
time: 112 us; the launch traced here: 111 us
  starting transfers between devices  55.6 us (50%)
  waiting for transfers between devices  36.9 us (33%)
  Pallas kernels  5.83 us (5%)
  local copies, waits for them, and re-layouts  5.03 us (4%)
  matrix products  4.66 us (4%)
  other arithmetic  2.62 us (2%)
    ppermute x10, waiting for transfers between devices, shift(): lax.ppermute(array, axis, [((i + by) % size, i) for i in range(size)])  36.9 us
    ppermute x10, starting transfers between devices, shift(): lax.ppermute(array, axis, [((i + by) % size, i) for i in range(size)])  34.5 us
    all_to_all x1, starting transfers between devices, body(): lax.all_to_all(rows, ('mp', 'x', 'c'), 0, 0, tiled=True)  13.2 us
    all_to_all x1, starting transfers between devices, body(): lax.all_to_all(partial_sums.reshape(16, 32, 1024), ('zl', 'y'), 0, 0, til...  7.95 us
    dot_general x1, matrix products, body(): lax.dot_general(grad_gate, tokens, (((0,), (0,)), ((), ())), preferred_el...  4.66 us
    pallas_call x1, Pallas kernels, partial_product(): pl.pallas_call(partial_kernel, grid_spec=pltpu.PrefetchScalarGridSpec(num...  3.84 us
  transfers between devices with their start and end apart: 12, of which 5 were waited for; matrix products, arithmetic and copies ran while one was open for 8% of the time, Pallas kernels for 0%

profile of v1, /device:TPU:8, one launch (start us, length us, event | category | flops | bytes accessed | tf_op | source)
XLA Modules:
  0.0 111.4 jit_solution(2434575075816712872)
XLA Ops:
  0.6 1.0 copy.9
  1.6 1.2 %broadcast_in_dim.8 = bf16[4,8,128,128]{3,2,1,0:T(8,128)(2,1)} broadcast(bf16[8,128,128]{2,1,0:T(8,128)(2,1)S(1)} %bitcast.21), dimensions={1,2,3} | broadcast | bytes 1310720 | tf_op jit(solution)/shard_map/broadcast_in_dim | solution.py:67
  2.8 13.2 %all-to-all-start = ((bf16[32,128,128]{2,1,0:T(8,128)(2,1)}), bf16[32,128,128]{2,1,0:T(8,128)(2,1)S(1)}, u32[]{:S(2)}, u32[]{:S(2)}) async-start(bf16[32,128,128]{2,1,0:T(8,128)(2,1)} %bitcast.11), calls=%async_computation | async-start | bytes 2097152 | tf_op jit(solution)/shard_map/all_to_all | solution.py:68
  16.0 1.4 %fusion.5.refs_0_ = bf16[1024,128]{1,0:T(8,128)(2,1)S(1)} fusion(bf16[1024,128]{1,0:T(8,128)(2,1)} %param.6, bf16[1024,128]{1,0:T(8,128)(2,1)} %param.7, bf16[1024,128]{1,0:T(8,128)(2,1)} %param.8), kind=kLoop, calls=%fused_computation.7 | loop fusion | flops 1703936 | bytes 1048576 | tf_op jit(solution)/shard_map/convert_element_type | solution.py:77
  17.3 4.9 %collective-permute-start = (bf16[1024,128]{1,0:T(8,128)(2,1)S(1)}, bf16[1024,128]{1,0:T(8,128)(2,1)S(1)}, u32[]{:S(2)}, u32[]{:S(2)}) collective-permute-start(bf16[1024,128]{1,0:T(8,128)(2,1)S(1)} %fusion.5.refs_0_), channel_id=1, source_target_pairs={{8,0},{16,8},{24,16},{0,24},{9,1},{17,9},{25,17},{1,25},{10,2},{18... | collective-permute-start | bytes 786440 | tf_op jit(solution)/shard_map/ppermute | solution.py:13
  22.3 1.9 %collective-permute-start.1 = (bf16[1024,128]{1,0:T(8,128)(2,1)S(1)}, bf16[1024,128]{1,0:T(8,128)(2,1)S(1)}, u32[]{:S(2)}, u32[]{:S(2)}) collective-permute-start(bf16[1024,128]{1,0:T(8,128)(2,1)S(1)} %fusion.5.refs_0_), channel_id=1, source_target_pairs={{24,0},{0,8},{8,16},{16,24},{25,1},{1,9},{9,17},{17,25},{26,2},{2,... | collective-permute-start | bytes 786440 | tf_op jit(solution)/shard_map/ppermute | solution.py:13
  24.2 4.2 %collective-permute-start.2 = (bf16[1024,128]{1,0:T(8,128)(2,1)S(1)}, bf16[1024,128]{1,0:T(8,128)(2,1)S(1)}, u32[]{:S(2)}, u32[]{:S(2)}) collective-permute-start(bf16[1024,128]{1,0:T(8,128)(2,1)S(1)} %fusion.5.refs_0_), channel_id=1, source_target_pairs={{16,0},{24,8},{0,16},{8,24},{17,1},{25,9},{1,17},{9,25},{18,2},{26... | collective-permute-start | bytes 786440 | tf_op jit(solution)/shard_map/ppermute | solution.py:13
  28.4 1.9 %collective-permute-start.3 = (bf16[1024,128]{1,0:T(8,128)(2,1)S(1)}, bf16[1024,128]{1,0:T(8,128)(2,1)S(1)}, u32[]{:S(2)}, u32[]{:S(2)}) collective-permute-start(bf16[1024,128]{1,0:T(8,128)(2,1)S(1)} %fusion.5.refs_0_), channel_id=1, source_target_pairs={{4,0},{0,4},{5,1},{1,5},{6,2},{2,6},{7,3},{3,7},{12,8},{8,12},{13,... | collective-permute-start | bytes 786440 | tf_op jit(solution)/shard_map/ppermute | solution.py:13
  30.3 5.0 %collective-permute-done.refs_1_ = bf16[1024,128]{1,0:T(8,128)(2,1)S(1)} collective-permute-done((bf16[1024,128]{1,0:T(8,128)(2,1)S(1)}, bf16[1024,128]{1,0:T(8,128)(2,1)S(1)}, u32[]{:S(2)}, u32[]{:S(2)}) %collective-permute-start) | collective-permute-done | bytes 262176 | tf_op jit(solution)/shard_map/ppermute | solution.py:13
  35.3 1.9 %collective-permute-start.4 = (bf16[1024,128]{1,0:T(8,128)(2,1)S(1)}, bf16[1024,128]{1,0:T(8,128)(2,1)S(1)}, u32[]{:S(2)}, u32[]{:S(2)}) collective-permute-start(bf16[1024,128]{1,0:T(8,128)(2,1)S(1)} %collective-permute-done.refs_1_), channel_id=1, source_target_pairs={{4,0},{0,4},{5,1},{1,5},{6,2},{2,6},{7,3},{3,7},{12,8},{8,12},{13,... | collective-permute-start | bytes 786440 | tf_op jit(solution)/shard_map/ppermute | solution.py:13
  37.2 7.8 %collective-permute-done.1.refs_2_ = bf16[1024,128]{1,0:T(8,128)(2,1)S(1)} collective-permute-done((bf16[1024,128]{1,0:T(8,128)(2,1)S(1)}, bf16[1024,128]{1,0:T(8,128)(2,1)S(1)}, u32[]{:S(2)}, u32[]{:S(2)}) %collective-permute-start.1) | collective-permute-done | bytes 262176 | tf_op jit(solution)/shard_map/ppermute | solution.py:13
  45.0 1.9 %collective-permute-start.5 = (bf16[1024,128]{1,0:T(8,128)(2,1)S(1)}, bf16[1024,128]{1,0:T(8,128)(2,1)S(1)}, u32[]{:S(2)}, u32[]{:S(2)}) collective-permute-start(bf16[1024,128]{1,0:T(8,128)(2,1)S(1)} %collective-permute-done.1.refs_2_), channel_id=1, source_target_pairs={{4,0},{0,4},{5,1},{1,5},{6,2},{2,6},{7,3},{3,7},{12,8},{8,12},{13,... | collective-permute-start | bytes 786440 | tf_op jit(solution)/shard_map/ppermute | solution.py:13
  47.0 0.0 collective-permute-done.2.refs_3_
  47.0 2.4 %collective-permute-start.6 = (bf16[1024,128]{1,0:T(8,128)(2,1)S(1)}, bf16[1024,128]{1,0:T(8,128)(2,1)S(1)}, u32[]{:S(2)}, u32[]{:S(2)}) collective-permute-start(bf16[1024,128]{1,0:T(8,128)(2,1)S(1)} %collective-permute-done.2.refs_3_), channel_id=1, source_target_pairs={{4,0},{0,4},{5,1},{1,5},{6,2},{2,6},{7,3},{3,7},{12,8},{8,12},{13,... | collective-permute-start | bytes 786440 | tf_op jit(solution)/shard_map/ppermute | solution.py:13
  49.4 0.1 stack.35.order
  49.5 0.0 collective-permute-done.3.refs_4_
  49.5 0.0 collective-permute-done.4.refs_5_
  49.5 0.0 collective-permute-done.5.refs_6_
  49.5 1.0 collective-permute-done.6.refs_7_
  50.5 0.0 all-to-all-done
  50.5 3.8 %shard_map.68 = bf16[512,1024]{1,0:T(8,128)(2,1)} custom-call(s32[8]{0:T(128)S(1)} %stack.35.order, bf16[4,8,128,128]{3,2,1,0:T(8,128)(2,1)S(1)} %bitcast.20, bf16[1024,128]{1,0:T(8,128)(2,1)S(1)} %fusion.5.refs_0_, bf16[1024,128]{1,0:T(8,128)(2,1)S(1)} %collective-permute-done.refs_1_, bf16[1024,128]{1,0:T(8,128)(2,1)S(1)} %collective-permute-done.1.refs_2_, ...), custom_call_target="tpu_custom_call" | custom-call | flops 1073741824 | bytes 4194304 | tf_op jit(solution)/shard_map/pallas_call | solution.py:33
  54.4 7.9 %all-to-all-start.1 = ((bf16[16,32,1024]{2,1,0:T(8,128)(2,1)}), bf16[16,32,1024]{2,1,0:T(8,128)(2,1)S(1)}, u32[]{:S(2)}, u32[]{:S(2)}) async-start(bf16[16,32,1024]{2,1,0:T(8,128)(2,1)} %bitcast.13), calls=%async_computation.1 | async-start | bytes 2097152 | tf_op jit(solution)/shard_map/all_to_all | solution.py:88
  62.3 4.7 %fusion.7 = f32[128,4096]{1,0:T(8,128)S(1)} fusion(bf16[1024,128]{1,0:T(8,128)(2,1)S(1)} %fusion.5.refs_0_, bf16[1024,4096]{1,0:T(8,128)(2,1)} %param.5), kind=kOutput, calls=%fused_computation.13 | convolution fusion | flops 1073741824 | bytes 10747904 | tf_op jit(solution)/shard_map/dot_general | solution.py:91
  67.0 0.9 dynamic-slice_convert_fusion.2
  67.9 8.5 %collective-permute-start.9 = (bf16[128,1024]{1,0:T(8,128)(2,1)}, bf16[128,1024]{1,0:T(8,128)(2,1)}, u32[]{:S(2)}, u32[]{:S(2)}) collective-permute-start(bf16[128,1024]{1,0:T(8,128)(2,1)} %get-tuple-element.9), channel_id=1, source_target_pairs={{2,0},{3,1},{0,2},{1,3},{6,4},{7,5},{4,6},{5,7},{10,8},{11,9},{8,1... | collective-permute-start | bytes 786440 | tf_op jit(solution)/shard_map/ppermute | solution.py:13
  76.5 2.8 %collective-permute-start.8 = (bf16[128,1024]{1,0:T(8,128)(2,1)}, bf16[128,1024]{1,0:T(8,128)(2,1)}, u32[]{:S(2)}, u32[]{:S(2)}) collective-permute-start(bf16[128,1024]{1,0:T(8,128)(2,1)} %get-tuple-element.10), channel_id=1, source_target_pairs={{1,0},{2,1},{3,2},{0,3},{5,4},{6,5},{7,6},{4,7},{9,8},{10,9},{11,1... | collective-permute-start | bytes 786440 | tf_op jit(solution)/shard_map/ppermute | solution.py:13
  79.3 3.9 %collective-permute-start.7 = (bf16[128,1024]{1,0:T(8,128)(2,1)S(1)}, bf16[128,1024]{1,0:T(8,128)(2,1)}, u32[]{:S(2)}, u32[]{:S(2)}) collective-permute-start(bf16[128,1024]{1,0:T(8,128)(2,1)S(1)} %get-tuple-element.8), channel_id=1, source_target_pairs={{3,0},{0,1},{1,2},{2,3},{7,4},{4,5},{5,6},{6,7},{11,8},{8,9},{9,10... | collective-permute-start | bytes 786440 | tf_op jit(solution)/shard_map/ppermute | solution.py:13
  83.2 19.4 %collective-permute-done.9 = bf16[128,1024]{1,0:T(8,128)(2,1)} collective-permute-done((bf16[128,1024]{1,0:T(8,128)(2,1)}, bf16[128,1024]{1,0:T(8,128)(2,1)}, u32[]{:S(2)}, u32[]{:S(2)}) %collective-permute-start.9) | collective-permute-done | bytes 262176 | tf_op jit(solution)/shard_map/ppermute | solution.py:13
  102.6 0.0 collective-permute-done.8
  102.6 3.8 %collective-permute-done.7 = bf16[128,1024]{1,0:T(8,128)(2,1)} collective-permute-done((bf16[128,1024]{1,0:T(8,128)(2,1)S(1)}, bf16[128,1024]{1,0:T(8,128)(2,1)}, u32[]{:S(2)}, u32[]{:S(2)}) %collective-permute-start.7) | collective-permute-done | bytes 262176 | tf_op jit(solution)/shard_map/ppermute | solution.py:13
  106.4 1.3 %fusion.6 = bf16[1024,128]{0,1:T(8,128)(2,1)S(1)} fusion(bf16[128,1024]{1,0:T(8,128)(2,1)} %collective-permute-done.9, bf16[128,1024]{1,0:T(8,128)(2,1)} %collective-permute-done.8, bf16[128,1024]{1,0:T(8,128)(2,1)} %collective-permute-done.7, f32[128,4096]{1,0:T(8,128)S(1)} %fusion.7, s32[]{:T(128)S(6)} %select_n.12), kind=kLoop, calls=%fused_computation.12 | loop fusion | flops 1048576 | bytes 1572868 | tf_op jit(solution)/shard_map/transpose | solution.py:99
  107.6 0.8 copy.10
  108.5 0.0 all-to-all-done.1.pieces_ref
  108.5 0.0 copy-start
  108.5 1.0 copy-done
  109.4 2.0 %shard_map.69 = bf16[32,1024]{1,0:T(8,128)(2,1)} custom-call(bf16[16,32,1024]{2,1,0:T(8,128)(2,1)} %copy-done), custom_call_target="tpu_custom_call" | custom-call | tf_op jit(solution)/shard_map/pallas_call | solution.py:57
Async XLA Ops:
  2.8 47.7 %all-to-all-start = ((bf16[32,128,128]{2,1,0:T(8,128)(2,1)}), bf16[32,128,128]{2,1,0:T(8,128)(2,1)S(1)}, u32[]{:S(2)}, u32[]{:S(2)}) async-start(bf16[32,128,128]{2,1,0:T(8,128)(2,1)} %bitcast.11), calls=%async_computation | async-start | bytes 2097152 | tf_op jit(solution)/shard_map/all_to_all | solution.py:68
  17.3 18.0 %collective-permute-start = (bf16[1024,128]{1,0:T(8,128)(2,1)S(1)}, bf16[1024,128]{1,0:T(8,128)(2,1)S(1)}, u32[]{:S(2)}, u32[]{:S(2)}) collective-permute-start(bf16[1024,128]{1,0:T(8,128)(2,1)S(1)} %fusion.5.refs_0_), channel_id=1, source_target_pairs={{8,0},{16,8},{24,16},{0,24},{9,1},{17,9},{25,17},{1,25},{10,2},{18... | collective-permute-start | bytes 786440 | tf_op jit(solution)/shard_map/ppermute | solution.py:13
  22.3 22.8 %collective-permute-start.1 = (bf16[1024,128]{1,0:T(8,128)(2,1)S(1)}, bf16[1024,128]{1,0:T(8,128)(2,1)S(1)}, u32[]{:S(2)}, u32[]{:S(2)}) collective-permute-start(bf16[1024,128]{1,0:T(8,128)(2,1)S(1)} %fusion.5.refs_0_), channel_id=1, source_target_pairs={{24,0},{0,8},{8,16},{16,24},{25,1},{1,9},{9,17},{17,25},{26,2},{2,... | collective-permute-start | bytes 786440 | tf_op jit(solution)/shard_map/ppermute | solution.py:13
  24.2 22.8 %collective-permute-start.2 = (bf16[1024,128]{1,0:T(8,128)(2,1)S(1)}, bf16[1024,128]{1,0:T(8,128)(2,1)S(1)}, u32[]{:S(2)}, u32[]{:S(2)}) collective-permute-start(bf16[1024,128]{1,0:T(8,128)(2,1)S(1)} %fusion.5.refs_0_), channel_id=1, source_target_pairs={{16,0},{24,8},{0,16},{8,24},{17,1},{25,9},{1,17},{9,25},{18,2},{26... | collective-permute-start | bytes 786440 | tf_op jit(solution)/shard_map/ppermute | solution.py:13
  28.4 21.1 %collective-permute-start.3 = (bf16[1024,128]{1,0:T(8,128)(2,1)S(1)}, bf16[1024,128]{1,0:T(8,128)(2,1)S(1)}, u32[]{:S(2)}, u32[]{:S(2)}) collective-permute-start(bf16[1024,128]{1,0:T(8,128)(2,1)S(1)} %fusion.5.refs_0_), channel_id=1, source_target_pairs={{4,0},{0,4},{5,1},{1,5},{6,2},{2,6},{7,3},{3,7},{12,8},{8,12},{13,... | collective-permute-start | bytes 786440 | tf_op jit(solution)/shard_map/ppermute | solution.py:13
  35.3 14.2 %collective-permute-start.4 = (bf16[1024,128]{1,0:T(8,128)(2,1)S(1)}, bf16[1024,128]{1,0:T(8,128)(2,1)S(1)}, u32[]{:S(2)}, u32[]{:S(2)}) collective-permute-start(bf16[1024,128]{1,0:T(8,128)(2,1)S(1)} %collective-permute-done.refs_1_), channel_id=1, source_target_pairs={{4,0},{0,4},{5,1},{1,5},{6,2},{2,6},{7,3},{3,7},{12,8},{8,12},{13,... | collective-permute-start | bytes 786440 | tf_op jit(solution)/shard_map/ppermute | solution.py:13
  45.0 4.5 %collective-permute-start.5 = (bf16[1024,128]{1,0:T(8,128)(2,1)S(1)}, bf16[1024,128]{1,0:T(8,128)(2,1)S(1)}, u32[]{:S(2)}, u32[]{:S(2)}) collective-permute-start(bf16[1024,128]{1,0:T(8,128)(2,1)S(1)} %collective-permute-done.1.refs_2_), channel_id=1, source_target_pairs={{4,0},{0,4},{5,1},{1,5},{6,2},{2,6},{7,3},{3,7},{12,8},{8,12},{13,... | collective-permute-start | bytes 786440 | tf_op jit(solution)/shard_map/ppermute | solution.py:13
  47.0 3.6 %collective-permute-start.6 = (bf16[1024,128]{1,0:T(8,128)(2,1)S(1)}, bf16[1024,128]{1,0:T(8,128)(2,1)S(1)}, u32[]{:S(2)}, u32[]{:S(2)}) collective-permute-start(bf16[1024,128]{1,0:T(8,128)(2,1)S(1)} %collective-permute-done.2.refs_3_), channel_id=1, source_target_pairs={{4,0},{0,4},{5,1},{1,5},{6,2},{2,6},{7,3},{3,7},{12,8},{8,12},{13,... | collective-permute-start | bytes 786440 | tf_op jit(solution)/shard_map/ppermute | solution.py:13
  54.4 54.1 %all-to-all-start.1 = ((bf16[16,32,1024]{2,1,0:T(8,128)(2,1)}), bf16[16,32,1024]{2,1,0:T(8,128)(2,1)S(1)}, u32[]{:S(2)}, u32[]{:S(2)}) async-start(bf16[16,32,1024]{2,1,0:T(8,128)(2,1)} %bitcast.13), calls=%async_computation.1 | async-start | bytes 2097152 | tf_op jit(solution)/shard_map/all_to_all | solution.py:88
  67.9 34.7 %collective-permute-start.9 = (bf16[128,1024]{1,0:T(8,128)(2,1)}, bf16[128,1024]{1,0:T(8,128)(2,1)}, u32[]{:S(2)}, u32[]{:S(2)}) collective-permute-start(bf16[128,1024]{1,0:T(8,128)(2,1)} %get-tuple-element.9), channel_id=1, source_target_pairs={{2,0},{3,1},{0,2},{1,3},{6,4},{7,5},{4,6},{5,7},{10,8},{11,9},{8,1... | collective-permute-start | bytes 786440 | tf_op jit(solution)/shard_map/ppermute | solution.py:13
  76.5 26.1 %collective-permute-start.8 = (bf16[128,1024]{1,0:T(8,128)(2,1)}, bf16[128,1024]{1,0:T(8,128)(2,1)}, u32[]{:S(2)}, u32[]{:S(2)}) collective-permute-start(bf16[128,1024]{1,0:T(8,128)(2,1)} %get-tuple-element.10), channel_id=1, source_target_pairs={{1,0},{2,1},{3,2},{0,3},{5,4},{6,5},{7,6},{4,7},{9,8},{10,9},{11,1... | collective-permute-start | bytes 786440 | tf_op jit(solution)/shard_map/ppermute | solution.py:13
  79.3 27.0 %collective-permute-start.7 = (bf16[128,1024]{1,0:T(8,128)(2,1)S(1)}, bf16[128,1024]{1,0:T(8,128)(2,1)}, u32[]{:S(2)}, u32[]{:S(2)}) collective-permute-start(bf16[128,1024]{1,0:T(8,128)(2,1)S(1)} %get-tuple-element.8), channel_id=1, source_target_pairs={{3,0},{0,1},{1,2},{2,3},{7,4},{4,5},{5,6},{6,7},{11,8},{8,9},{9,10... | collective-permute-start | bytes 786440 | tf_op jit(solution)/shard_map/ppermute | solution.py:13
  108.5 1.0 copy-start

commit v2 on v1

v2 whole, which is shorter than its diff:
```python
import functools

import jax
import jax.numpy as jnp
from jax import lax
from jax.experimental import pallas as pl
from jax.experimental.pallas import tpu as pltpu
from jax.sharding import Mesh, PartitionSpec as P

AXES = ("zl", "y", "x", "c", "mp")
TURNS = (1, 3, 2)
BF16, F32 = jnp.bfloat16, jnp.float32
IN_HBM = pl.BlockSpec(memory_space=pltpu.HBM)
IN_VMEM = pl.BlockSpec(memory_space=pltpu.VMEM)


def shift(array, axis, size, by):
    return lax.ppermute(array, axis, [((i + by) % size, i) for i in range(size)])


def params(limit=24):
    return pltpu.CompilerParams(vmem_limit_bytes=limit << 20)


def whole(shape):
    return pl.BlockSpec(shape, lambda *_: (0,) * len(shape))


def spread_kernel(weight_ref, out_ref, weight, sem):
    copy = pltpu.make_async_copy(weight_ref, weight, sem)
    copy.start()
    copy.wait()
    for k in range(8):
        for q in range(4):
            piece = weight[(q * 8 + k) * 32 : (q * 8 + k + 1) * 32, :]
            for m in range(4):
                out_ref[m, k, q * 32 : (q + 1) * 32, :] = piece


def spread_rows(weight):
    return pl.pallas_call(
        spread_kernel,
        in_specs=[IN_HBM],
        out_specs=IN_VMEM,
        scratch_shapes=[pltpu.VMEM((1024, 128), BF16), pltpu.SemaphoreType.DMA],
        out_shape=jax.ShapeDtypeStruct((4, 8, 128, 128), BF16),
        compiler_params=params(58),
    )(weight)


def gate_kernel(gate_hbm, up_hbm, hidden_hbm, out_ref, *scratch):
    sems = scratch[3]
    copies = []
    for step in range(4):
        rows = pl.ds(step * 256, 256)
        for n, source in enumerate((gate_hbm, up_hbm, hidden_hbm)):
            copy = pltpu.make_async_copy(source.at[rows], scratch[n].at[rows], sems.at[n, step])
            copy.start()
            copies.append(copy)
    for step in range(4):
        rows = pl.ds(step * 256, 256)
        for copy in copies[step * 3 : step * 3 + 3]:
            copy.wait()
        gate, up, hidden = (ref[rows].astype(F32) for ref in scratch[:3])
        sigma = jax.nn.sigmoid(gate)
        product = hidden * up * sigma * (1.0 + gate * (1.0 - sigma))
        out_ref[:, rows] = product.T.astype(BF16)


def gate_gradient(gate_pre, up_value, grad_hidden):
    return pl.pallas_call(
        gate_kernel,
        in_specs=[IN_HBM] * 3,
        out_specs=IN_VMEM,
        scratch_shapes=[pltpu.VMEM((1024, 128), BF16)] * 3 + [pltpu.SemaphoreType.DMA((3, 4))],
        out_shape=jax.ShapeDtypeStruct((128, 1024), BF16),
        compiler_params=params(58),
    )(gate_pre, up_value, grad_hidden)


def share_kernel(gates_ref, tokens_hbm, own_ref, a_ref, b_ref, c_ref, tokens, sems):
    m = lax.axis_index("mp")
    copies = []
    for step in range(8):
        column = jnp.bitwise_and(m + (TURNS + (0,))[step // 2], 3) * 1024 + step % 2 * 512
        copy = pltpu.make_async_copy(
            tokens_hbm.at[:, pl.ds(pl.multiple_of(column, 512), 512)], tokens.at[step], sems.at[step]
        )
        copy.start()
        copies.append(copy)
    for step, copy in enumerate(copies):
        copy.wait()
        out_ref = (a_ref, b_ref, c_ref, own_ref)[step // 2]
        share = jnp.dot(gates_ref[...], tokens[step], preferred_element_type=F32)
        out_ref[:, step % 2 * 512 : (step % 2 + 1) * 512] = share.astype(out_ref.dtype)


def weight_shares(gates, tokens):
    return pl.pallas_call(
        share_kernel,
        in_specs=[IN_VMEM, IN_HBM],
        out_specs=[IN_VMEM] * 4,
        scratch_shapes=[pltpu.VMEM((8, 1024, 512), BF16), pltpu.SemaphoreType.DMA((8,))],
        out_shape=[jax.ShapeDtypeStruct((128, 1024), F32)]
        + [jax.ShapeDtypeStruct((128, 1024), BF16)] * 3,
        compiler_params=params(58),
        cost_estimate=pl.CostEstimate(flops=1 << 30, bytes_accessed=10 << 20, transcendentals=0),
    )(gates, tokens)


def add_kernel(scale, own_ref, *refs):
    total = own_ref[...]
    for ref in refs[:3]:
        total = total + ref[...].astype(F32)
    refs[3][...] = (total * scale).T.astype(BF16)


def add_shares(own, away, scale):
    return pl.pallas_call(
        functools.partial(add_kernel, scale),
        grid=(4,),
        in_specs=[pl.BlockSpec((128, 256), lambda d: (0, d))] * 4,
        out_specs=pl.BlockSpec((256, 128), lambda d: (d, 0)),
        out_shape=jax.ShapeDtypeStruct((1024, 128), BF16),
        compiler_params=params(),
    )(own, *away)


def partial_kernel(order, rows_ref, *refs):
    gates, out_ref, rows, block = refs[:8], refs[8], refs[9], refs[10]
    for k in range(8):
        for m in range(4):
            rows[m * 128 : (m + 1) * 128, k * 128 : (k + 1) * 128] = rows_ref[m, order[k]]
        block[k * 128 : (k + 1) * 128, :] = gates[k][...]
    out_ref[...] = jnp.dot(rows[...], block[...], preferred_element_type=F32).astype(BF16)


def partial_product(order, rows, gates):
    return pl.pallas_call(
        partial_kernel,
        grid_spec=pltpu.PrefetchScalarGridSpec(
            num_scalar_prefetch=1,
            grid=(1,),
            in_specs=[whole((4, 8, 128, 128))] + [whole((128, 1024))] * 8,
            out_specs=whole((512, 1024)),
            scratch_shapes=[pltpu.VMEM((512, 1024), BF16), pltpu.VMEM((1024, 1024), BF16)],
        ),
        out_shape=jax.ShapeDtypeStruct((512, 1024), BF16),
        compiler_params=params(),
        cost_estimate=pl.CostEstimate(flops=1 << 30, bytes_accessed=4 << 20, transcendentals=0),
    )(order, rows, *gates)


def sum_kernel(pieces_ref, out_ref):
    out_ref[...] = jnp.sum(pieces_ref[...].astype(F32), axis=0).astype(BF16)


def sum_pieces(pieces):
    return pl.pallas_call(
        sum_kernel,
        grid=(4,),
        in_specs=[pl.BlockSpec((16, 32, 256), lambda t: (0, 0, t))],
        out_specs=pl.BlockSpec((32, 256), lambda t: (0, t)),
        out_shape=jax.ShapeDtypeStruct((32, 1024), BF16),
        compiler_params=params(),
    )(pieces)


def body(tokens, gate_pre, up_value, grad_hidden, gate_weight):
    x, c = lax.axis_index("x"), lax.axis_index("c")
    norm_factor = float(tokens.shape[0] * lax.axis_size("mp")) ** (-0.5)

    gates = gate_gradient(gate_pre, up_value, grad_hidden)
    mine = [gates] + [shift(gates, "x", 4, k) for k in TURNS]
    other = [shift(block, "c", 2, 1) for block in mine]

    rows = spread_rows(gate_weight).reshape(32, 128, 128)
    rows = lax.all_to_all(rows, ("mp", "x", "c"), 0, 0, tiled=True).reshape(4, 8, 128, 128)

    own, *shares = weight_shares(gates, tokens)
    away = [shift(share, "mp", 4, -k) for k, share in zip(TURNS, shares)]

    order = jnp.stack(
        [((x + k) & 3) * 2 + c for k in (0,) + TURNS]
        + [((x + k) & 3) * 2 + 1 - c for k in (0,) + TURNS]
    ).astype(jnp.int32)
    order, away[0] = lax.optimization_barrier((order, away[0]))
    partial_sums = partial_product(order, rows, mine + other)
    pieces = lax.all_to_all(partial_sums.reshape(16, 32, 1024), ("zl", "y"), 0, 0, tiled=True)
    grad_tokens = sum_pieces(pieces).T
    grad_gate_weight = add_shares(own, away, norm_factor)
    return (grad_tokens, grad_gate_weight)


def solution(mesh):
    fine = Mesh(mesh.devices.reshape(2, 8, 4, 2, 4), AXES)
    dp = ("zl", "y", "x", "c")
    in_specs = (P("mp", None), P("mp", dp), P("mp", dp), P("mp", dp), P("mp", dp))
    out_specs = (P("mp", dp), P("mp", dp))
    return jax.shard_map(body, mesh=fine, in_specs=in_specs, out_specs=out_specs, check_vma=False)
```

time: 112 us -> 111 us (level)
  the two profiles are of different devices: /device:TPU:8 before, /device:TPU:65 now
where the time goes in v2:
time: 111 us; the launch traced here: 110 us
  starting transfers between devices  55.1 us (50%)
  waiting for transfers between devices  37.5 us (34%)
  Pallas kernels  15.9 us (14%)
  local copies, waits for them, and re-layouts  1.13 us (1%)
    ppermute x10, waiting for transfers between devices, shift(): lax.ppermute(array, axis, [((i + by) % size, i) for i in range(size)])  37.5 us
    ppermute x10, starting transfers between devices, shift(): lax.ppermute(array, axis, [((i + by) % size, i) for i in range(size)])  34.3 us
    all_to_all x1, starting transfers between devices, body(): lax.all_to_all(rows, ('mp', 'x', 'c'), 0, 0, tiled=True)  12.7 us
    all_to_all x1, starting transfers between devices, body(): lax.all_to_all(partial_sums.reshape(16, 32, 1024), ('zl', 'y'), 0, 0, til...  8.01 us
    pallas_call x1, Pallas kernels, weight_shares(): pl.pallas_call(share_kernel, in_specs=[IN_VMEM, IN_HBM], out_specs=[IN_VM...  5.64 us
    pallas_call x1, Pallas kernels, partial_product(): pl.pallas_call(partial_kernel, grid_spec=pltpu.PrefetchScalarGridSpec(num...  2.78 us
    pallas_call x1, Pallas kernels, gate_gradient(): pl.pallas_call(gate_kernel, in_specs=[IN_HBM] * 3, out_specs=IN_VMEM, scr...  2.23 us
  transfers between devices with their start and end apart: 12, of which 3 were waited for; matrix products, arithmetic and copies ran while one was open for 0% of the time, Pallas kernels for 9%

profile of v2, /device:TPU:65, one launch (start us, length us, event | category | flops | bytes accessed | tf_op | source)
XLA Modules:
  0.0 110.4 jit_solution(1590104028518680525)
XLA Ops:
  0.6 2.1 %shard_map.70 = bf16[4,8,128,128]{3,2,1,0:T(8,128)(2,1)} custom-call(bf16[1024,128]{1,0:T(8,128)(2,1)} %weight_ref.1), custom_call_target="tpu_custom_call" | custom-call | tf_op jit(solution)/shard_map/pallas_call | solution.py:41
  2.7 12.7 %all-to-all-start = ((bf16[32,128,128]{2,1,0:T(8,128)(2,1)}), bf16[32,128,128]{2,1,0:T(8,128)(2,1)S(1)}, u32[]{:S(2)}, u32[]{:S(2)}) async-start(bf16[32,128,128]{2,1,0:T(8,128)(2,1)} %bitcast.13), calls=%async_computation | async-start | bytes 2097152 | tf_op jit(solution)/shard_map/all_to_all | solution.py:178
  15.4 2.2 %shard_map.68.gates_ref.refs_0_ = bf16[128,1024]{1,0:T(8,128)(2,1)} custom-call(bf16[1024,128]{1,0:T(8,128)(2,1)} %gate_hbm.1, bf16[1024,128]{1,0:T(8,128)(2,1)} %up_hbm.1, bf16[1024,128]{1,0:T(8,128)(2,1)} %hidden_hbm.1), custom_call_target="tpu_custom_call" | custom-call | tf_op jit(solution)/shard_map/pallas_call | solution.py:71
  17.7 0.0 copy-start
  17.7 4.6 %collective-permute-start.1 = (bf16[128,1024]{1,0:T(8,128)(2,1)}, bf16[128,1024]{1,0:T(8,128)(2,1)S(1)}, u32[]{:S(2)}, u32[]{:S(2)}) collective-permute-start(bf16[128,1024]{1,0:T(8,128)(2,1)} %shard_map.68.gates_ref.refs_0_), channel_id=1, source_target_pairs={{8,0},{16,8},{24,16},{0,24},{9,1},{17,9},{25,17},{1,25},{10,2},{18... | collective-permute-start | bytes 786440 | tf_op jit(solution)/shard_map/ppermute | solution.py:18
  22.3 1.9 %collective-permute-start.2 = (bf16[128,1024]{1,0:T(8,128)(2,1)}, bf16[128,1024]{1,0:T(8,128)(2,1)S(1)}, u32[]{:S(2)}, u32[]{:S(2)}) collective-permute-start(bf16[128,1024]{1,0:T(8,128)(2,1)} %shard_map.68.gates_ref.refs_0_), channel_id=1, source_target_pairs={{24,0},{0,8},{8,16},{16,24},{25,1},{1,9},{9,17},{17,25},{26,2},{2,... | collective-permute-start | bytes 786440 | tf_op jit(solution)/shard_map/ppermute | solution.py:18
  24.2 3.7 %collective-permute-start.3 = (bf16[128,1024]{1,0:T(8,128)(2,1)}, bf16[128,1024]{1,0:T(8,128)(2,1)S(1)}, u32[]{:S(2)}, u32[]{:S(2)}) collective-permute-start(bf16[128,1024]{1,0:T(8,128)(2,1)} %shard_map.68.gates_ref.refs_0_), channel_id=1, source_target_pairs={{16,0},{24,8},{0,16},{8,24},{17,1},{25,9},{1,17},{9,25},{18,2},{26... | collective-permute-start | bytes 786440 | tf_op jit(solution)/shard_map/ppermute | solution.py:18
  27.9 3.1 %collective-permute-start.4 = (bf16[128,1024]{1,0:T(8,128)(2,1)}, bf16[128,1024]{1,0:T(8,128)(2,1)S(1)}, u32[]{:S(2)}, u32[]{:S(2)}) collective-permute-start(bf16[128,1024]{1,0:T(8,128)(2,1)} %shard_map.68.gates_ref.refs_0_), channel_id=1, source_target_pairs={{4,0},{0,4},{5,1},{1,5},{6,2},{2,6},{7,3},{3,7},{12,8},{8,12},{13,... | collective-permute-start | bytes 786440 | tf_op jit(solution)/shard_map/ppermute | solution.py:18
  31.0 5.6 %shard_map.69 = (f32[128,1024]{1,0:T(8,128)}, bf16[128,1024]{1,0:T(8,128)(2,1)}, bf16[128,1024]{1,0:T(8,128)(2,1)}, bf16[128,1024]{1,0:T(8,128)(2,1)}) custom-call(bf16[128,1024]{1,0:T(8,128)(2,1)} %shard_map.68.gates_ref.refs_0_, bf16[1024,4096]{1,0:T(8,128)(2,1)} %tokens_hbm.1), custom_call_target="tpu_custom_call" | custom-call | flops 1073741824 | bytes 10485760 | tf_op jit(solution)/shard_map/pallas_call | solution.py:99
  36.7 4.0 %collective-permute-start = (bf16[128,1024]{1,0:T(8,128)(2,1)}, bf16[128,1024]{1,0:T(8,128)(2,1)S(1)}, u32[]{:S(2)}, u32[]{:S(2)}) collective-permute-start(bf16[128,1024]{1,0:T(8,128)(2,1)} %get-tuple-element.8), channel_id=1, source_target_pairs={{3,0},{0,1},{1,2},{2,3},{7,4},{4,5},{5,6},{6,7},{11,8},{8,9},{9,10... | collective-permute-start | bytes 786440 | tf_op jit(solution)/shard_map/ppermute | solution.py:18
  40.7 0.0 collective-permute-done.1.refs_1_
  40.7 2.2 %collective-permute-start.5 = (bf16[128,1024]{1,0:T(8,128)(2,1)S(1)}, bf16[128,1024]{1,0:T(8,128)(2,1)S(1)}, u32[]{:S(2)}, u32[]{:S(2)}) collective-permute-start(bf16[128,1024]{1,0:T(8,128)(2,1)S(1)} %collective-permute-done.1.refs_1_), channel_id=1, source_target_pairs={{4,0},{0,4},{5,1},{1,5},{6,2},{2,6},{7,3},{3,7},{12,8},{8,12},{13,... | collective-permute-start | bytes 786440 | tf_op jit(solution)/shard_map/ppermute | solution.py:18
  42.9 0.0 collective-permute-done.2.refs_2_
  42.9 3.5 %collective-permute-start.6 = (bf16[128,1024]{1,0:T(8,128)(2,1)S(1)}, bf16[128,1024]{1,0:T(8,128)(2,1)S(1)}, u32[]{:S(2)}, u32[]{:S(2)}) collective-permute-start(bf16[128,1024]{1,0:T(8,128)(2,1)S(1)} %collective-permute-done.2.refs_2_), channel_id=1, source_target_pairs={{4,0},{0,4},{5,1},{1,5},{6,2},{2,6},{7,3},{3,7},{12,8},{8,12},{13,... | collective-permute-start | bytes 786440 | tf_op jit(solution)/shard_map/ppermute | solution.py:18
  46.4 0.0 collective-permute-done.3.refs_3_
  46.4 2.3 %collective-permute-start.7 = (bf16[128,1024]{1,0:T(8,128)(2,1)S(1)}, bf16[128,1024]{1,0:T(8,128)(2,1)S(1)}, u32[]{:S(2)}, u32[]{:S(2)}) collective-permute-start(bf16[128,1024]{1,0:T(8,128)(2,1)S(1)} %collective-permute-done.3.refs_3_), channel_id=1, source_target_pairs={{4,0},{0,4},{5,1},{1,5},{6,2},{2,6},{7,3},{3,7},{12,8},{8,12},{13,... | collective-permute-start | bytes 786440 | tf_op jit(solution)/shard_map/ppermute | solution.py:18
  48.7 0.1 stack.35.order
  48.8 5.7 %collective-permute-done.refs_0_ = bf16[128,1024]{1,0:T(8,128)(2,1)S(1)} collective-permute-done((bf16[128,1024]{1,0:T(8,128)(2,1)}, bf16[128,1024]{1,0:T(8,128)(2,1)S(1)}, u32[]{:S(2)}, u32[]{:S(2)}) %collective-permute-start) | collective-permute-done | bytes 262176 | tf_op jit(solution)/shard_map/ppermute | solution.py:18
  54.5 0.0 collective-permute-done.4.refs_4_
  54.5 0.0 collective-permute-done.5.refs_5_
  54.5 0.0 collective-permute-done.6.refs_6_
  54.5 0.0 collective-permute-done.7.refs_7_
  54.5 0.0 all-to-all-done
  54.5 0.0 copy-done
  54.5 2.8 %shard_map.71 = bf16[512,1024]{1,0:T(8,128)(2,1)} custom-call(s32[8]{0:T(128)S(1)} %stack.35.order, bf16[4,8,128,128]{3,2,1,0:T(8,128)(2,1)S(1)} %bitcast.12, bf16[128,1024]{1,0:T(8,128)(2,1)S(1)} %copy-done, bf16[128,1024]{1,0:T(8,128)(2,1)S(1)} %collective-permute-done.1.refs_1_, bf16[128,1024]{1,0:T(8,128)(2,1)S(1)} %collective-permute-done.2.refs_2_, ...), custom_call_target="tpu_custom_call" | custom-call | flops 1073741824 | bytes 4194304 | tf_op jit(solution)/shard_map/pallas_call | solution.py:139
  57.3 8.0 %all-to-all-start.1 = ((bf16[16,32,1024]{2,1,0:T(8,128)(2,1)}), bf16[16,32,1024]{2,1,0:T(8,128)(2,1)S(1)}, u32[]{:S(2)}, u32[]{:S(2)}) async-start(bf16[16,32,1024]{2,1,0:T(8,128)(2,1)} %bitcast.10), calls=%async_computation.1 | async-start | bytes 2097152 | tf_op jit(solution)/shard_map/all_to_all | solution.py:189
  65.3 4.4 %collective-permute-start.8 = (bf16[128,1024]{1,0:T(8,128)(2,1)}, bf16[128,1024]{1,0:T(8,128)(2,1)S(1)}, u32[]{:S(2)}, u32[]{:S(2)}) collective-permute-start(bf16[128,1024]{1,0:T(8,128)(2,1)} %get-tuple-element.12), channel_id=1, source_target_pairs={{1,0},{2,1},{3,2},{0,3},{5,4},{6,5},{7,6},{4,7},{9,8},{10,9},{11,1... | collective-permute-start | bytes 786440 | tf_op jit(solution)/shard_map/ppermute | solution.py:18
  69.7 4.7 %collective-permute-start.9 = (bf16[128,1024]{1,0:T(8,128)(2,1)}, bf16[128,1024]{1,0:T(8,128)(2,1)S(1)}, u32[]{:S(2)}, u32[]{:S(2)}) collective-permute-start(bf16[128,1024]{1,0:T(8,128)(2,1)} %get-tuple-element.13), channel_id=1, source_target_pairs={{2,0},{3,1},{0,2},{1,3},{6,4},{7,5},{4,6},{5,7},{10,8},{11,9},{8,1... | collective-permute-start | bytes 786440 | tf_op jit(solution)/shard_map/ppermute | solution.py:18
  74.4 14.9 %collective-permute-done.8.refs_1_ = bf16[128,1024]{1,0:T(8,128)(2,1)S(1)} collective-permute-done((bf16[128,1024]{1,0:T(8,128)(2,1)}, bf16[128,1024]{1,0:T(8,128)(2,1)S(1)}, u32[]{:S(2)}, u32[]{:S(2)}) %collective-permute-start.8) | collective-permute-done | bytes 262176 | tf_op jit(solution)/shard_map/ppermute | solution.py:18
  89.3 16.9 %collective-permute-done.9.refs_2_ = bf16[128,1024]{1,0:T(8,128)(2,1)S(1)} collective-permute-done((bf16[128,1024]{1,0:T(8,128)(2,1)}, bf16[128,1024]{1,0:T(8,128)(2,1)S(1)}, u32[]{:S(2)}, u32[]{:S(2)}) %collective-permute-start.9) | collective-permute-done | bytes 262176 | tf_op jit(solution)/shard_map/ppermute | solution.py:18
  106.1 0.0 copy-start.1
  106.2 1.0 copy-done.1
  107.2 1.7 %shard_map.73 = bf16[1024,128]{1,0:T(8,128)(2,1)} custom-call(f32[128,1024]{1,0:T(8,128)S(1)} %copy-done.1, bf16[128,1024]{1,0:T(8,128)(2,1)S(1)} %collective-permute-done.refs_0_, bf16[128,1024]{1,0:T(8,128)(2,1)S(1)} %collective-permute-done.8.refs_1_, bf16[128,1024]{1,0:T(8,128)(2,1)S(1)} %collective-permute-done.9.refs_2_), custom_call_target="tpu_custom_call" | custom-call | tf_op jit(solution)/shard_map/pallas_call | solution.py:119
  108.9 0.0 all-to-all-done.1.pieces_ref
  108.9 1.5 %shard_map.72 = bf16[32,1024]{1,0:T(8,128)(2,1)} custom-call(bf16[16,32,1024]{2,1,0:T(8,128)(2,1)S(1)} %all-to-all-done.1.pieces_ref), custom_call_target="tpu_custom_call" | custom-call | tf_op jit(solution)/shard_map/pallas_call | solution.py:159
Async XLA Ops:
  2.7 51.8 %all-to-all-start = ((bf16[32,128,128]{2,1,0:T(8,128)(2,1)}), bf16[32,128,128]{2,1,0:T(8,128)(2,1)S(1)}, u32[]{:S(2)}, u32[]{:S(2)}) async-start(bf16[32,128,128]{2,1,0:T(8,128)(2,1)} %bitcast.13), calls=%async_computation | async-start | bytes 2097152 | tf_op jit(solution)/shard_map/all_to_all | solution.py:178
  17.7 36.9 %copy-start = (bf16[128,1024]{1,0:T(8,128)(2,1)S(1)}, bf16[128,1024]{1,0:T(8,128)(2,1)}, u32[]{:S(2)}) copy-start(bf16[128,1024]{1,0:T(8,128)(2,1)} %shard_map.68.gates_ref.refs_0_) | copy-start | bytes 786436
  17.7 23.0 %collective-permute-start.1 = (bf16[128,1024]{1,0:T(8,128)(2,1)}, bf16[128,1024]{1,0:T(8,128)(2,1)S(1)}, u32[]{:S(2)}, u32[]{:S(2)}) collective-permute-start(bf16[128,1024]{1,0:T(8,128)(2,1)} %shard_map.68.gates_ref.refs_0_), channel_id=1, source_target_pairs={{8,0},{16,8},{24,16},{0,24},{9,1},{17,9},{25,17},{1,25},{10,2},{18... | collective-permute-start | bytes 786440 | tf_op jit(solution)/shard_map/ppermute | solution.py:18
  22.3 20.6 %collective-permute-start.2 = (bf16[128,1024]{1,0:T(8,128)(2,1)}, bf16[128,1024]{1,0:T(8,128)(2,1)S(1)}, u32[]{:S(2)}, u32[]{:S(2)}) collective-permute-start(bf16[128,1024]{1,0:T(8,128)(2,1)} %shard_map.68.gates_ref.refs_0_), channel_id=1, source_target_pairs={{24,0},{0,8},{8,16},{16,24},{25,1},{1,9},{9,17},{17,25},{26,2},{2,... | collective-permute-start | bytes 786440 | tf_op jit(solution)/shard_map/ppermute | solution.py:18
  24.2 22.2 %collective-permute-start.3 = (bf16[128,1024]{1,0:T(8,128)(2,1)}, bf16[128,1024]{1,0:T(8,128)(2,1)S(1)}, u32[]{:S(2)}, u32[]{:S(2)}) collective-permute-start(bf16[128,1024]{1,0:T(8,128)(2,1)} %shard_map.68.gates_ref.refs_0_), channel_id=1, source_target_pairs={{16,0},{24,8},{0,16},{8,24},{17,1},{25,9},{1,17},{9,25},{18,2},{26... | collective-permute-start | bytes 786440 | tf_op jit(solution)/shard_map/ppermute | solution.py:18
  27.9 26.6 %collective-permute-start.4 = (bf16[128,1024]{1,0:T(8,128)(2,1)}, bf16[128,1024]{1,0:T(8,128)(2,1)S(1)}, u32[]{:S(2)}, u32[]{:S(2)}) collective-permute-start(bf16[128,1024]{1,0:T(8,128)(2,1)} %shard_map.68.gates_ref.refs_0_), channel_id=1, source_target_pairs={{4,0},{0,4},{5,1},{1,5},{6,2},{2,6},{7,3},{3,7},{12,8},{8,12},{13,... | collective-permute-start | bytes 786440 | tf_op jit(solution)/shard_map/ppermute | solution.py:18
  36.7 17.8 %collective-permute-start = (bf16[128,1024]{1,0:T(8,128)(2,1)}, bf16[128,1024]{1,0:T(8,128)(2,1)S(1)}, u32[]{:S(2)}, u32[]{:S(2)}) collective-permute-start(bf16[128,1024]{1,0:T(8,128)(2,1)} %get-tuple-element.8), channel_id=1, source_target_pairs={{3,0},{0,1},{1,2},{2,3},{7,4},{4,5},{5,6},{6,7},{11,8},{8,9},{9,10... | collective-permute-start | bytes 786440 | tf_op jit(solution)/shard_map/ppermute | solution.py:18
  40.7 13.8 %collective-permute-start.5 = (bf16[128,1024]{1,0:T(8,128)(2,1)S(1)}, bf16[128,1024]{1,0:T(8,128)(2,1)S(1)}, u32[]{:S(2)}, u32[]{:S(2)}) collective-permute-start(bf16[128,1024]{1,0:T(8,128)(2,1)S(1)} %collective-permute-done.1.refs_1_), channel_id=1, source_target_pairs={{4,0},{0,4},{5,1},{1,5},{6,2},{2,6},{7,3},{3,7},{12,8},{8,12},{13,... | collective-permute-start | bytes 786440 | tf_op jit(solution)/shard_map/ppermute | solution.py:18
  42.9 11.6 %collective-permute-start.6 = (bf16[128,1024]{1,0:T(8,128)(2,1)S(1)}, bf16[128,1024]{1,0:T(8,128)(2,1)S(1)}, u32[]{:S(2)}, u32[]{:S(2)}) collective-permute-start(bf16[128,1024]{1,0:T(8,128)(2,1)S(1)} %collective-permute-done.2.refs_2_), channel_id=1, source_target_pairs={{4,0},{0,4},{5,1},{1,5},{6,2},{2,6},{7,3},{3,7},{12,8},{8,12},{13,... | collective-permute-start | bytes 786440 | tf_op jit(solution)/shard_map/ppermute | solution.py:18
  46.4 8.1 %collective-permute-start.7 = (bf16[128,1024]{1,0:T(8,128)(2,1)S(1)}, bf16[128,1024]{1,0:T(8,128)(2,1)S(1)}, u32[]{:S(2)}, u32[]{:S(2)}) collective-permute-start(bf16[128,1024]{1,0:T(8,128)(2,1)S(1)} %collective-permute-done.3.refs_3_), channel_id=1, source_target_pairs={{4,0},{0,4},{5,1},{1,5},{6,2},{2,6},{7,3},{3,7},{12,8},{8,12},{13,... | collective-permute-start | bytes 786440 | tf_op jit(solution)/shard_map/ppermute | solution.py:18
  57.3 51.6 %all-to-all-start.1 = ((bf16[16,32,1024]{2,1,0:T(8,128)(2,1)}), bf16[16,32,1024]{2,1,0:T(8,128)(2,1)S(1)}, u32[]{:S(2)}, u32[]{:S(2)}) async-start(bf16[16,32,1024]{2,1,0:T(8,128)(2,1)} %bitcast.10), calls=%async_computation.1 | async-start | bytes 2097152 | tf_op jit(solution)/shard_map/all_to_all | solution.py:189
  65.3 24.0 %collective-permute-start.8 = (bf16[128,1024]{1,0:T(8,128)(2,1)}, bf16[128,1024]{1,0:T(8,128)(2,1)S(1)}, u32[]{:S(2)}, u32[]{:S(2)}) collective-permute-start(bf16[128,1024]{1,0:T(8,128)(2,1)} %get-tuple-element.12), channel_id=1, source_target_pairs={{1,0},{2,1},{3,2},{0,3},{5,4},{6,5},{7,6},{4,7},{9,8},{10,9},{11,1... | collective-permute-start | bytes 786440 | tf_op jit(solution)/shard_map/ppermute | solution.py:18
  69.7 36.5 %collective-permute-start.9 = (bf16[128,1024]{1,0:T(8,128)(2,1)}, bf16[128,1024]{1,0:T(8,128)(2,1)S(1)}, u32[]{:S(2)}, u32[]{:S(2)}) collective-permute-start(bf16[128,1024]{1,0:T(8,128)(2,1)} %get-tuple-element.13), channel_id=1, source_target_pairs={{2,0},{3,1},{0,2},{1,3},{6,4},{7,5},{4,6},{5,7},{10,8},{11,9},{8,1... | collective-permute-start | bytes 786440 | tf_op jit(solution)/shard_map/ppermute | solution.py:18
  106.1 1.0 copy-start.1

commit v3 on v2

--- a/solution.py
+++ b/solution.py
@@ -78,11 +78,12 @@
     )(gate_pre, up_value, grad_hidden)
 
 
-def share_kernel(gates_ref, tokens_hbm, own_ref, a_ref, b_ref, c_ref, tokens, sems):
+def share_kernel(gates_ref, tokens_hbm, own_ref, right_ref, left_ref, far_a_ref, far_b_ref, tokens, sems):
     m = lax.axis_index("mp")
+    turns = (2, 1, 3, 0)
     copies = []
     for step in range(8):
-        column = jnp.bitwise_and(m + (TURNS + (0,))[step // 2], 3) * 1024 + step % 2 * 512
+        column = jnp.bitwise_and(m + turns[step // 2], 3) * 1024 + step % 2 * 512
         copy = pltpu.make_async_copy(
             tokens_hbm.at[:, pl.ds(pl.multiple_of(column, 512), 512)], tokens.at[step], sems.at[step]
         )
@@ -90,65 +91,88 @@
         copies.append(copy)
     for step, copy in enumerate(copies):
         copy.wait()
-        out_ref = (a_ref, b_ref, c_ref, own_ref)[step // 2]
+        columns = pl.ds(step % 2 * 512, 512)
         share = jnp.dot(gates_ref[...], tokens[step], preferred_element_type=F32)
-        out_ref[:, step % 2 * 512 : (step % 2 + 1) * 512] = share.astype(out_ref.dtype)
+        if step < 2:
+            far_a_ref[:, columns] = share[:64].astype(BF16)
+            far_b_ref[:, columns] = share[64:].astype(BF16)
+        else:
+            (right_ref, left_ref, own_ref)[step // 2 - 1][:, columns] = share
 
 
 def weight_shares(gates, tokens):
+    full, half = jax.ShapeDtypeStruct((128, 1024), F32), jax.ShapeDtypeStruct((64, 1024), BF16)
     return pl.pallas_call(
         share_kernel,
         in_specs=[IN_VMEM, IN_HBM],
-        out_specs=[IN_VMEM] * 4,
+        out_specs=[IN_VMEM] * 5,
         scratch_shapes=[pltpu.VMEM((8, 1024, 512), BF16), pltpu.SemaphoreType.DMA((8,))],
-        out_shape=[jax.ShapeDtypeStruct((128, 1024), F32)]
-        + [jax.ShapeDtypeStruct((128, 1024), BF16)] * 3,
-        compiler_params=params(58),
+        out_shape=[full, full, full, half, half],
+        compiler_params=params(55),
         cost_estimate=pl.CostEstimate(flops=1 << 30, bytes_accessed=10 << 20, transcendentals=0),
     )(gates, tokens)
 
 
+def relay_kernel(right_ref, left_ref, far_a_ref, far_b_ref, right_out, left_out):
+    right_out[:64] = (right_ref[:64] + far_a_ref[...].astype(F32)).astype(BF16)
+    right_out[64:] = right_ref[64:].astype(BF16)
+    left_out[:64] = left_ref[:64].astype(BF16)
+    left_out[64:] = (left_ref[64:] + far_b_ref[...].astype(F32)).astype(BF16)
+
+
+def relay_shares(right, left, far_a, far_b):
+    return pl.pallas_call(
+        relay_kernel,
+        grid=(4,),
+        in_specs=[pl.BlockSpec((128, 256), lambda d: (0, d))] * 2
+        + [pl.BlockSpec((64, 256), lambda d: (0, d))] * 2,
+        out_specs=[pl.BlockSpec((128, 256), lambda d: (0, d))] * 2,
+        out_shape=[jax.ShapeDtypeStruct((128, 1024), BF16)] * 2,
+        compiler_params=params(),
+    )(right, left, far_a, far_b)
+
+
 def add_kernel(scale, own_ref, *refs):
     total = own_ref[...]
-    for ref in refs[:3]:
+    for ref in refs[:2]:
         total = total + ref[...].astype(F32)
-    refs[3][...] = (total * scale).T.astype(BF16)
+    refs[2][...] = (total * scale).T.astype(BF16)
 
 
 def add_shares(own, away, scale):
     return pl.pallas_call(
         functools.partial(add_kernel, scale),
         grid=(4,),
-        in_specs=[pl.BlockSpec((128, 256), lambda d: (0, d))] * 4,
+        in_specs=[pl.BlockSpec((128, 256), lambda d: (0, d))] * 3,
         out_specs=pl.BlockSpec((256, 128), lambda d: (d, 0)),
         out_shape=jax.ShapeDtypeStruct((1024, 128), BF16),
         compiler_params=params(),
     )(own, *away)
 
 
-def partial_kernel(order, rows_ref, *refs):
-    gates, out_ref, rows, block = refs[:8], refs[8], refs[9], refs[10]
+def partial_kernel(order, rows_ref, mine_ref, other_ref, out_ref, rows):
     for k in range(8):
         for m in range(4):
             rows[m * 128 : (m + 1) * 128, k * 128 : (k + 1) * 128] = rows_ref[m, order[k]]
-        block[k * 128 : (k + 1) * 128, :] = gates[k][...]
-    out_ref[...] = jnp.dot(rows[...], block[...], preferred_element_type=F32).astype(BF16)
-
-
-def partial_product(order, rows, gates):
+    total = jnp.dot(rows[:, :512], mine_ref[...].reshape(512, 1024), preferred_element_type=F32)
+    total += jnp.dot(rows[:, 512:], other_ref[...].reshape(512, 1024), preferred_element_type=F32)
+    out_ref[...] = total.astype(BF16)
+
+
+def partial_product(order, rows, mine, other):
     return pl.pallas_call(
         partial_kernel,
         grid_spec=pltpu.PrefetchScalarGridSpec(
             num_scalar_prefetch=1,
             grid=(1,),
-            in_specs=[whole((4, 8, 128, 128))] + [whole((128, 1024))] * 8,
+            in_specs=[whole((4, 8, 128, 128))] + [whole((4, 128, 1024))] * 2,
             out_specs=whole((512, 1024)),
-            scratch_shapes=[pltpu.VMEM((512, 1024), BF16), pltpu.VMEM((1024, 1024), BF16)],
+            scratch_shapes=[pltpu.VMEM((512, 1024), BF16)],
         ),
         out_shape=jax.ShapeDtypeStruct((512, 1024), BF16),
         compiler_params=params(),
         cost_estimate=pl.CostEstimate(flops=1 << 30, bytes_accessed=4 << 20, transcendentals=0),
-    )(order, rows, *gates)
+    )(order, rows, mine, other)
 
 
 def sum_kernel(pieces_ref, out_ref):
@@ -171,24 +195,29 @@
     norm_factor = float(tokens.shape[0] * lax.axis_size("mp")) ** (-0.5)
 
     gates = gate_gradient(gate_pre, up_value, grad_hidden)
-    mine = [gates] + [shift(gates, "x", 4, k) for k in TURNS]
-    other = [shift(block, "c", 2, 1) for block in mine]
-
-    rows = spread_rows(gate_weight).reshape(32, 128, 128)
+    weight, gates = lax.optimization_barrier((gate_weight, gates))
+    rows = spread_rows(weight).reshape(32, 128, 128)
     rows = lax.all_to_all(rows, ("mp", "x", "c"), 0, 0, tiled=True).reshape(4, 8, 128, 128)
 
-    own, *shares = weight_shares(gates, tokens)
-    away = [shift(share, "mp", 4, -k) for k, share in zip(TURNS, shares)]
+    mine = [shift(gates, "x", 4, k) for k in TURNS]
+    own, right, left, far_a, far_b = weight_shares(gates, tokens)
+    *mine, own = lax.optimization_barrier((*mine, own))
+    far_a, far_b = shift(far_a, "mp", 4, -1), shift(far_b, "mp", 4, 1)
+    mine = jnp.stack([gates, *mine])
+    other = shift(mine, "c", 2, 1)
 
     order = jnp.stack(
         [((x + k) & 3) * 2 + c for k in (0,) + TURNS]
         + [((x + k) & 3) * 2 + 1 - c for k in (0,) + TURNS]
     ).astype(jnp.int32)
-    order, away[0] = lax.optimization_barrier((order, away[0]))
-    partial_sums = partial_product(order, rows, mine + other)
+    partial_sums = partial_product(order, rows, mine, other)
+    partial_sums, far_a, far_b = lax.optimization_barrier((partial_sums, far_a, far_b))
     pieces = lax.all_to_all(partial_sums.reshape(16, 32, 1024), ("zl", "y"), 0, 0, tiled=True)
+
+    right, left = relay_shares(right, left, far_a, far_b)
+    away = shift(right, "mp", 4, -1), shift(left, "mp", 4, 1)
+    grad_gate_weight = add_shares(own, away, norm_factor)
     grad_tokens = sum_pieces(pieces).T
-    grad_gate_weight = add_shares(own, away, norm_factor)
     return (grad_tokens, grad_gate_weight)
 
 

time: 111 us -> 107 us (0.964)
  the two profiles are of different devices: /device:TPU:65 before, /device:TPU:73 now
where the time goes in v3:
time: 107 us; the launch traced here: 106 us
  starting transfers between devices  55.2 us (52%)
  waiting for transfers between devices  30 us (28%)
  Pallas kernels  16.4 us (15%)
  local copies, waits for them, and re-layouts  3.21 us (3%)
    ppermute x8, starting transfers between devices, shift(): lax.ppermute(array, axis, [((i + by) % size, i) for i in range(size)])  31.4 us
    ppermute x8, waiting for transfers between devices, shift(): lax.ppermute(array, axis, [((i + by) % size, i) for i in range(size)])  30 us
    all_to_all x1, starting transfers between devices, body(): lax.all_to_all(rows, ('mp', 'x', 'c'), 0, 0, tiled=True)  12.7 us
    all_to_all x1, starting transfers between devices, body(): lax.all_to_all(partial_sums.reshape(16, 32, 1024), ('zl', 'y'), 0, 0, til...  11.1 us
    pallas_call x1, Pallas kernels, weight_shares(): pl.pallas_call(share_kernel, in_specs=[IN_VMEM, IN_HBM], out_specs=[IN_VM...  5.77 us
    unnamed x8, local copies, waits for them, and re-layouts  3.13 us
    pallas_call x1, Pallas kernels, partial_product(): pl.pallas_call(partial_kernel, grid_spec=pltpu.PrefetchScalarGridSpec(num...  2.79 us
    pallas_call x1, Pallas kernels, gate_gradient(): pl.pallas_call(gate_kernel, in_specs=[IN_HBM] * 3, out_specs=IN_VMEM, scr...  2.22 us
  transfers between devices with their start and end apart: 10, of which 4 were waited for; matrix products, arithmetic and copies ran while one was open for 0% of the time, Pallas kernels for 10%

profile of v3, /device:TPU:73, one launch (start us, length us, event | category | flops | bytes accessed | tf_op | source)
XLA Modules:
  0.0 105.8 jit_solution(888914493192710553)
XLA Ops:
  0.6 2.2 %shard_map.68.gates_ref = bf16[128,1024]{1,0:T(8,128)(2,1)} custom-call(bf16[1024,128]{1,0:T(8,128)(2,1)} %gate_hbm.1, bf16[1024,128]{1,0:T(8,128)(2,1)} %up_hbm.1, bf16[1024,128]{1,0:T(8,128)(2,1)} %hidden_hbm.1), custom_call_target="tpu_custom_call" | custom-call | tf_op jit(solution)/shard_map/pallas_call | solution.py:71
  2.9 0.0 copy-start.3
  2.9 2.1 %shard_map.69 = bf16[4,8,128,128]{3,2,1,0:T(8,128)(2,1)} custom-call(bf16[1024,128]{1,0:T(8,128)(2,1)} %weight_ref), custom_call_target="tpu_custom_call" | custom-call | tf_op jit(solution)/shard_map/pallas_call | solution.py:41
  5.0 12.7 %all-to-all-start = ((bf16[32,128,128]{2,1,0:T(8,128)(2,1)}), bf16[32,128,128]{2,1,0:T(8,128)(2,1)S(1)}, u32[]{:S(2)}, u32[]{:S(2)}) async-start(bf16[32,128,128]{2,1,0:T(8,128)(2,1)} %bitcast.17), calls=%async_computation | async-start | bytes 2097152 | tf_op jit(solution)/shard_map/all_to_all | solution.py:200
  17.7 4.8 %collective-permute-start.2 = (bf16[128,1024]{1,0:T(8,128)(2,1)}, bf16[128,1024]{1,0:T(8,128)(2,1)S(1)}, u32[]{:S(2)}, u32[]{:S(2)}) collective-permute-start(bf16[128,1024]{1,0:T(8,128)(2,1)} %shard_map.68.gates_ref), channel_id=1, source_target_pairs={{16,0},{24,8},{0,16},{8,24},{17,1},{25,9},{1,17},{9,25},{18,2},{26... | collective-permute-start | bytes 786440 | tf_op jit(solution)/shard_map/ppermute | solution.py:18
  22.5 2.2 %collective-permute-start.1 = (bf16[128,1024]{1,0:T(8,128)(2,1)}, bf16[128,1024]{1,0:T(8,128)(2,1)S(1)}, u32[]{:S(2)}, u32[]{:S(2)}) collective-permute-start(bf16[128,1024]{1,0:T(8,128)(2,1)} %shard_map.68.gates_ref), channel_id=1, source_target_pairs={{24,0},{0,8},{8,16},{16,24},{25,1},{1,9},{9,17},{17,25},{26,2},{2,... | collective-permute-start | bytes 786440 | tf_op jit(solution)/shard_map/ppermute | solution.py:18
  24.7 4.3 %collective-permute-start = (bf16[128,1024]{1,0:T(8,128)(2,1)}, bf16[128,1024]{1,0:T(8,128)(2,1)S(1)}, u32[]{:S(2)}, u32[]{:S(2)}) collective-permute-start(bf16[128,1024]{1,0:T(8,128)(2,1)} %shard_map.68.gates_ref), channel_id=1, source_target_pairs={{8,0},{16,8},{24,16},{0,24},{9,1},{17,9},{25,17},{1,25},{10,2},{18... | collective-permute-start | bytes 786440 | tf_op jit(solution)/shard_map/ppermute | solution.py:18
  29.0 5.8 %shard_map.70 = (f32[128,1024]{1,0:T(8,128)}, f32[128,1024]{1,0:T(8,128)}, f32[128,1024]{1,0:T(8,128)}, bf16[64,1024]{1,0:T(8,128)(2,1)}, bf16[64,1024]{1,0:T(8,128)(2,1)}) custom-call(bf16[128,1024]{1,0:T(8,128)(2,1)} %shard_map.68.gates_ref, bf16[1024,4096]{1,0:T(8,128)(2,1)} %tokens_hbm.1), custom_call_target="tpu_custom_call" | custom-call | flops 1073741824 | bytes 10485760 | tf_op jit(solution)/shard_map/pallas_call | solution.py:105
  34.8 0.0 collective-permute-done.2
  34.8 4.5 %collective-permute-done.1 = bf16[128,1024]{1,0:T(8,128)(2,1)S(1)} collective-permute-done((bf16[128,1024]{1,0:T(8,128)(2,1)}, bf16[128,1024]{1,0:T(8,128)(2,1)S(1)}, u32[]{:S(2)}, u32[]{:S(2)}) %collective-permute-start.1) | collective-permute-done | bytes 262176 | tf_op jit(solution)/shard_map/ppermute | solution.py:18
  39.3 0.0 collective-permute-done
  39.3 0.0 copy-done.3
  39.3 0.1 pad_maximum_fusion.mine_ref
  39.5 2.3 %collective-permute-start.3 = (bf16[4,128,1024]{2,1,0:T(8,128)(2,1)S(1)}, bf16[4,128,1024]{2,1,0:T(8,128)(2,1)S(1)}, u32[]{:S(2)}, u32[]{:S(2)}) collective-permute-start(bf16[4,128,1024]{2,1,0:T(8,128)(2,1)S(1)} %pad_maximum_fusion.mine_ref), channel_id=1, source_target_pairs={{4,0},{0,4},{5,1},{1,5},{6,2},{2,6},{7,3},{3,7},{12,8},{8,12},{13,... | collective-permute-start | bytes 3145736 | tf_op jit(solution)/shard_map/ppermute | solution.py:18
  41.8 8.5 %collective-permute-start.4 = (bf16[64,1024]{1,0:T(8,128)(2,1)}, bf16[64,1024]{1,0:T(8,128)(2,1)S(1)}, u32[]{:S(2)}, u32[]{:S(2)}) collective-permute-start(bf16[64,1024]{1,0:T(8,128)(2,1)} %get-tuple-element.24), channel_id=1, source_target_pairs={{3,0},{0,1},{1,2},{2,3},{7,4},{4,5},{5,6},{6,7},{11,8},{8,9},{9,10... | collective-permute-start | bytes 393224 | tf_op jit(solution)/shard_map/ppermute | solution.py:18
  50.3 1.9 %collective-permute-start.5 = (bf16[64,1024]{1,0:T(8,128)(2,1)}, bf16[64,1024]{1,0:T(8,128)(2,1)S(1)}, u32[]{:S(2)}, u32[]{:S(2)}) collective-permute-start(bf16[64,1024]{1,0:T(8,128)(2,1)} %get-tuple-element.25), channel_id=1, source_target_pairs={{1,0},{2,1},{3,2},{0,3},{5,4},{6,5},{7,6},{4,7},{9,8},{10,9},{11,1... | collective-permute-start | bytes 393224 | tf_op jit(solution)/shard_map/ppermute | solution.py:18
  52.3 0.1 stack.50.order
  52.3 0.0 collective-permute-done.3.other_ref
  52.3 0.0 all-to-all-done
  52.4 2.8 %shard_map.71 = bf16[512,1024]{1,0:T(8,128)(2,1)} custom-call(s32[8]{0:T(128)S(1)} %stack.50.order, bf16[4,8,128,128]{3,2,1,0:T(8,128)(2,1)S(1)} %bitcast.16, bf16[4,128,1024]{2,1,0:T(8,128)(2,1)S(1)} %pad_maximum_fusion.mine_ref, bf16[4,128,1024]{2,1,0:T(8,128)(2,1)S(1)} %collective-permute-done.3.other_ref), custom_call_target="tpu_custom_call" | custom-call | flops 1073741824 | bytes 4194304 | tf_op jit(solution)/shard_map/pallas_call | solution.py:163
  55.1 0.0 collective-permute-done.4.far_a_ref
  55.2 3.5 %collective-permute-done.5.far_b_ref = bf16[64,1024]{1,0:T(8,128)(2,1)S(1)} collective-permute-done((bf16[64,1024]{1,0:T(8,128)(2,1)}, bf16[64,1024]{1,0:T(8,128)(2,1)S(1)}, u32[]{:S(2)}, u32[]{:S(2)}) %collective-permute-start.5) | collective-permute-done | bytes 131104 | tf_op jit(solution)/shard_map/ppermute | solution.py:18
  58.7 11.1 %all-to-all-start.1 = ((bf16[16,32,1024]{2,1,0:T(8,128)(2,1)}), bf16[16,32,1024]{2,1,0:T(8,128)(2,1)S(1)}, u32[]{:S(2)}, u32[]{:S(2)}) async-start(bf16[16,32,1024]{2,1,0:T(8,128)(2,1)} %bitcast.14), calls=%async_computation.1 | async-start | bytes 2097152 | tf_op jit(solution)/shard_map/all_to_all | solution.py:215
  69.7 0.0 copy-start.1
  69.7 1.0 copy-done.1
  70.8 0.0 copy-start.2
  70.8 1.0 copy-done.2
  71.8 0.3 shard_map.73
  72.2 4.8 %collective-permute-start.6 = (bf16[128,1024]{1,0:T(8,128)(2,1)S(1)}, bf16[128,1024]{1,0:T(8,128)(2,1)S(1)}, u32[]{:S(2)}, u32[]{:S(2)}) collective-permute-start(bf16[128,1024]{1,0:T(8,128)(2,1)S(1)} %get-tuple-element.32), channel_id=1, source_target_pairs={{3,0},{0,1},{1,2},{2,3},{7,4},{4,5},{5,6},{6,7},{11,8},{8,9},{9,10... | collective-permute-start | bytes 786440 | tf_op jit(solution)/shard_map/ppermute | solution.py:18
  77.0 2.6 %collective-permute-start.7 = (bf16[128,1024]{1,0:T(8,128)(2,1)S(1)}, bf16[128,1024]{1,0:T(8,128)(2,1)S(1)}, u32[]{:S(2)}, u32[]{:S(2)}) collective-permute-start(bf16[128,1024]{1,0:T(8,128)(2,1)S(1)} %get-tuple-element.33), channel_id=1, source_target_pairs={{1,0},{2,1},{3,2},{0,3},{5,4},{6,5},{7,6},{4,7},{9,8},{10,9},{11,1... | collective-permute-start | bytes 786440 | tf_op jit(solution)/shard_map/ppermute | solution.py:18
  79.6 6.1 %collective-permute-done.6.refs_0_ = bf16[128,1024]{1,0:T(8,128)(2,1)S(1)} collective-permute-done((bf16[128,1024]{1,0:T(8,128)(2,1)S(1)}, bf16[128,1024]{1,0:T(8,128)(2,1)S(1)}, u32[]{:S(2)}, u32[]{:S(2)}) %collective-permute-start.6) | collective-permute-done | bytes 262176 | tf_op jit(solution)/shard_map/ppermute | solution.py:18
  85.6 15.9 %collective-permute-done.7.refs_1_ = bf16[128,1024]{1,0:T(8,128)(2,1)S(1)} collective-permute-done((bf16[128,1024]{1,0:T(8,128)(2,1)S(1)}, bf16[128,1024]{1,0:T(8,128)(2,1)S(1)}, u32[]{:S(2)}, u32[]{:S(2)}) %collective-permute-start.7) | collective-permute-done | bytes 262176 | tf_op jit(solution)/shard_map/ppermute | solution.py:18
  101.6 0.0 copy-start
  101.6 1.0 copy-done
  102.6 1.7 %shard_map.74 = bf16[1024,128]{1,0:T(8,128)(2,1)} custom-call(f32[128,1024]{1,0:T(8,128)S(1)} %copy-done, bf16[128,1024]{1,0:T(8,128)(2,1)S(1)} %collective-permute-done.6.refs_0_, bf16[128,1024]{1,0:T(8,128)(2,1)S(1)} %collective-permute-done.7.refs_1_), custom_call_target="tpu_custom_call" | custom-call | tf_op jit(solution)/shard_map/pallas_call | solution.py:143
  104.3 0.0 all-to-all-done.1.pieces_ref
  104.3 1.5 %shard_map.72 = bf16[32,1024]{1,0:T(8,128)(2,1)} custom-call(bf16[16,32,1024]{2,1,0:T(8,128)(2,1)S(1)} %all-to-all-done.1.pieces_ref), custom_call_target="tpu_custom_call" | custom-call | tf_op jit(solution)/shard_map/pallas_call | solution.py:183
Async XLA Ops:
  2.9 36.5 %copy-start.3 = (bf16[128,1024]{1,0:T(8,128)(2,1)S(1)}, bf16[128,1024]{1,0:T(8,128)(2,1)}, u32[]{:S(2)}) copy-start(bf16[128,1024]{1,0:T(8,128)(2,1)} %shard_map.68.gates_ref) | copy-start | bytes 786436
  5.0 47.3 %all-to-all-start = ((bf16[32,128,128]{2,1,0:T(8,128)(2,1)}), bf16[32,128,128]{2,1,0:T(8,128)(2,1)S(1)}, u32[]{:S(2)}, u32[]{:S(2)}) async-start(bf16[32,128,128]{2,1,0:T(8,128)(2,1)} %bitcast.17), calls=%async_computation | async-start | bytes 2097152 | tf_op jit(solution)/shard_map/all_to_all | solution.py:200
  17.7 17.1 %collective-permute-start.2 = (bf16[128,1024]{1,0:T(8,128)(2,1)}, bf16[128,1024]{1,0:T(8,128)(2,1)S(1)}, u32[]{:S(2)}, u32[]{:S(2)}) collective-permute-start(bf16[128,1024]{1,0:T(8,128)(2,1)} %shard_map.68.gates_ref), channel_id=1, source_target_pairs={{16,0},{24,8},{0,16},{8,24},{17,1},{25,9},{1,17},{9,25},{18,2},{26... | collective-permute-start | bytes 786440 | tf_op jit(solution)/shard_map/ppermute | solution.py:18
  22.5 16.8 %collective-permute-start.1 = (bf16[128,1024]{1,0:T(8,128)(2,1)}, bf16[128,1024]{1,0:T(8,128)(2,1)S(1)}, u32[]{:S(2)}, u32[]{:S(2)}) collective-permute-start(bf16[128,1024]{1,0:T(8,128)(2,1)} %shard_map.68.gates_ref), channel_id=1, source_target_pairs={{24,0},{0,8},{8,16},{16,24},{25,1},{1,9},{9,17},{17,25},{26,2},{2,... | collective-permute-start | bytes 786440 | tf_op jit(solution)/shard_map/ppermute | solution.py:18
  24.7 14.6 %collective-permute-start = (bf16[128,1024]{1,0:T(8,128)(2,1)}, bf16[128,1024]{1,0:T(8,128)(2,1)S(1)}, u32[]{:S(2)}, u32[]{:S(2)}) collective-permute-start(bf16[128,1024]{1,0:T(8,128)(2,1)} %shard_map.68.gates_ref), channel_id=1, source_target_pairs={{8,0},{16,8},{24,16},{0,24},{9,1},{17,9},{25,17},{1,25},{10,2},{18... | collective-permute-start | bytes 786440 | tf_op jit(solution)/shard_map/ppermute | solution.py:18
  39.5 12.9 %collective-permute-start.3 = (bf16[4,128,1024]{2,1,0:T(8,128)(2,1)S(1)}, bf16[4,128,1024]{2,1,0:T(8,128)(2,1)S(1)}, u32[]{:S(2)}, u32[]{:S(2)}) collective-permute-start(bf16[4,128,1024]{2,1,0:T(8,128)(2,1)S(1)} %pad_maximum_fusion.mine_ref), channel_id=1, source_target_pairs={{4,0},{0,4},{5,1},{1,5},{6,2},{2,6},{7,3},{3,7},{12,8},{8,12},{13,... | collective-permute-start | bytes 3145736 | tf_op jit(solution)/shard_map/ppermute | solution.py:18
  41.8 13.4 %collective-permute-start.4 = (bf16[64,1024]{1,0:T(8,128)(2,1)}, bf16[64,1024]{1,0:T(8,128)(2,1)S(1)}, u32[]{:S(2)}, u32[]{:S(2)}) collective-permute-start(bf16[64,1024]{1,0:T(8,128)(2,1)} %get-tuple-element.24), channel_id=1, source_target_pairs={{3,0},{0,1},{1,2},{2,3},{7,4},{4,5},{5,6},{6,7},{11,8},{8,9},{9,10... | collective-permute-start | bytes 393224 | tf_op jit(solution)/shard_map/ppermute | solution.py:18
  50.3 8.3 %collective-permute-start.5 = (bf16[64,1024]{1,0:T(8,128)(2,1)}, bf16[64,1024]{1,0:T(8,128)(2,1)S(1)}, u32[]{:S(2)}, u32[]{:S(2)}) collective-permute-start(bf16[64,1024]{1,0:T(8,128)(2,1)} %get-tuple-element.25), channel_id=1, source_target_pairs={{1,0},{2,1},{3,2},{0,3},{5,4},{6,5},{7,6},{4,7},{9,8},{10,9},{11,1... | collective-permute-start | bytes 393224 | tf_op jit(solution)/shard_map/ppermute | solution.py:18
  58.7 45.7 %all-to-all-start.1 = ((bf16[16,32,1024]{2,1,0:T(8,128)(2,1)}), bf16[16,32,1024]{2,1,0:T(8,128)(2,1)S(1)}, u32[]{:S(2)}, u32[]{:S(2)}) async-start(bf16[16,32,1024]{2,1,0:T(8,128)(2,1)} %bitcast.14), calls=%async_computation.1 | async-start | bytes 2097152 | tf_op jit(solution)/shard_map/all_to_all | solution.py:215
  69.7 1.0 copy-start.1
  70.8 1.0 copy-start.2
  72.2 13.5 %collective-permute-start.6 = (bf16[128,1024]{1,0:T(8,128)(2,1)S(1)}, bf16[128,1024]{1,0:T(8,128)(2,1)S(1)}, u32[]{:S(2)}, u32[]{:S(2)}) collective-permute-start(bf16[128,1024]{1,0:T(8,128)(2,1)S(1)} %get-tuple-element.32), channel_id=1, source_target_pairs={{3,0},{0,1},{1,2},{2,3},{7,4},{4,5},{5,6},{6,7},{11,8},{8,9},{9,10... | collective-permute-start | bytes 786440 | tf_op jit(solution)/shard_map/ppermute | solution.py:18
  77.0 24.6 %collective-permute-start.7 = (bf16[128,1024]{1,0:T(8,128)(2,1)S(1)}, bf16[128,1024]{1,0:T(8,128)(2,1)S(1)}, u32[]{:S(2)}, u32[]{:S(2)}) collective-permute-start(bf16[128,1024]{1,0:T(8,128)(2,1)S(1)} %get-tuple-element.33), channel_id=1, source_target_pairs={{1,0},{2,1},{3,2},{0,3},{5,4},{6,5},{7,6},{4,7},{9,8},{10,9},{11,1... | collective-permute-start | bytes 786440 | tf_op jit(solution)/shard_map/ppermute | solution.py:18
  101.6 1.0 copy-start

commit v4 on v2

--- a/solution.py
+++ b/solution.py
@@ -82,7 +82,7 @@
     m = lax.axis_index("mp")
     copies = []
     for step in range(8):
-        column = jnp.bitwise_and(m + (TURNS + (0,))[step // 2], 3) * 1024 + step % 2 * 512
+        column = jnp.bitwise_and(m + ((2, 1, 3, 0)[step // 2]), 3) * 1024 + step % 2 * 512
         copy = pltpu.make_async_copy(
             tokens_hbm.at[:, pl.ds(pl.multiple_of(column, 512), 512)], tokens.at[step], sems.at[step]
         )
@@ -90,7 +90,7 @@
         copies.append(copy)
     for step, copy in enumerate(copies):
         copy.wait()
-        out_ref = (a_ref, b_ref, c_ref, own_ref)[step // 2]
+        out_ref = (c_ref, a_ref, b_ref, own_ref)[step // 2]
         share = jnp.dot(gates_ref[...], tokens[step], preferred_element_type=F32)
         out_ref[:, step % 2 * 512 : (step % 2 + 1) * 512] = share.astype(out_ref.dtype)
 
@@ -126,29 +126,29 @@
     )(own, *away)
 
 
-def partial_kernel(order, rows_ref, *refs):
-    gates, out_ref, rows, block = refs[:8], refs[8], refs[9], refs[10]
+def partial_kernel(order, rows_ref, mine_ref, other_ref, out_ref, rows):
     for k in range(8):
         for m in range(4):
             rows[m * 128 : (m + 1) * 128, k * 128 : (k + 1) * 128] = rows_ref[m, order[k]]
-        block[k * 128 : (k + 1) * 128, :] = gates[k][...]
-    out_ref[...] = jnp.dot(rows[...], block[...], preferred_element_type=F32).astype(BF16)
-
-
-def partial_product(order, rows, gates):
+    total = jnp.dot(rows[:, :512], mine_ref[...].reshape(512, 1024), preferred_element_type=F32)
+    total += jnp.dot(rows[:, 512:], other_ref[...].reshape(512, 1024), preferred_element_type=F32)
+    out_ref[...] = total.astype(BF16)
+
+
+def partial_product(order, rows, mine, other):
     return pl.pallas_call(
         partial_kernel,
         grid_spec=pltpu.PrefetchScalarGridSpec(
             num_scalar_prefetch=1,
             grid=(1,),
-            in_specs=[whole((4, 8, 128, 128))] + [whole((128, 1024))] * 8,
+            in_specs=[whole((4, 8, 128, 128))] + [whole((4, 128, 1024))] * 2,
             out_specs=whole((512, 1024)),
-            scratch_shapes=[pltpu.VMEM((512, 1024), BF16), pltpu.VMEM((1024, 1024), BF16)],
+            scratch_shapes=[pltpu.VMEM((512, 1024), BF16)],
         ),
         out_shape=jax.ShapeDtypeStruct((512, 1024), BF16),
         compiler_params=params(),
         cost_estimate=pl.CostEstimate(flops=1 << 30, bytes_accessed=4 << 20, transcendentals=0),
-    )(order, rows, *gates)
+    )(order, rows, mine, other)
 
 
 def sum_kernel(pieces_ref, out_ref):
@@ -170,26 +170,34 @@
     x, c = lax.axis_index("x"), lax.axis_index("c")
     norm_factor = float(tokens.shape[0] * lax.axis_size("mp")) ** (-0.5)
 
-    gates = gate_gradient(gate_pre, up_value, grad_hidden)
-    mine = [gates] + [shift(gates, "x", 4, k) for k in TURNS]
-    other = [shift(block, "c", 2, 1) for block in mine]
-
     rows = spread_rows(gate_weight).reshape(32, 128, 128)
     rows = lax.all_to_all(rows, ("mp", "x", "c"), 0, 0, tiled=True).reshape(4, 8, 128, 128)
 
+    gates = gate_gradient(gate_pre, up_value, grad_hidden)
+    mine = [shift(gates, "x", 4, k) for k in TURNS]
     own, *shares = weight_shares(gates, tokens)
+    *mine, own = lax.optimization_barrier((*mine, own))
     away = [shift(share, "mp", 4, -k) for k, share in zip(TURNS, shares)]
+    mine = jnp.stack([gates, *mine])
+    other = shift(mine, "c", 2, 1)
 
     order = jnp.stack(
         [((x + k) & 3) * 2 + c for k in (0,) + TURNS]
         + [((x + k) & 3) * 2 + 1 - c for k in (0,) + TURNS]
     ).astype(jnp.int32)
-    order, away[0] = lax.optimization_barrier((order, away[0]))
-    partial_sums = partial_product(order, rows, mine + other)
-    pieces = lax.all_to_all(partial_sums.reshape(16, 32, 1024), ("zl", "y"), 0, 0, tiled=True)
-    grad_tokens = sum_pieces(pieces).T
+
+    def exchange(order, rows, mine, other):
+        partial_sums = partial_product(order, rows, mine, other)
+        pieces = lax.all_to_all(partial_sums.reshape(16, 32, 1024), ("zl", "y"), 0, 0, tiled=True)
+        return sum_pieces(pieces)
+
+    def never(order, rows, mine, other):
+        return jnp.zeros((32, 1024), BF16)
+
+    grad_tokens = lax.cond(order[0] >= 0, exchange, never, order, rows, mine, other)
+    grad_tokens, own, *away = lax.optimization_barrier((grad_tokens, own, *away))
     grad_gate_weight = add_shares(own, away, norm_factor)
-    return (grad_tokens, grad_gate_weight)
+    return (grad_tokens.T, grad_gate_weight)
 
 
 def solution(mesh):

time: 111 us -> 101 us (0.910)
  the two profiles are of different devices: /device:TPU:65 before, /device:TPU:8 now
where the time goes in v4:
time: 101 us
  starting transfers between devices  42.1 us (42%)
  blocking collectives  34.6 us (34%)
  Pallas kernels  15.1 us (15%)
  waiting for transfers between devices  7.8 us (8%)
    all_to_all x1, blocking collectives, exchange(): lax.all_to_all(partial_sums.reshape(16, 32, 1024), ('zl', 'y'), 0, 0, til...  34.6 us
    ppermute x7, starting transfers between devices, shift(): lax.ppermute(array, axis, [((i + by) % size, i) for i in range(size)])  28.9 us
    all_to_all x1, starting transfers between devices, body(): lax.all_to_all(rows, ('mp', 'x', 'c'), 0, 0, tiled=True)  13.2 us
    ppermute x7, waiting for transfers between devices, shift(): lax.ppermute(array, axis, [((i + by) % size, i) for i in range(size)])  7.79 us
    pallas_call x1, Pallas kernels, weight_shares(): pl.pallas_call(share_kernel, in_specs=[IN_VMEM, IN_HBM], out_specs=[IN_VM...  5.62 us
    pallas_call x1, Pallas kernels, partial_product(): pl.pallas_call(partial_kernel, grid_spec=pltpu.PrefetchScalarGridSpec(num...  3.02 us
    pallas_call x1, Pallas kernels, gate_gradient(): pl.pallas_call(gate_kernel, in_specs=[IN_HBM] * 3, out_specs=IN_VMEM, scr...  2.23 us
    pallas_call x1, Pallas kernels, spread_rows(): pl.pallas_call(spread_kernel, in_specs=[IN_HBM], out_specs=IN_VMEM, scrat...  2.08 us
  transfers between devices with their start and end apart: 8, of which 2 were waited for; matrix products, arithmetic and copies ran while one was open for 0% of the time, Pallas kernels for 11%

profile of v4, /device:TPU:8, one launch (start us, length us, event | category | flops | bytes accessed | tf_op | source)
XLA Modules:
  0.0 100.6 jit_solution(8342832524743689577)
XLA Ops:
  0.6 2.1 %shard_map.68 = bf16[4,8,128,128]{3,2,1,0:T(8,128)(2,1)} custom-call(bf16[1024,128]{1,0:T(8,128)(2,1)} %weight_ref.1), custom_call_target="tpu_custom_call" | custom-call | tf_op jit(solution)/shard_map/pallas_call | solution.py:41
  2.7 13.2 %all-to-all-start.1 = ((bf16[32,128,128]{2,1,0:T(8,128)(2,1)}), bf16[32,128,128]{2,1,0:T(8,128)(2,1)S(1)}, u32[]{:S(2)}, u32[]{:S(2)}) async-start(bf16[32,128,128]{2,1,0:T(8,128)(2,1)} %bitcast.18), calls=%async_computation.1 | async-start | bytes 2097152 | tf_op jit(solution)/shard_map/all_to_all | solution.py:174
  15.9 2.2 %shard_map.69.gates_ref = bf16[128,1024]{1,0:T(8,128)(2,1)} custom-call(bf16[1024,128]{1,0:T(8,128)(2,1)} %gate_hbm.1, bf16[1024,128]{1,0:T(8,128)(2,1)} %up_hbm.1, bf16[1024,128]{1,0:T(8,128)(2,1)} %hidden_hbm.1), custom_call_target="tpu_custom_call" | custom-call | tf_op jit(solution)/shard_map/pallas_call | solution.py:71
  18.1 0.0 copy-start.1
  18.1 5.3 %collective-permute-start.2 = (bf16[128,1024]{1,0:T(8,128)(2,1)}, bf16[128,1024]{1,0:T(8,128)(2,1)S(1)}, u32[]{:S(2)}, u32[]{:S(2)}) collective-permute-start(bf16[128,1024]{1,0:T(8,128)(2,1)} %shard_map.69.gates_ref), channel_id=1, source_target_pairs={{16,0},{24,8},{0,16},{8,24},{17,1},{25,9},{1,17},{9,25},{18,2},{26... | collective-permute-start | bytes 786440 | tf_op jit(solution)/shard_map/ppermute | solution.py:18
  23.5 2.5 %collective-permute-start.1 = (bf16[128,1024]{1,0:T(8,128)(2,1)}, bf16[128,1024]{1,0:T(8,128)(2,1)S(1)}, u32[]{:S(2)}, u32[]{:S(2)}) collective-permute-start(bf16[128,1024]{1,0:T(8,128)(2,1)} %shard_map.69.gates_ref), channel_id=1, source_target_pairs={{24,0},{0,8},{8,16},{16,24},{25,1},{1,9},{9,17},{17,25},{26,2},{2,... | collective-permute-start | bytes 786440 | tf_op jit(solution)/shard_map/ppermute | solution.py:18
  26.0 4.6 %collective-permute-start = (bf16[128,1024]{1,0:T(8,128)(2,1)}, bf16[128,1024]{1,0:T(8,128)(2,1)S(1)}, u32[]{:S(2)}, u32[]{:S(2)}) collective-permute-start(bf16[128,1024]{1,0:T(8,128)(2,1)} %shard_map.69.gates_ref), channel_id=1, source_target_pairs={{8,0},{16,8},{24,16},{0,24},{9,1},{17,9},{25,17},{1,25},{10,2},{18... | collective-permute-start | bytes 786440 | tf_op jit(solution)/shard_map/ppermute | solution.py:18
  30.5 5.6 %shard_map.70 = (f32[128,1024]{1,0:T(8,128)}, bf16[128,1024]{1,0:T(8,128)(2,1)}, bf16[128,1024]{1,0:T(8,128)(2,1)}, bf16[128,1024]{1,0:T(8,128)(2,1)}) custom-call(bf16[128,1024]{1,0:T(8,128)(2,1)} %shard_map.69.gates_ref, bf16[1024,4096]{1,0:T(8,128)(2,1)} %tokens_hbm.1), custom_call_target="tpu_custom_call" | custom-call | flops 1073741824 | bytes 10485760 | tf_op jit(solution)/shard_map/pallas_call | solution.py:99
  36.2 0.0 copy-start
  36.2 1.7 %collective-permute-done.2 = bf16[128,1024]{1,0:T(8,128)(2,1)S(1)} collective-permute-done((bf16[128,1024]{1,0:T(8,128)(2,1)}, bf16[128,1024]{1,0:T(8,128)(2,1)S(1)}, u32[]{:S(2)}, u32[]{:S(2)}) %collective-permute-start.2) | collective-permute-done | bytes 262176 | tf_op jit(solution)/shard_map/ppermute | solution.py:18
  37.9 6.0 %collective-permute-done.1 = bf16[128,1024]{1,0:T(8,128)(2,1)S(1)} collective-permute-done((bf16[128,1024]{1,0:T(8,128)(2,1)}, bf16[128,1024]{1,0:T(8,128)(2,1)S(1)}, u32[]{:S(2)}, u32[]{:S(2)}) %collective-permute-start.1) | collective-permute-done | bytes 262176 | tf_op jit(solution)/shard_map/ppermute | solution.py:18
  44.0 0.0 collective-permute-done
  44.0 0.0 copy-done.1
  44.0 0.1 pad_maximum_fusion
  44.1 2.0 %collective-permute-start.3 = (bf16[4,128,1024]{2,1,0:T(8,128)(2,1)S(1)}, bf16[4,128,1024]{2,1,0:T(8,128)(2,1)}, u32[]{:S(2)}, u32[]{:S(2)}) collective-permute-start(bf16[4,128,1024]{2,1,0:T(8,128)(2,1)S(1)} %pad_maximum_fusion), channel_id=1, source_target_pairs={{4,0},{0,4},{5,1},{1,5},{6,2},{2,6},{7,3},{3,7},{12,8},{8,12},{13,... | collective-permute-start | bytes 3145736 | tf_op jit(solution)/shard_map/ppermute | solution.py:18
  46.1 3.4 %collective-permute-start.4 = (bf16[128,1024]{1,0:T(8,128)(2,1)}, bf16[128,1024]{1,0:T(8,128)(2,1)S(1)}, u32[]{:S(2)}, u32[]{:S(2)}) collective-permute-start(bf16[128,1024]{1,0:T(8,128)(2,1)} %get-tuple-element.36), channel_id=1, source_target_pairs={{3,0},{0,1},{1,2},{2,3},{7,4},{4,5},{5,6},{6,7},{11,8},{8,9},{9,10... | collective-permute-start | bytes 786440 | tf_op jit(solution)/shard_map/ppermute | solution.py:18
  49.5 4.6 %collective-permute-start.5 = (bf16[128,1024]{1,0:T(8,128)(2,1)}, bf16[128,1024]{1,0:T(8,128)(2,1)S(1)}, u32[]{:S(2)}, u32[]{:S(2)}) collective-permute-start(bf16[128,1024]{1,0:T(8,128)(2,1)} %get-tuple-element.37), channel_id=1, source_target_pairs={{1,0},{2,1},{3,2},{0,3},{5,4},{6,5},{7,6},{4,7},{9,8},{10,9},{11,1... | collective-permute-start | bytes 786440 | tf_op jit(solution)/shard_map/ppermute | solution.py:18
  54.1 6.5 %collective-permute-start.6 = (bf16[128,1024]{1,0:T(8,128)(2,1)}, bf16[128,1024]{1,0:T(8,128)(2,1)S(1)}, u32[]{:S(2)}, u32[]{:S(2)}) collective-permute-start(bf16[128,1024]{1,0:T(8,128)(2,1)} %get-tuple-element.38), channel_id=1, source_target_pairs={{2,0},{3,1},{0,2},{1,3},{6,4},{7,5},{4,6},{5,7},{10,8},{11,9},{8,1... | collective-permute-start | bytes 786440 | tf_op jit(solution)/shard_map/ppermute | solution.py:18
  60.7 0.1 stack.50
  60.7 0.0 collective-permute-done.3
  60.7 0.0 all-to-all-done.1
  60.8 38.0 %conditional.1 = (bf16[32,1024]{1,0:T(8,128)(2,1)S(1)}) conditional(s32[]{:T(128)} %convert_element_type.3, () %tuple.16, (bf16[32,128,128]{2,1,0:T(8,128)(2,1)S(1)}, s32[8]{0:T(128)S(1)}, bf16[4,128,1024]{2,1,0:T(8,128)(2,1)S(1)}, bf16[4,128,1024]{2,1,0:T(8,128)(2,1)}) %tuple.18), branch_computations={%region_0.0_spmd, %region_1.0_spmd} | conditional | flops 1073741824 | bytes 6291464 | solution.py:197
  60.8 3.0 %branch_1_fun.2 = bf16[512,1024]{1,0:T(8,128)(2,1)S(1)} custom-call(s32[8]{0:T(128)S(1)} %get-tuple-element.12.order, bf16[4,8,128,128]{3,2,1,0:T(8,128)(2,1)S(1)} %bitcast.17, bf16[4,128,1024]{2,1,0:T(8,128)(2,1)S(1)} %get-tuple-element.14.mine_ref, bf16[4,128,1024]{2,1,0:T(8,128)(2,1)} %get-tuple-element.15.other_ref), custom_call_target="tpu_custom_call" | custom-call | flops 1073741824 | bytes 4194304 | tf_op jit(solution)/shard_map/cond/branch_1_fun/pallas_call | solution.py:139
  63.8 34.6 %all_to_all.9.pieces_ref = bf16[16,32,1024]{2,1,0:T(8,128)(2,1)S(1)} all-to-all(bf16[16,32,1024]{2,1,0:T(8,128)(2,1)S(1)} %bitcast.16), channel_id=1, replica_groups=mesh['zl'=2,'y'=8,'x'=4,'c'=2,'mp'=4] {'zl','y'}, dimensions={0} | all-to-all | bytes 2097152 | tf_op jit(solution)/shard_map/cond/branch_1_fun/all_to_all | solution.py:191
  98.4 0.4 branch_1_fun.3
  98.8 0.0 copy-start.2
  98.8 0.0 collective-permute-done.4.refs_0_
  98.8 0.0 collective-permute-done.5.refs_1_
  98.8 0.0 collective-permute-done.6.refs_2_
  98.8 0.0 copy-done
  98.9 1.7 %shard_map.71 = bf16[1024,128]{1,0:T(8,128)(2,1)} custom-call(f32[128,1024]{1,0:T(8,128)S(1)} %copy-done, bf16[128,1024]{1,0:T(8,128)(2,1)S(1)} %collective-permute-done.4.refs_0_, bf16[128,1024]{1,0:T(8,128)(2,1)S(1)} %collective-permute-done.5.refs_1_, bf16[128,1024]{1,0:T(8,128)(2,1)S(1)} %collective-permute-done.6.refs_2_), custom_call_target="tpu_custom_call" | custom-call | tf_op jit(solution)/shard_map/pallas_call | solution.py:119
  100.6 0.0 copy-done.2
Async XLA Ops:
  2.7 58.0 %all-to-all-start.1 = ((bf16[32,128,128]{2,1,0:T(8,128)(2,1)}), bf16[32,128,128]{2,1,0:T(8,128)(2,1)S(1)}, u32[]{:S(2)}, u32[]{:S(2)}) async-start(bf16[32,128,128]{2,1,0:T(8,128)(2,1)} %bitcast.18), calls=%async_computation.1 | async-start | bytes 2097152 | tf_op jit(solution)/shard_map/all_to_all | solution.py:174
  18.1 25.8 %copy-start.1 = (bf16[128,1024]{1,0:T(8,128)(2,1)S(1)}, bf16[128,1024]{1,0:T(8,128)(2,1)}, u32[]{:S(2)}) copy-start(bf16[128,1024]{1,0:T(8,128)(2,1)} %shard_map.69.gates_ref) | copy-start | bytes 786436
  18.1 19.8 %collective-permute-start.2 = (bf16[128,1024]{1,0:T(8,128)(2,1)}, bf16[128,1024]{1,0:T(8,128)(2,1)S(1)}, u32[]{:S(2)}, u32[]{:S(2)}) collective-permute-start(bf16[128,1024]{1,0:T(8,128)(2,1)} %shard_map.69.gates_ref), channel_id=1, source_target_pairs={{16,0},{24,8},{0,16},{8,24},{17,1},{25,9},{1,17},{9,25},{18,2},{26... | collective-permute-start | bytes 786440 | tf_op jit(solution)/shard_map/ppermute | solution.py:18
  23.5 20.5 %collective-permute-start.1 = (bf16[128,1024]{1,0:T(8,128)(2,1)}, bf16[128,1024]{1,0:T(8,128)(2,1)S(1)}, u32[]{:S(2)}, u32[]{:S(2)}) collective-permute-start(bf16[128,1024]{1,0:T(8,128)(2,1)} %shard_map.69.gates_ref), channel_id=1, source_target_pairs={{24,0},{0,8},{8,16},{16,24},{25,1},{1,9},{9,17},{17,25},{26,2},{2,... | collective-permute-start | bytes 786440 | tf_op jit(solution)/shard_map/ppermute | solution.py:18
  26.0 18.0 %collective-permute-start = (bf16[128,1024]{1,0:T(8,128)(2,1)}, bf16[128,1024]{1,0:T(8,128)(2,1)S(1)}, u32[]{:S(2)}, u32[]{:S(2)}) collective-permute-start(bf16[128,1024]{1,0:T(8,128)(2,1)} %shard_map.69.gates_ref), channel_id=1, source_target_pairs={{8,0},{16,8},{24,16},{0,24},{9,1},{17,9},{25,17},{1,25},{10,2},{18... | collective-permute-start | bytes 786440 | tf_op jit(solution)/shard_map/ppermute | solution.py:18
  36.2 62.7 %copy-start = (f32[128,1024]{1,0:T(8,128)S(1)}, f32[128,1024]{1,0:T(8,128)}, u32[]{:S(2)}) copy-start(f32[128,1024]{1,0:T(8,128)} %get-tuple-element.40.own_ref) | copy-start | bytes 1572868
  44.1 16.6 %collective-permute-start.3 = (bf16[4,128,1024]{2,1,0:T(8,128)(2,1)S(1)}, bf16[4,128,1024]{2,1,0:T(8,128)(2,1)}, u32[]{:S(2)}, u32[]{:S(2)}) collective-permute-start(bf16[4,128,1024]{2,1,0:T(8,128)(2,1)S(1)} %pad_maximum_fusion), channel_id=1, source_target_pairs={{4,0},{0,4},{5,1},{1,5},{6,2},{2,6},{7,3},{3,7},{12,8},{8,12},{13,... | collective-permute-start | bytes 3145736 | tf_op jit(solution)/shard_map/ppermute | solution.py:18
  46.1 52.7 %collective-permute-start.4 = (bf16[128,1024]{1,0:T(8,128)(2,1)}, bf16[128,1024]{1,0:T(8,128)(2,1)S(1)}, u32[]{:S(2)}, u32[]{:S(2)}) collective-permute-start(bf16[128,1024]{1,0:T(8,128)(2,1)} %get-tuple-element.36), channel_id=1, source_target_pairs={{3,0},{0,1},{1,2},{2,3},{7,4},{4,5},{5,6},{6,7},{11,8},{8,9},{9,10... | collective-permute-start | bytes 786440 | tf_op jit(solution)/shard_map/ppermute | solution.py:18
  49.5 49.3 %collective-permute-start.5 = (bf16[128,1024]{1,0:T(8,128)(2,1)}, bf16[128,1024]{1,0:T(8,128)(2,1)S(1)}, u32[]{:S(2)}, u32[]{:S(2)}) collective-permute-start(bf16[128,1024]{1,0:T(8,128)(2,1)} %get-tuple-element.37), channel_id=1, source_target_pairs={{1,0},{2,1},{3,2},{0,3},{5,4},{6,5},{7,6},{4,7},{9,8},{10,9},{11,1... | collective-permute-start | bytes 786440 | tf_op jit(solution)/shard_map/ppermute | solution.py:18
  54.1 44.7 %collective-permute-start.6 = (bf16[128,1024]{1,0:T(8,128)(2,1)}, bf16[128,1024]{1,0:T(8,128)(2,1)S(1)}, u32[]{:S(2)}, u32[]{:S(2)}) collective-permute-start(bf16[128,1024]{1,0:T(8,128)(2,1)} %get-tuple-element.38), channel_id=1, source_target_pairs={{2,0},{3,1},{0,2},{1,3},{6,4},{7,5},{4,6},{5,7},{10,8},{11,9},{8,1... | collective-permute-start | bytes 786440 | tf_op jit(solution)/shard_map/ppermute | solution.py:18
  98.8 1.8 %copy-start.2 = (bf16[32,1024]{1,0:T(8,128)(2,1)}, bf16[32,1024]{1,0:T(8,128)(2,1)S(1)}, u32[]{:S(2)}) copy-start(bf16[32,1024]{1,0:T(8,128)(2,1)S(1)} %get-tuple-element.44) | copy-start | bytes 196612

commit v5 on v4

v5 whole, which is shorter than its diff:
```python
import functools

import jax
import jax.numpy as jnp
from jax import lax
from jax.experimental import pallas as pl
from jax.experimental.pallas import tpu as pltpu
from jax.sharding import Mesh, PartitionSpec as P

TURNS = (1, 3, 2)
AXES = ("zl", "y", "x", "c", "mp")
BF16, F32 = jnp.bfloat16, jnp.float32
IN_HBM = pl.BlockSpec(memory_space=pltpu.HBM)
IN_VMEM = pl.BlockSpec(memory_space=pltpu.VMEM)


def shift(array, axis, size, by):
    return lax.ppermute(array, axis, [((i + by) % size, i) for i in range(size)])


def params(limit=24):
    return pltpu.CompilerParams(vmem_limit_bytes=limit << 20)


def spread_kernel(weight_ref, out_ref, sems):
    copies = [
        pltpu.make_async_copy(weight_ref.at[:, k], out_ref.at[m, k], sems.at[m, k])
        for m in range(4)
        for k in range(8)
    ]
    for copy in copies:
        copy.start()
    for copy in copies:
        copy.wait()


def spread_rows(weight):
    return pl.pallas_call(
        spread_kernel,
        in_specs=[IN_HBM],
        out_specs=IN_HBM,
        scratch_shapes=[pltpu.SemaphoreType.DMA((4, 8))],
        out_shape=jax.ShapeDtypeStruct((4, 8, 4, 32, 128), BF16),
        compiler_params=params(58),
    )(weight.reshape(4, 8, 32, 128))


def gate_kernel(gate_hbm, up_hbm, hidden_hbm, out_ref, *scratch):
    sems = scratch[3]
    copies = []
    for step in range(4):
        rows = pl.ds(step * 256, 256)
        for n, source in enumerate((gate_hbm, up_hbm, hidden_hbm)):
            copy = pltpu.make_async_copy(source.at[rows], scratch[n].at[rows], sems.at[n, step])
            copy.start()
            copies.append(copy)
    for step in range(4):
        rows = pl.ds(step * 256, 256)
        for copy in copies[step * 3 : step * 3 + 3]:
            copy.wait()
        gate, up, hidden = (ref[rows].astype(F32) for ref in scratch[:3])
        sigma = jax.nn.sigmoid(gate)
        product = hidden * up * sigma * (1.0 + gate * (1.0 - sigma))
        out_ref[:, rows] = product.T.astype(BF16)


def gate_gradient(gate_pre, up_value, grad_hidden):
    return pl.pallas_call(
        gate_kernel,
        in_specs=[IN_HBM] * 3,
        out_specs=IN_VMEM,
        scratch_shapes=[pltpu.VMEM((1024, 128), BF16)] * 3 + [pltpu.SemaphoreType.DMA((3, 4))],
        out_shape=jax.ShapeDtypeStruct((128, 1024), BF16),
        compiler_params=params(58),
    )(gate_pre, up_value, grad_hidden)


def share_kernel(gates_ref, tokens_hbm, own_ref, right_ref, left_ref, far_ref, tokens, sems):
    m = lax.axis_index("mp")
    copies = []
    for step in range(8):
        column = jnp.bitwise_and(m + (2, 1, 3, 0)[step // 2], 3) * 1024 + step % 2 * 512
        copy = pltpu.make_async_copy(
            tokens_hbm.at[:, pl.ds(pl.multiple_of(column, 512), 512)], tokens.at[step], sems.at[step]
        )
        copy.start()
        copies.append(copy)
    for step, copy in enumerate(copies):
        copy.wait()
        out_ref = (far_ref, right_ref, left_ref, own_ref)[step // 2]
        share = jnp.dot(gates_ref[...], tokens[step], preferred_element_type=F32)
        out_ref[:, step % 2 * 512 : (step % 2 + 1) * 512] = share.astype(out_ref.dtype)


def weight_shares(gates, tokens):
    return pl.pallas_call(
        share_kernel,
        in_specs=[IN_VMEM, IN_HBM],
        out_specs=[IN_VMEM] * 4,
        scratch_shapes=[pltpu.VMEM((8, 1024, 512), BF16), pltpu.SemaphoreType.DMA((8,))],
        out_shape=[jax.ShapeDtypeStruct((128, 1024), F32)]
        + [jax.ShapeDtypeStruct((128, 1024), BF16)] * 3,
        compiler_params=params(54),
        cost_estimate=pl.CostEstimate(flops=1 << 30, bytes_accessed=10 << 20, transcendentals=0),
    )(gates, tokens)


def add_kernel(scale, own_ref, right_ref, left_ref, far_ref, out_ref):
    total = own_ref[...]
    for ref in (right_ref, left_ref, far_ref):
        total += ref[...].astype(F32)
    out_ref[...] = (total * scale).T.astype(BF16)


def add_shares(own, away, scale):
    return pl.pallas_call(
        functools.partial(add_kernel, scale),
        in_specs=[IN_VMEM] * 4,
        out_specs=IN_VMEM,
        out_shape=jax.ShapeDtypeStruct((1024, 128), BF16),
        compiler_params=params(),
    )(own, *away)


def partial_kernel(rows_ref, mine_ref, other_ref, out_ref, rows):
    x, c = lax.axis_index("x"), lax.axis_index("c")
    for k in range(8):
        turn = ((0,) + TURNS)[k % 4]
        source = jnp.bitwise_and(x + turn, 3) * 2 + (c if k < 4 else 1 - c)
        for m in range(4):
            rows[m * 128 : (m + 1) * 128, k * 128 : (k + 1) * 128] = rows_ref[m, source]
    for t in range(2):
        columns = pl.ds(t * 512, 512)
        total = jnp.dot(
            rows[:, :512], mine_ref[:, :, columns].reshape(512, 512), preferred_element_type=F32
        )
        total += jnp.dot(
            rows[:, 512:], other_ref[:, :, columns].reshape(512, 512), preferred_element_type=F32
        )
        out_ref[:, columns] = total.astype(BF16)


def partial_product(rows, mine, other):
    return pl.pallas_call(
        partial_kernel,
        in_specs=[IN_VMEM] * 3,
        out_specs=IN_VMEM,
        scratch_shapes=[pltpu.VMEM((512, 1024), BF16)],
        out_shape=jax.ShapeDtypeStruct((512, 1024), BF16),
        compiler_params=params(),
        cost_estimate=pl.CostEstimate(flops=1 << 30, bytes_accessed=4 << 20, transcendentals=0),
    )(rows, mine, other)


def sum_kernel(pieces_ref, out_ref):
    out_ref[...] = jnp.sum(pieces_ref[...].astype(F32), axis=0).astype(BF16)


def sum_pieces(pieces):
    return pl.pallas_call(
        sum_kernel,
        in_specs=[IN_VMEM],
        out_specs=IN_VMEM,
        out_shape=jax.ShapeDtypeStruct((32, 1024), BF16),
        compiler_params=params(),
    )(pieces)


def always(function, *operands):
    shapes = jax.eval_shape(function, *operands)

    def never(*_):
        return jax.tree.map(lambda shape: jnp.zeros(shape.shape, shape.dtype), shapes)

    return lax.cond(lax.axis_index("x") * 2 + lax.axis_index("c") >= 0, function, never, *operands)


def body(tokens, gate_pre, up_value, grad_hidden, gate_weight):
    norm_factor = float(tokens.shape[0] * lax.axis_size("mp")) ** (-0.5)

    rows = spread_rows(gate_weight).reshape(32, 128, 128)
    rows = lax.all_to_all(rows, ("mp", "x", "c"), 0, 0, tiled=True).reshape(4, 8, 128, 128)

    gates = gate_gradient(gate_pre, up_value, grad_hidden)
    mine = [shift(gates, "x", 4, k) for k in TURNS]
    own, *shares = weight_shares(gates, tokens)
    *mine, own = lax.optimization_barrier((*mine, own))
    away = [shift(share, "mp", 4, -k) for k, share in zip(TURNS, shares)]

    def exchange(rows, *mine):
        mine = jnp.stack(mine)
        partial_sums = partial_product(rows, mine, shift(mine, "c", 2, 1))
        pieces = lax.all_to_all(partial_sums.reshape(16, 32, 1024), ("zl", "y"), 0, 0, tiled=True)
        return sum_pieces(pieces)

    grad_tokens = always(exchange, rows, gates, *mine)
    grad_tokens, own, *away = lax.optimization_barrier((grad_tokens, own, *away))
    return (grad_tokens.T, add_shares(own, away, norm_factor))


def solution(mesh):
    fine = Mesh(mesh.devices.reshape(2, 8, 4, 2, 4), AXES)
    dp = ("zl", "y", "x", "c")
    in_specs = (P("mp", None), P("mp", dp), P("mp", dp), P("mp", dp), P("mp", dp))
    out_specs = (P("mp", dp), P("mp", dp))
    return jax.shard_map(body, mesh=fine, in_specs=in_specs, out_specs=out_specs, check_vma=False)
```

time: 101 us -> 125 us (1.24)
  Pallas kernels: 15.1 us -> 41.7 us
  waiting for transfers between devices: 7.8 us -> 2.64 us
  blocking collectives: 34.6 us -> 36.3 us
    pallas_call x4, Pallas kernels: 7.24 us -> 35.5 us  [the longest x1 33.2 us: spread_rows(): pl.pallas_call(spread_kernel, in_specs=[IN_HBM], out_specs=IN_HBM, scratc...]
    ppermute x7, waiting for transfers between devices: 7.79 us -> 2.64 us  [shift(): lax.ppermute(array, axis, [((i + by) % size, i) for i in range(size)])]
    all_to_all x1, blocking collectives: 34.6 us -> 36.3 us  [exchange(): lax.all_to_all(partial_sums.reshape(16, 32, 1024), ('zl', 'y'), 0, 0, til...]
  transfers between devices with their start and end apart: 8 -> 8, of which waited for: 2 -> 1; matrix products, arithmetic and copies ran while one was open for 0% -> 0% of each run, Pallas kernels for 11% -> 6%
where the time goes in v5:
time: 125 us; the launch traced here: 124 us
  starting transfers between devices  42.7 us (34%)
  Pallas kernels  41.7 us (33%)
  blocking collectives  36.3 us (29%)
  waiting for transfers between devices  2.64 us (2%)
    all_to_all x1, blocking collectives, exchange(): lax.all_to_all(partial_sums.reshape(16, 32, 1024), ('zl', 'y'), 0, 0, til...  36.3 us
    pallas_call x1, Pallas kernels, spread_rows(): pl.pallas_call(spread_kernel, in_specs=[IN_HBM], out_specs=IN_HBM, scratc...  33.2 us
    ppermute x7, starting transfers between devices, shift(): lax.ppermute(array, axis, [((i + by) % size, i) for i in range(size)])  29.5 us
    all_to_all x1, starting transfers between devices, body(): lax.all_to_all(rows, ('mp', 'x', 'c'), 0, 0, tiled=True)  13.2 us
    pallas_call x1, Pallas kernels, weight_shares(): pl.pallas_call(share_kernel, in_specs=[IN_VMEM, IN_HBM], out_specs=[IN_VM...  4.71 us
    ppermute x7, waiting for transfers between devices, shift(): lax.ppermute(array, axis, [((i + by) % size, i) for i in range(size)])  2.64 us
  transfers between devices with their start and end apart: 8, of which 1 were waited for; matrix products, arithmetic and copies ran while one was open for 0% of the time, Pallas kernels for 6%

profile of v5, /device:TPU:8, one launch (start us, length us, event | category | flops | bytes accessed | tf_op | source)
XLA Modules:
  0.0 124.3 jit_solution(6944747240730315581)
XLA Ops:
  0.6 33.2 %shard_map.68 = bf16[4,8,4,32,128]{4,3,2,1,0:T(8,128)(2,1)} custom-call(bf16[4,8,32,128]{3,2,1,0:T(8,128)(2,1)} %bitcast.13), custom_call_target="tpu_custom_call" | custom-call | tf_op jit(solution)/shard_map/pallas_call | solution.py:38
  33.8 13.2 %all-to-all-start.1 = ((bf16[32,128,128]{2,1,0:T(8,128)(2,1)}), bf16[32,128,128]{2,1,0:T(8,128)(2,1)S(1)}, u32[]{:S(2)}, u32[]{:S(2)}) async-start(bf16[32,128,128]{2,1,0:T(8,128)(2,1)} %bitcast.10), calls=%async_computation.1 | async-start | bytes 2097152 | tf_op jit(solution)/shard_map/all_to_all | solution.py:182
  47.0 1.5 %shard_map.69.gates_ref = bf16[128,1024]{1,0:T(8,128)(2,1)S(1)} custom-call(bf16[1024,128]{1,0:T(8,128)(2,1)} %gate_hbm.1, bf16[1024,128]{1,0:T(8,128)(2,1)} %up_hbm.1, bf16[1024,128]{1,0:T(8,128)(2,1)} %hidden_hbm.1), custom_call_target="tpu_custom_call" | custom-call | tf_op jit(solution)/shard_map/pallas_call | solution.py:68
  48.5 5.2 %collective-permute-start.3 = (bf16[128,1024]{1,0:T(8,128)(2,1)S(1)}, bf16[128,1024]{1,0:T(8,128)(2,1)S(1)}, u32[]{:S(2)}, u32[]{:S(2)}) collective-permute-start(bf16[128,1024]{1,0:T(8,128)(2,1)S(1)} %shard_map.69.gates_ref), channel_id=1, source_target_pairs={{16,0},{24,8},{0,16},{8,24},{17,1},{25,9},{1,17},{9,25},{18,2},{26... | collective-permute-start | bytes 786440 | tf_op jit(solution)/shard_map/ppermute | solution.py:18
  53.7 2.5 %collective-permute-start.2 = (bf16[128,1024]{1,0:T(8,128)(2,1)S(1)}, bf16[128,1024]{1,0:T(8,128)(2,1)S(1)}, u32[]{:S(2)}, u32[]{:S(2)}) collective-permute-start(bf16[128,1024]{1,0:T(8,128)(2,1)S(1)} %shard_map.69.gates_ref), channel_id=1, source_target_pairs={{24,0},{0,8},{8,16},{16,24},{25,1},{1,9},{9,17},{17,25},{26,2},{2,... | collective-permute-start | bytes 786440 | tf_op jit(solution)/shard_map/ppermute | solution.py:18
  56.2 4.6 %collective-permute-start.1 = (bf16[128,1024]{1,0:T(8,128)(2,1)S(1)}, bf16[128,1024]{1,0:T(8,128)(2,1)S(1)}, u32[]{:S(2)}, u32[]{:S(2)}) collective-permute-start(bf16[128,1024]{1,0:T(8,128)(2,1)S(1)} %shard_map.69.gates_ref), channel_id=1, source_target_pairs={{8,0},{16,8},{24,16},{0,24},{9,1},{17,9},{25,17},{1,25},{10,2},{18... | collective-permute-start | bytes 786440 | tf_op jit(solution)/shard_map/ppermute | solution.py:18
  60.8 4.7 %shard_map.70 = (f32[128,1024]{1,0:T(8,128)}, bf16[128,1024]{1,0:T(8,128)(2,1)}, bf16[128,1024]{1,0:T(8,128)(2,1)}, bf16[128,1024]{1,0:T(8,128)(2,1)}) custom-call(bf16[128,1024]{1,0:T(8,128)(2,1)S(1)} %shard_map.69.gates_ref, bf16[1024,4096]{1,0:T(8,128)(2,1)} %tokens_hbm.1), custom_call_target="tpu_custom_call" | custom-call | flops 1073741824 | bytes 10485760 | tf_op jit(solution)/shard_map/pallas_call | solution.py:96
  65.5 0.0 copy-start
  65.5 4.4 %collective-permute-start.4 = (bf16[128,1024]{1,0:T(8,128)(2,1)}, bf16[128,1024]{1,0:T(8,128)(2,1)S(1)}, u32[]{:S(2)}, u32[]{:S(2)}) collective-permute-start(bf16[128,1024]{1,0:T(8,128)(2,1)} %get-tuple-element.39), channel_id=1, source_target_pairs={{3,0},{0,1},{1,2},{2,3},{7,4},{4,5},{5,6},{6,7},{11,8},{8,9},{9,10... | collective-permute-start | bytes 786440 | tf_op jit(solution)/shard_map/ppermute | solution.py:18
  69.9 3.7 %collective-permute-start.5 = (bf16[128,1024]{1,0:T(8,128)(2,1)}, bf16[128,1024]{1,0:T(8,128)(2,1)S(1)}, u32[]{:S(2)}, u32[]{:S(2)}) collective-permute-start(bf16[128,1024]{1,0:T(8,128)(2,1)} %get-tuple-element.40), channel_id=1, source_target_pairs={{1,0},{2,1},{3,2},{0,3},{5,4},{6,5},{7,6},{4,7},{9,8},{10,9},{11,1... | collective-permute-start | bytes 786440 | tf_op jit(solution)/shard_map/ppermute | solution.py:18
  73.6 0.0 collective-permute-done.3
  73.6 7.3 %collective-permute-start.6 = (bf16[128,1024]{1,0:T(8,128)(2,1)}, bf16[128,1024]{1,0:T(8,128)(2,1)S(1)}, u32[]{:S(2)}, u32[]{:S(2)}) collective-permute-start(bf16[128,1024]{1,0:T(8,128)(2,1)} %get-tuple-element.41), channel_id=1, source_target_pairs={{2,0},{3,1},{0,2},{1,3},{6,4},{7,5},{4,6},{5,7},{10,8},{11,9},{8,1... | collective-permute-start | bytes 786440 | tf_op jit(solution)/shard_map/ppermute | solution.py:18
  80.9 0.0 collective-permute-done.2
  80.9 0.0 collective-permute-done.1
  80.9 0.0 all-to-all-done.1
  80.9 42.4 %conditional.1 = (bf16[32,1024]{1,0:T(8,128)(2,1)S(1)}) conditional(s32[]{:T(128)} %convert_element_type.3, () %tuple.16, (bf16[32,128,128]{2,1,0:T(8,128)(2,1)S(1)}, bf16[128,1024]{1,0:T(8,128)(2,1)S(1)}, bf16[128,1024]{1,0:T(8,128)(2,1)S(1)}, bf16[128,1024]{1,0:T(8,128)(2,1)S(1)}, bf16[128,1024]{1,0:T(8,128)(2,1)S(1)}) %tuple.18), branch_computations={%region_0.0_spmd, %region_1.0_spmd} | conditional | flops 1075314688 | bytes 12582960 | solution.py:175
  80.9 0.1 pad_maximum_fusion.mine_ref
  81.1 1.9 %collective-permute-start = (bf16[4,128,1024]{2,1,0:T(8,128)(2,1)S(1)}, bf16[4,128,1024]{2,1,0:T(8,128)(2,1)S(1)}, u32[]{:S(2)}, u32[]{:S(2)}) collective-permute-start(bf16[4,128,1024]{2,1,0:T(8,128)(2,1)S(1)} %pad_maximum_fusion.mine_ref), channel_id=1, source_target_pairs={{4,0},{0,4},{5,1},{1,5},{6,2},{2,6},{7,3},{3,7},{12,8},{8,12},{13,... | collective-permute-start | bytes 3145736 | tf_op jit(solution)/shard_map/cond/branch_1_fun/ppermute | solution.py:18
  83.0 2.6 %collective-permute-done.other_ref = bf16[4,128,1024]{2,1,0:T(8,128)(2,1)S(1)} collective-permute-done((bf16[4,128,1024]{2,1,0:T(8,128)(2,1)S(1)}, bf16[4,128,1024]{2,1,0:T(8,128)(2,1)S(1)}, u32[]{:S(2)}, u32[]{:S(2)}) %collective-permute-start) | collective-permute-done | bytes 1048608 | tf_op jit(solution)/shard_map/cond/branch_1_fun/ppermute | solution.py:18
  85.6 1.3 %branch_1_fun.2 = bf16[512,1024]{1,0:T(8,128)(2,1)S(1)} custom-call(bf16[4,8,128,128]{3,2,1,0:T(8,128)(2,1)S(1)} %bitcast.11, bf16[4,128,1024]{2,1,0:T(8,128)(2,1)S(1)} %pad_maximum_fusion.mine_ref, bf16[4,128,1024]{2,1,0:T(8,128)(2,1)S(1)} %collective-permute-done.other_ref), custom_call_target="tpu_custom_call" | custom-call | flops 1073741824 | bytes 4194304 | tf_op jit(solution)/shard_map/cond/branch_1_fun/pallas_call | solution.py:144
  86.9 36.3 %all_to_all.9.pieces_ref = bf16[16,32,1024]{2,1,0:T(8,128)(2,1)S(1)} all-to-all(bf16[16,32,1024]{2,1,0:T(8,128)(2,1)S(1)} %bitcast.9), channel_id=1, replica_groups=mesh['zl'=2,'y'=8,'x'=4,'c'=2,'mp'=4] {'zl','y'}, dimensions={0} | all-to-all | bytes 2097152 | tf_op jit(solution)/shard_map/cond/branch_1_fun/all_to_all | solution.py:193
  123.2 0.1 branch_1_fun.3
  123.4 0.0 copy-start.1
  123.4 0.0 collective-permute-done.4.right_ref
  123.4 0.0 collective-permute-done.5.left_ref
  123.4 0.0 collective-permute-done.6.far_ref
  123.4 0.0 copy-done
  123.4 0.9 shard_map.71
  124.3 0.0 copy-done.1
Async XLA Ops:
  33.8 47.1 %all-to-all-start.1 = ((bf16[32,128,128]{2,1,0:T(8,128)(2,1)}), bf16[32,128,128]{2,1,0:T(8,128)(2,1)S(1)}, u32[]{:S(2)}, u32[]{:S(2)}) async-start(bf16[32,128,128]{2,1,0:T(8,128)(2,1)} %bitcast.10), calls=%async_computation.1 | async-start | bytes 2097152 | tf_op jit(solution)/shard_map/all_to_all | solution.py:182
  48.5 25.1 %collective-permute-start.3 = (bf16[128,1024]{1,0:T(8,128)(2,1)S(1)}, bf16[128,1024]{1,0:T(8,128)(2,1)S(1)}, u32[]{:S(2)}, u32[]{:S(2)}) collective-permute-start(bf16[128,1024]{1,0:T(8,128)(2,1)S(1)} %shard_map.69.gates_ref), channel_id=1, source_target_pairs={{16,0},{24,8},{0,16},{8,24},{17,1},{25,9},{1,17},{9,25},{18,2},{26... | collective-permute-start | bytes 786440 | tf_op jit(solution)/shard_map/ppermute | solution.py:18
  53.7 27.2 %collective-permute-start.2 = (bf16[128,1024]{1,0:T(8,128)(2,1)S(1)}, bf16[128,1024]{1,0:T(8,128)(2,1)S(1)}, u32[]{:S(2)}, u32[]{:S(2)}) collective-permute-start(bf16[128,1024]{1,0:T(8,128)(2,1)S(1)} %shard_map.69.gates_ref), channel_id=1, source_target_pairs={{24,0},{0,8},{8,16},{16,24},{25,1},{1,9},{9,17},{17,25},{26,2},{2,... | collective-permute-start | bytes 786440 | tf_op jit(solution)/shard_map/ppermute | solution.py:18
  56.2 24.7 %collective-permute-start.1 = (bf16[128,1024]{1,0:T(8,128)(2,1)S(1)}, bf16[128,1024]{1,0:T(8,128)(2,1)S(1)}, u32[]{:S(2)}, u32[]{:S(2)}) collective-permute-start(bf16[128,1024]{1,0:T(8,128)(2,1)S(1)} %shard_map.69.gates_ref), channel_id=1, source_target_pairs={{8,0},{16,8},{24,16},{0,24},{9,1},{17,9},{25,17},{1,25},{10,2},{18... | collective-permute-start | bytes 786440 | tf_op jit(solution)/shard_map/ppermute | solution.py:18
  65.5 57.9 %copy-start = (f32[128,1024]{1,0:T(8,128)S(1)}, f32[128,1024]{1,0:T(8,128)}, u32[]{:S(2)}) copy-start(f32[128,1024]{1,0:T(8,128)} %get-tuple-element.43.own_ref) | copy-start | bytes 1572868
  65.5 57.9 %collective-permute-start.4 = (bf16[128,1024]{1,0:T(8,128)(2,1)}, bf16[128,1024]{1,0:T(8,128)(2,1)S(1)}, u32[]{:S(2)}, u32[]{:S(2)}) collective-permute-start(bf16[128,1024]{1,0:T(8,128)(2,1)} %get-tuple-element.39), channel_id=1, source_target_pairs={{3,0},{0,1},{1,2},{2,3},{7,4},{4,5},{5,6},{6,7},{11,8},{8,9},{9,10... | collective-permute-start | bytes 786440 | tf_op jit(solution)/shard_map/ppermute | solution.py:18
  69.9 53.5 %collective-permute-start.5 = (bf16[128,1024]{1,0:T(8,128)(2,1)}, bf16[128,1024]{1,0:T(8,128)(2,1)S(1)}, u32[]{:S(2)}, u32[]{:S(2)}) collective-permute-start(bf16[128,1024]{1,0:T(8,128)(2,1)} %get-tuple-element.40), channel_id=1, source_target_pairs={{1,0},{2,1},{3,2},{0,3},{5,4},{6,5},{7,6},{4,7},{9,8},{10,9},{11,1... | collective-permute-start | bytes 786440 | tf_op jit(solution)/shard_map/ppermute | solution.py:18
  73.6 49.8 %collective-permute-start.6 = (bf16[128,1024]{1,0:T(8,128)(2,1)}, bf16[128,1024]{1,0:T(8,128)(2,1)S(1)}, u32[]{:S(2)}, u32[]{:S(2)}) collective-permute-start(bf16[128,1024]{1,0:T(8,128)(2,1)} %get-tuple-element.41), channel_id=1, source_target_pairs={{2,0},{3,1},{0,2},{1,3},{6,4},{7,5},{4,6},{5,7},{10,8},{11,9},{8,1... | collective-permute-start | bytes 786440 | tf_op jit(solution)/shard_map/ppermute | solution.py:18
  81.1 4.6 %collective-permute-start = (bf16[4,128,1024]{2,1,0:T(8,128)(2,1)S(1)}, bf16[4,128,1024]{2,1,0:T(8,128)(2,1)S(1)}, u32[]{:S(2)}, u32[]{:S(2)}) collective-permute-start(bf16[4,128,1024]{2,1,0:T(8,128)(2,1)S(1)} %pad_maximum_fusion.mine_ref), channel_id=1, source_target_pairs={{4,0},{0,4},{5,1},{1,5},{6,2},{2,6},{7,3},{3,7},{12,8},{8,12},{13,... | collective-permute-start | bytes 3145736 | tf_op jit(solution)/shard_map/cond/branch_1_fun/ppermute | solution.py:18
  123.4 1.0 copy-start.1

commit v6 on v5

--- a/solution.py
+++ b/solution.py
@@ -8,6 +8,7 @@
 from jax.sharding import Mesh, PartitionSpec as P
 
 TURNS = (1, 3, 2)
+AHEAD = 3
 AXES = ("zl", "y", "x", "c", "mp")
 BF16, F32 = jnp.bfloat16, jnp.float32
 IN_HBM = pl.BlockSpec(memory_space=pltpu.HBM)
@@ -22,12 +23,14 @@
     return pltpu.CompilerParams(vmem_limit_bytes=limit << 20)
 
 
-def spread_kernel(weight_ref, out_ref, sems):
-    copies = [
-        pltpu.make_async_copy(weight_ref.at[:, k], out_ref.at[m, k], sems.at[m, k])
-        for m in range(4)
-        for k in range(8)
-    ]
+def spread_kernel(weight_hbm, out_hbm, weight, spread, sems):
+    copy = pltpu.make_async_copy(weight_hbm, weight, sems.at[4])
+    copy.start()
+    copy.wait()
+    for k in range(8):
+        for q in range(4):
+            spread[k, q * 32 : (q + 1) * 32, :] = weight[(q * 8 + k) * 32 : (q * 8 + k + 1) * 32, :]
+    copies = [pltpu.make_async_copy(spread, out_hbm.at[m], sems.at[m]) for m in range(4)]
     for copy in copies:
         copy.start()
     for copy in copies:
@@ -39,10 +42,14 @@
         spread_kernel,
         in_specs=[IN_HBM],
         out_specs=IN_HBM,
-        scratch_shapes=[pltpu.SemaphoreType.DMA((4, 8))],
-        out_shape=jax.ShapeDtypeStruct((4, 8, 4, 32, 128), BF16),
+        scratch_shapes=[
+            pltpu.VMEM((1024, 128), BF16),
+            pltpu.VMEM((8, 128, 128), BF16),
+            pltpu.SemaphoreType.DMA((5,)),
+        ],
+        out_shape=jax.ShapeDtypeStruct((4, 8, 128, 128), BF16),
         compiler_params=params(58),
-    )(weight.reshape(4, 8, 32, 128))
+    )(weight)
 
 
 def gate_kernel(gate_hbm, up_hbm, hidden_hbm, out_ref, *scratch):
@@ -75,33 +82,40 @@
     )(gate_pre, up_value, grad_hidden)
 
 
-def share_kernel(gates_ref, tokens_hbm, own_ref, right_ref, left_ref, far_ref, tokens, sems):
+def share_kernel(turns, gates_ref, tokens_hbm, *refs):
+    out_refs, tokens, sems = refs[: len(turns)], refs[-2], refs[-1]
     m = lax.axis_index("mp")
     copies = []
-    for step in range(8):
-        column = jnp.bitwise_and(m + (2, 1, 3, 0)[step // 2], 3) * 1024 + step % 2 * 512
-        copy = pltpu.make_async_copy(
-            tokens_hbm.at[:, pl.ds(pl.multiple_of(column, 512), 512)], tokens.at[step], sems.at[step]
+    for step in range(2 * len(turns)):
+        column = jnp.bitwise_and(m + turns[step // 2], 3) * 1024 + step % 2 * 512
+        copies.append(
+            pltpu.make_async_copy(
+                tokens_hbm.at[:, pl.ds(pl.multiple_of(column, 512), 512)], tokens.at[step], sems.at[step]
+            )
         )
+    for copy in copies[:AHEAD]:
         copy.start()
-        copies.append(copy)
     for step, copy in enumerate(copies):
         copy.wait()
-        out_ref = (far_ref, right_ref, left_ref, own_ref)[step // 2]
+        if step + AHEAD < len(copies):
+            copies[step + AHEAD].start()
+        out_ref = out_refs[step // 2]
         share = jnp.dot(gates_ref[...], tokens[step], preferred_element_type=F32)
         out_ref[:, step % 2 * 512 : (step % 2 + 1) * 512] = share.astype(out_ref.dtype)
 
 
-def weight_shares(gates, tokens):
-    return pl.pallas_call(
-        share_kernel,
+def weight_shares(turns, gates, tokens):
+    return pl.pallas_call(
+        functools.partial(share_kernel, turns),
         in_specs=[IN_VMEM, IN_HBM],
-        out_specs=[IN_VMEM] * 4,
-        scratch_shapes=[pltpu.VMEM((8, 1024, 512), BF16), pltpu.SemaphoreType.DMA((8,))],
-        out_shape=[jax.ShapeDtypeStruct((128, 1024), F32)]
-        + [jax.ShapeDtypeStruct((128, 1024), BF16)] * 3,
+        out_specs=[IN_VMEM] * len(turns),
+        scratch_shapes=[
+            pltpu.VMEM((2 * len(turns), 1024, 512), BF16),
+            pltpu.SemaphoreType.DMA((2 * len(turns),)),
+        ],
+        out_shape=[jax.ShapeDtypeStruct((128, 1024), BF16 if turn else F32) for turn in turns],
         compiler_params=params(54),
-        cost_estimate=pl.CostEstimate(flops=1 << 30, bytes_accessed=10 << 20, transcendentals=0),
+        cost_estimate=pl.CostEstimate(flops=1 << 29, bytes_accessed=5 << 20, transcendentals=0),
     )(gates, tokens)
 
 
@@ -183,19 +197,19 @@
 
     gates = gate_gradient(gate_pre, up_value, grad_hidden)
     mine = [shift(gates, "x", 4, k) for k in TURNS]
-    own, *shares = weight_shares(gates, tokens)
-    *mine, own = lax.optimization_barrier((*mine, own))
-    away = [shift(share, "mp", 4, -k) for k, share in zip(TURNS, shares)]
-
-    def exchange(rows, *mine):
-        mine = jnp.stack(mine)
+    right, left = weight_shares((1, 3), gates, tokens)
+    right, left = shift(right, "mp", 4, -1), shift(left, "mp", 4, 1)
+
+    def exchange(rows, tokens, *mine):
+        gates, mine = mine[0], jnp.stack(mine)
         partial_sums = partial_product(rows, mine, shift(mine, "c", 2, 1))
         pieces = lax.all_to_all(partial_sums.reshape(16, 32, 1024), ("zl", "y"), 0, 0, tiled=True)
-        return sum_pieces(pieces)
-
-    grad_tokens = always(exchange, rows, gates, *mine)
-    grad_tokens, own, *away = lax.optimization_barrier((grad_tokens, own, *away))
-    return (grad_tokens.T, add_shares(own, away, norm_factor))
+        far, own = weight_shares((2, 0), gates, tokens)
+        return sum_pieces(pieces), own, shift(far, "mp", 4, 2)
+
+    grad_tokens, own, far = always(exchange, rows, tokens, gates, *mine)
+    grad_tokens, own, right, left, far = lax.optimization_barrier((grad_tokens, own, right, left, far))
+    return (grad_tokens.T, add_shares(own, (right, left, far), norm_factor))
 
 
 def solution(mesh):

time: 125 us -> 99.2 us (0.79)
  the two profiles are of different devices: /device:TPU:8 before, /device:TPU:56 now
where the time goes in v6:
time: 99.2 us; the launch traced here: 98.6 us
  starting transfers between devices  52 us (52%)
  waiting for transfers between devices  30.9 us (31%)
  Pallas kernels  14.8 us (15%)
    ppermute x7, starting transfers between devices, shift(): lax.ppermute(array, axis, [((i + by) % size, i) for i in range(size)])  24.7 us
    all_to_all x1, waiting for transfers between devices, exchange(): lax.all_to_all(partial_sums.reshape(16, 32, 1024), ('zl', 'y'), 0, 0, til...  19 us
    all_to_all x1, starting transfers between devices, exchange(): lax.all_to_all(partial_sums.reshape(16, 32, 1024), ('zl', 'y'), 0, 0, til...  14.1 us
    all_to_all x1, starting transfers between devices, body(): lax.all_to_all(rows, ('mp', 'x', 'c'), 0, 0, tiled=True)  13.2 us
    ppermute x7, waiting for transfers between devices, shift(): lax.ppermute(array, axis, [((i + by) % size, i) for i in range(size)])  11.8 us
    pallas_call x2, Pallas kernels, weight_shares(): pl.pallas_call(functools.partial(share_kernel, turns), in_specs=[IN_VMEM,...  7.05 us
    pallas_call x1, Pallas kernels, partial_product(): pl.pallas_call(partial_kernel, in_specs=[IN_VMEM] * 3, out_specs=IN_VMEM,...  2.25 us
    pallas_call x1, Pallas kernels, spread_rows(): pl.pallas_call(spread_kernel, in_specs=[IN_HBM], out_specs=IN_HBM, scratc...  1.99 us
  transfers between devices with their start and end apart: 9, of which 4 were waited for; matrix products, arithmetic and copies ran while one was open for 0% of the time, Pallas kernels for 11%

profile of v6, /device:TPU:56, one launch (start us, length us, event | category | flops | bytes accessed | tf_op | source)
XLA Modules:
  0.0 98.6 jit_solution(3195291609326669500)
XLA Ops:
  0.6 2.0 %shard_map.68 = bf16[4,8,128,128]{3,2,1,0:T(8,128)(2,1)} custom-call(bf16[1024,128]{1,0:T(8,128)(2,1)} %weight_hbm.1), custom_call_target="tpu_custom_call" | custom-call | tf_op jit(solution)/shard_map/pallas_call | solution.py:41
  2.6 13.2 %all-to-all-start.1 = ((bf16[32,128,128]{2,1,0:T(8,128)(2,1)}), bf16[32,128,128]{2,1,0:T(8,128)(2,1)S(1)}, u32[]{:S(2)}, u32[]{:S(2)}) async-start(bf16[32,128,128]{2,1,0:T(8,128)(2,1)} %bitcast.8), calls=%async_computation.1 | async-start | bytes 2097152 | tf_op jit(solution)/shard_map/all_to_all | solution.py:196
  15.8 1.5 %shard_map.69.gates_ref = bf16[128,1024]{1,0:T(8,128)(2,1)S(1)} custom-call(bf16[1024,128]{1,0:T(8,128)(2,1)} %gate_hbm.1, bf16[1024,128]{1,0:T(8,128)(2,1)} %up_hbm.1, bf16[1024,128]{1,0:T(8,128)(2,1)} %hidden_hbm.1), custom_call_target="tpu_custom_call" | custom-call | tf_op jit(solution)/shard_map/pallas_call | solution.py:75
  17.3 4.9 %collective-permute-start.2 = (bf16[128,1024]{1,0:T(8,128)(2,1)S(1)}, bf16[128,1024]{1,0:T(8,128)(2,1)S(1)}, u32[]{:S(2)}, u32[]{:S(2)}) collective-permute-start(bf16[128,1024]{1,0:T(8,128)(2,1)S(1)} %shard_map.69.gates_ref), channel_id=1, source_target_pairs={{8,0},{16,8},{24,16},{0,24},{9,1},{17,9},{25,17},{1,25},{10,2},{18... | collective-permute-start | bytes 786440 | tf_op jit(solution)/shard_map/ppermute | solution.py:19
  22.3 1.9 %collective-permute-start.3 = (bf16[128,1024]{1,0:T(8,128)(2,1)S(1)}, bf16[128,1024]{1,0:T(8,128)(2,1)S(1)}, u32[]{:S(2)}, u32[]{:S(2)}) collective-permute-start(bf16[128,1024]{1,0:T(8,128)(2,1)S(1)} %shard_map.69.gates_ref), channel_id=1, source_target_pairs={{24,0},{0,8},{8,16},{16,24},{25,1},{1,9},{9,17},{17,25},{26,2},{2,... | collective-permute-start | bytes 786440 | tf_op jit(solution)/shard_map/ppermute | solution.py:19
  24.2 4.2 %collective-permute-start.4 = (bf16[128,1024]{1,0:T(8,128)(2,1)S(1)}, bf16[128,1024]{1,0:T(8,128)(2,1)S(1)}, u32[]{:S(2)}, u32[]{:S(2)}) collective-permute-start(bf16[128,1024]{1,0:T(8,128)(2,1)S(1)} %shard_map.69.gates_ref), channel_id=1, source_target_pairs={{16,0},{24,8},{0,16},{8,24},{17,1},{25,9},{1,17},{9,25},{18,2},{26... | collective-permute-start | bytes 786440 | tf_op jit(solution)/shard_map/ppermute | solution.py:19
  28.4 3.7 %shard_map.70 = (bf16[128,1024]{1,0:T(8,128)(2,1)}, bf16[128,1024]{1,0:T(8,128)(2,1)}) custom-call(bf16[128,1024]{1,0:T(8,128)(2,1)S(1)} %shard_map.69.gates_ref, bf16[1024,4096]{1,0:T(8,128)(2,1)} %tokens_hbm.1), custom_call_target="tpu_custom_call" | custom-call | flops 536870912 | bytes 5242880 | tf_op jit(solution)/shard_map/pallas_call | solution.py:108
  32.1 4.3 %collective-permute-start.5 = (bf16[128,1024]{1,0:T(8,128)(2,1)}, bf16[128,1024]{1,0:T(8,128)(2,1)S(1)}, u32[]{:S(2)}, u32[]{:S(2)}) collective-permute-start(bf16[128,1024]{1,0:T(8,128)(2,1)} %get-tuple-element.35), channel_id=1, source_target_pairs={{3,0},{0,1},{1,2},{2,3},{7,4},{4,5},{5,6},{6,7},{11,8},{8,9},{9,10... | collective-permute-start | bytes 786440 | tf_op jit(solution)/shard_map/ppermute | solution.py:19
  36.4 3.7 %collective-permute-start.6 = (bf16[128,1024]{1,0:T(8,128)(2,1)}, bf16[128,1024]{1,0:T(8,128)(2,1)S(1)}, u32[]{:S(2)}, u32[]{:S(2)}) collective-permute-start(bf16[128,1024]{1,0:T(8,128)(2,1)} %get-tuple-element.36), channel_id=1, source_target_pairs={{1,0},{2,1},{3,2},{0,3},{5,4},{6,5},{7,6},{4,7},{9,8},{10,9},{11,1... | collective-permute-start | bytes 786440 | tf_op jit(solution)/shard_map/ppermute | solution.py:19
  40.1 0.0 collective-permute-done.2
  40.1 4.9 %collective-permute-done.3 = bf16[128,1024]{1,0:T(8,128)(2,1)S(1)} collective-permute-done((bf16[128,1024]{1,0:T(8,128)(2,1)S(1)}, bf16[128,1024]{1,0:T(8,128)(2,1)S(1)}, u32[]{:S(2)}, u32[]{:S(2)}) %collective-permute-start.3) | collective-permute-done | bytes 262176 | tf_op jit(solution)/shard_map/ppermute | solution.py:19
  44.9 0.0 collective-permute-done.4
  45.0 0.0 all-to-all-done.1
  45.0 51.8 %conditional.1 = (bf16[32,1024]{1,0:T(8,128)(2,1)S(1)}, f32[128,1024]{1,0:T(8,128)S(1)}, bf16[128,1024]{1,0:T(8,128)(2,1)}) conditional(s32[]{:T(128)} %convert_element_type.3, () %tuple.17, (bf16[32,128,128]{2,1,0:T(8,128)(2,1)S(1)}, bf16[128,1024]{1,0:T(8,128)(2,1)S(1)}, bf16[128,1024]{1,0:T(8,128)(2,1)S(1)}, bf16[128,1024]{1,0:T(8,128)(2,1)S(1)}, ...), branch_computations={%region_0.0_spmd, %region_1.0_spmd} | conditional | flops 1612185600 | bytes 19923080 | solution.py:189
  45.0 0.1 pad_maximum_fusion.mine_ref
  45.1 1.9 %collective-permute-start = (bf16[4,128,1024]{2,1,0:T(8,128)(2,1)S(1)}, bf16[4,128,1024]{2,1,0:T(8,128)(2,1)S(1)}, u32[]{:S(2)}, u32[]{:S(2)}) collective-permute-start(bf16[4,128,1024]{2,1,0:T(8,128)(2,1)S(1)} %pad_maximum_fusion.mine_ref), channel_id=1, source_target_pairs={{4,0},{0,4},{5,1},{1,5},{6,2},{2,6},{7,3},{3,7},{12,8},{8,12},{13,... | collective-permute-start | bytes 3145736 | tf_op jit(solution)/shard_map/cond/branch_1_fun/ppermute | solution.py:19
  47.0 2.6 %collective-permute-done.other_ref = bf16[4,128,1024]{2,1,0:T(8,128)(2,1)S(1)} collective-permute-done((bf16[4,128,1024]{2,1,0:T(8,128)(2,1)S(1)}, bf16[4,128,1024]{2,1,0:T(8,128)(2,1)S(1)}, u32[]{:S(2)}, u32[]{:S(2)}) %collective-permute-start) | collective-permute-done | bytes 1048608 | tf_op jit(solution)/shard_map/cond/branch_1_fun/ppermute | solution.py:19
  49.6 2.2 %branch_1_fun.3 = bf16[512,1024]{1,0:T(8,128)(2,1)} custom-call(bf16[4,8,128,128]{3,2,1,0:T(8,128)(2,1)S(1)} %bitcast.9, bf16[4,128,1024]{2,1,0:T(8,128)(2,1)S(1)} %pad_maximum_fusion.mine_ref, bf16[4,128,1024]{2,1,0:T(8,128)(2,1)S(1)} %collective-permute-done.other_ref), custom_call_target="tpu_custom_call" | custom-call | flops 1073741824 | bytes 4194304 | tf_op jit(solution)/shard_map/cond/branch_1_fun/pallas_call | solution.py:158
  51.9 14.1 %all-to-all-start = ((bf16[16,32,1024]{2,1,0:T(8,128)(2,1)}), bf16[16,32,1024]{2,1,0:T(8,128)(2,1)S(1)}, u32[]{:S(2)}, u32[]{:S(2)}) async-start(bf16[16,32,1024]{2,1,0:T(8,128)(2,1)} %bitcast.5), calls=%async_computation | async-start | bytes 2097152 | tf_op jit(solution)/shard_map/cond/branch_1_fun/all_to_all | solution.py:206
  66.0 3.4 %branch_1_fun.5 = (bf16[128,1024]{1,0:T(8,128)(2,1)}, f32[128,1024]{1,0:T(8,128)S(1)}) custom-call(bf16[128,1024]{1,0:T(8,128)(2,1)S(1)} %get-tuple-element.14.gates_ref, bf16[1024,4096]{1,0:T(8,128)(2,1)} %get-tuple-element.18.tokens_hbm), custom_call_target="tpu_custom_call" | custom-call | flops 536870912 | bytes 5242880 | tf_op jit(solution)/shard_map/cond/branch_1_fun/pallas_call | solution.py:108
  69.4 3.8 %collective-permute-start.1 = (bf16[128,1024]{1,0:T(8,128)(2,1)}, bf16[128,1024]{1,0:T(8,128)(2,1)}, u32[]{:S(2)}, u32[]{:S(2)}) collective-permute-start(bf16[128,1024]{1,0:T(8,128)(2,1)} %get-tuple-element.20), channel_id=1, source_target_pairs={{2,0},{3,1},{0,2},{1,3},{6,4},{7,5},{4,6},{5,7},{10,8},{11,9},{8,1... | collective-permute-start | bytes 786440 | tf_op jit(solution)/shard_map/cond/branch_1_fun/ppermute | solution.py:19
  73.2 19.0 %all-to-all-done.pieces_ref = bf16[16,32,1024]{2,1,0:T(8,128)(2,1)S(1)} async-done(((bf16[16,32,1024]{2,1,0:T(8,128)(2,1)}), bf16[16,32,1024]{2,1,0:T(8,128)(2,1)S(1)}, u32[]{:S(2)}, u32[]{:S(2)}) %all-to-all-start) | async-done | bytes 1048608 | tf_op jit(solution)/shard_map/cond/branch_1_fun/all_to_all | solution.py:206
  92.3 0.1 branch_1_fun.4
  92.4 4.3 %collective-permute-done.1 = bf16[128,1024]{1,0:T(8,128)(2,1)} collective-permute-done((bf16[128,1024]{1,0:T(8,128)(2,1)}, bf16[128,1024]{1,0:T(8,128)(2,1)}, u32[]{:S(2)}, u32[]{:S(2)}) %collective-permute-start.1) | collective-permute-done | bytes 262176 | tf_op jit(solution)/shard_map/cond/branch_1_fun/ppermute | solution.py:19
  96.7 0.0 copy-start
  96.7 0.0 collective-permute-done.5.right_ref
  96.7 0.0 collective-permute-done.6.left_ref
  96.7 1.9 %shard_map.71 = bf16[1024,128]{1,0:T(8,128)(2,1)} custom-call(f32[128,1024]{1,0:T(8,128)S(1)} %get-tuple-element.39.own_ref, bf16[128,1024]{1,0:T(8,128)(2,1)S(1)} %collective-permute-done.5.right_ref, bf16[128,1024]{1,0:T(8,128)(2,1)S(1)} %collective-permute-done.6.left_ref, bf16[128,1024]{1,0:T(8,128)(2,1)} %get-tuple-element.42.far_ref), custom_call_target="tpu_custom_call" | custom-call | tf_op jit(solution)/shard_map/pallas_call | solution.py:130
  98.6 0.0 copy-done
Async XLA Ops:
  2.6 42.3 %all-to-all-start.1 = ((bf16[32,128,128]{2,1,0:T(8,128)(2,1)}), bf16[32,128,128]{2,1,0:T(8,128)(2,1)S(1)}, u32[]{:S(2)}, u32[]{:S(2)}) async-start(bf16[32,128,128]{2,1,0:T(8,128)(2,1)} %bitcast.8), calls=%async_computation.1 | async-start | bytes 2097152 | tf_op jit(solution)/shard_map/all_to_all | solution.py:196
  17.3 22.7 %collective-permute-start.2 = (bf16[128,1024]{1,0:T(8,128)(2,1)S(1)}, bf16[128,1024]{1,0:T(8,128)(2,1)S(1)}, u32[]{:S(2)}, u32[]{:S(2)}) collective-permute-start(bf16[128,1024]{1,0:T(8,128)(2,1)S(1)} %shard_map.69.gates_ref), channel_id=1, source_target_pairs={{8,0},{16,8},{24,16},{0,24},{9,1},{17,9},{25,17},{1,25},{10,2},{18... | collective-permute-start | bytes 786440 | tf_op jit(solution)/shard_map/ppermute | solution.py:19
  22.3 22.7 %collective-permute-start.3 = (bf16[128,1024]{1,0:T(8,128)(2,1)S(1)}, bf16[128,1024]{1,0:T(8,128)(2,1)S(1)}, u32[]{:S(2)}, u32[]{:S(2)}) collective-permute-start(bf16[128,1024]{1,0:T(8,128)(2,1)S(1)} %shard_map.69.gates_ref), channel_id=1, source_target_pairs={{24,0},{0,8},{8,16},{16,24},{25,1},{1,9},{9,17},{17,25},{26,2},{2,... | collective-permute-start | bytes 786440 | tf_op jit(solution)/shard_map/ppermute | solution.py:19
  24.2 20.8 %collective-permute-start.4 = (bf16[128,1024]{1,0:T(8,128)(2,1)S(1)}, bf16[128,1024]{1,0:T(8,128)(2,1)S(1)}, u32[]{:S(2)}, u32[]{:S(2)}) collective-permute-start(bf16[128,1024]{1,0:T(8,128)(2,1)S(1)} %shard_map.69.gates_ref), channel_id=1, source_target_pairs={{16,0},{24,8},{0,16},{8,24},{17,1},{25,9},{1,17},{9,25},{18,2},{26... | collective-permute-start | bytes 786440 | tf_op jit(solution)/shard_map/ppermute | solution.py:19
  32.1 64.6 %collective-permute-start.5 = (bf16[128,1024]{1,0:T(8,128)(2,1)}, bf16[128,1024]{1,0:T(8,128)(2,1)S(1)}, u32[]{:S(2)}, u32[]{:S(2)}) collective-permute-start(bf16[128,1024]{1,0:T(8,128)(2,1)} %get-tuple-element.35), channel_id=1, source_target_pairs={{3,0},{0,1},{1,2},{2,3},{7,4},{4,5},{5,6},{6,7},{11,8},{8,9},{9,10... | collective-permute-start | bytes 786440 | tf_op jit(solution)/shard_map/ppermute | solution.py:19
  36.4 60.4 %collective-permute-start.6 = (bf16[128,1024]{1,0:T(8,128)(2,1)}, bf16[128,1024]{1,0:T(8,128)(2,1)S(1)}, u32[]{:S(2)}, u32[]{:S(2)}) collective-permute-start(bf16[128,1024]{1,0:T(8,128)(2,1)} %get-tuple-element.36), channel_id=1, source_target_pairs={{1,0},{2,1},{3,2},{0,3},{5,4},{6,5},{7,6},{4,7},{9,8},{10,9},{11,1... | collective-permute-start | bytes 786440 | tf_op jit(solution)/shard_map/ppermute | solution.py:19
  45.1 4.6 %collective-permute-start = (bf16[4,128,1024]{2,1,0:T(8,128)(2,1)S(1)}, bf16[4,128,1024]{2,1,0:T(8,128)(2,1)S(1)}, u32[]{:S(2)}, u32[]{:S(2)}) collective-permute-start(bf16[4,128,1024]{2,1,0:T(8,128)(2,1)S(1)} %pad_maximum_fusion.mine_ref), channel_id=1, source_target_pairs={{4,0},{0,4},{5,1},{1,5},{6,2},{2,6},{7,3},{3,7},{12,8},{8,12},{13,... | collective-permute-start | bytes 3145736 | tf_op jit(solution)/shard_map/cond/branch_1_fun/ppermute | solution.py:19
  51.9 40.4 %all-to-all-start = ((bf16[16,32,1024]{2,1,0:T(8,128)(2,1)}), bf16[16,32,1024]{2,1,0:T(8,128)(2,1)S(1)}, u32[]{:S(2)}, u32[]{:S(2)}) async-start(bf16[16,32,1024]{2,1,0:T(8,128)(2,1)} %bitcast.5), calls=%async_computation | async-start | bytes 2097152 | tf_op jit(solution)/shard_map/cond/branch_1_fun/all_to_all | solution.py:206
  69.4 27.3 %collective-permute-start.1 = (bf16[128,1024]{1,0:T(8,128)(2,1)}, bf16[128,1024]{1,0:T(8,128)(2,1)}, u32[]{:S(2)}, u32[]{:S(2)}) collective-permute-start(bf16[128,1024]{1,0:T(8,128)(2,1)} %get-tuple-element.20), channel_id=1, source_target_pairs={{2,0},{3,1},{0,2},{1,3},{6,4},{7,5},{4,6},{5,7},{10,8},{11,9},{8,1... | collective-permute-start | bytes 786440 | tf_op jit(solution)/shard_map/cond/branch_1_fun/ppermute | solution.py:19
  96.7 1.9 %copy-start = (bf16[32,1024]{1,0:T(8,128)(2,1)}, bf16[32,1024]{1,0:T(8,128)(2,1)S(1)}, u32[]{:S(2)}) copy-start(bf16[32,1024]{1,0:T(8,128)(2,1)S(1)} %get-tuple-element.38) | copy-start | bytes 196612

commit v7 on v5

--- a/solution.py
+++ b/solution.py
@@ -22,12 +22,14 @@
     return pltpu.CompilerParams(vmem_limit_bytes=limit << 20)
 
 
-def spread_kernel(weight_ref, out_ref, sems):
-    copies = [
-        pltpu.make_async_copy(weight_ref.at[:, k], out_ref.at[m, k], sems.at[m, k])
-        for m in range(4)
-        for k in range(8)
-    ]
+def spread_kernel(weight_hbm, out_hbm, weight, spread, sems):
+    copy = pltpu.make_async_copy(weight_hbm, weight, sems.at[4])
+    copy.start()
+    copy.wait()
+    for k in range(8):
+        for q in range(4):
+            spread[k, q * 32 : (q + 1) * 32, :] = weight[(q * 8 + k) * 32 : (q * 8 + k + 1) * 32, :]
+    copies = [pltpu.make_async_copy(spread, out_hbm.at[m], sems.at[m]) for m in range(4)]
     for copy in copies:
         copy.start()
     for copy in copies:
@@ -39,10 +41,14 @@
         spread_kernel,
         in_specs=[IN_HBM],
         out_specs=IN_HBM,
-        scratch_shapes=[pltpu.SemaphoreType.DMA((4, 8))],
-        out_shape=jax.ShapeDtypeStruct((4, 8, 4, 32, 128), BF16),
+        scratch_shapes=[
+            pltpu.VMEM((1024, 128), BF16),
+            pltpu.VMEM((8, 128, 128), BF16),
+            pltpu.SemaphoreType.DMA((5,)),
+        ],
+        out_shape=jax.ShapeDtypeStruct((4, 8, 128, 128), BF16),
         compiler_params=params(58),
-    )(weight.reshape(4, 8, 32, 128))
+    )(weight)
 
 
 def gate_kernel(gate_hbm, up_hbm, hidden_hbm, out_ref, *scratch):

time: 125 us -> 93.7 us (0.75)
  Pallas kernels: 41.7 us -> 10.5 us
    pallas_call x1, Pallas kernels: 33.2 us -> 1.98 us  [spread_rows(): pl.pallas_call(spread_kernel, in_specs=[IN_HBM], out_specs=IN_HBM, scratc...]
  transfers between devices with their start and end apart: 8 -> 8, of which waited for: 1 -> 1; matrix products, arithmetic and copies ran while one was open for 0% -> 0% of each run, Pallas kernels for 6% -> 8%
where the time goes in v7:
time: 93.7 us; the launch traced here: 93.2 us
  starting transfers between devices  42.7 us (46%)
  blocking collectives  36.3 us (39%)
  Pallas kernels  10.5 us (11%)
  waiting for transfers between devices  2.64 us (3%)
    all_to_all x1, blocking collectives, exchange(): lax.all_to_all(partial_sums.reshape(16, 32, 1024), ('zl', 'y'), 0, 0, til...  36.3 us
    ppermute x7, starting transfers between devices, shift(): lax.ppermute(array, axis, [((i + by) % size, i) for i in range(size)])  29.6 us
    all_to_all x1, starting transfers between devices, body(): lax.all_to_all(rows, ('mp', 'x', 'c'), 0, 0, tiled=True)  13.2 us
    pallas_call x1, Pallas kernels, weight_shares(): pl.pallas_call(share_kernel, in_specs=[IN_VMEM, IN_HBM], out_specs=[IN_VM...  4.71 us
    ppermute x7, waiting for transfers between devices, shift(): lax.ppermute(array, axis, [((i + by) % size, i) for i in range(size)])  2.64 us
    pallas_call x1, Pallas kernels, spread_rows(): pl.pallas_call(spread_kernel, in_specs=[IN_HBM], out_specs=IN_HBM, scratc...  1.98 us
  transfers between devices with their start and end apart: 8, of which 1 were waited for; matrix products, arithmetic and copies ran while one was open for 0% of the time, Pallas kernels for 8%

profile of v7, /device:TPU:8, one launch (start us, length us, event | category | flops | bytes accessed | tf_op | source)
XLA Modules:
  0.0 93.2 jit_solution(5489476774602794726)
XLA Ops:
  0.6 2.0 %shard_map.68 = bf16[4,8,128,128]{3,2,1,0:T(8,128)(2,1)} custom-call(bf16[1024,128]{1,0:T(8,128)(2,1)} %weight_hbm.1), custom_call_target="tpu_custom_call" | custom-call | tf_op jit(solution)/shard_map/pallas_call | solution.py:40
  2.6 13.2 %all-to-all-start.1 = ((bf16[32,128,128]{2,1,0:T(8,128)(2,1)}), bf16[32,128,128]{2,1,0:T(8,128)(2,1)S(1)}, u32[]{:S(2)}, u32[]{:S(2)}) async-start(bf16[32,128,128]{2,1,0:T(8,128)(2,1)} %bitcast.9), calls=%async_computation.1 | async-start | bytes 2097152 | tf_op jit(solution)/shard_map/all_to_all | solution.py:188
  15.8 1.5 %shard_map.69.gates_ref = bf16[128,1024]{1,0:T(8,128)(2,1)S(1)} custom-call(bf16[1024,128]{1,0:T(8,128)(2,1)} %gate_hbm.1, bf16[1024,128]{1,0:T(8,128)(2,1)} %up_hbm.1, bf16[1024,128]{1,0:T(8,128)(2,1)} %hidden_hbm.1), custom_call_target="tpu_custom_call" | custom-call | tf_op jit(solution)/shard_map/pallas_call | solution.py:74
  17.3 5.2 %collective-permute-start.3 = (bf16[128,1024]{1,0:T(8,128)(2,1)S(1)}, bf16[128,1024]{1,0:T(8,128)(2,1)S(1)}, u32[]{:S(2)}, u32[]{:S(2)}) collective-permute-start(bf16[128,1024]{1,0:T(8,128)(2,1)S(1)} %shard_map.69.gates_ref), channel_id=1, source_target_pairs={{16,0},{24,8},{0,16},{8,24},{17,1},{25,9},{1,17},{9,25},{18,2},{26... | collective-permute-start | bytes 786440 | tf_op jit(solution)/shard_map/ppermute | solution.py:18
  22.5 2.5 %collective-permute-start.2 = (bf16[128,1024]{1,0:T(8,128)(2,1)S(1)}, bf16[128,1024]{1,0:T(8,128)(2,1)S(1)}, u32[]{:S(2)}, u32[]{:S(2)}) collective-permute-start(bf16[128,1024]{1,0:T(8,128)(2,1)S(1)} %shard_map.69.gates_ref), channel_id=1, source_target_pairs={{24,0},{0,8},{8,16},{16,24},{25,1},{1,9},{9,17},{17,25},{26,2},{2,... | collective-permute-start | bytes 786440 | tf_op jit(solution)/shard_map/ppermute | solution.py:18
  25.0 4.6 %collective-permute-start.1 = (bf16[128,1024]{1,0:T(8,128)(2,1)S(1)}, bf16[128,1024]{1,0:T(8,128)(2,1)S(1)}, u32[]{:S(2)}, u32[]{:S(2)}) collective-permute-start(bf16[128,1024]{1,0:T(8,128)(2,1)S(1)} %shard_map.69.gates_ref), channel_id=1, source_target_pairs={{8,0},{16,8},{24,16},{0,24},{9,1},{17,9},{25,17},{1,25},{10,2},{18... | collective-permute-start | bytes 786440 | tf_op jit(solution)/shard_map/ppermute | solution.py:18
  29.6 4.7 %shard_map.70 = (f32[128,1024]{1,0:T(8,128)}, bf16[128,1024]{1,0:T(8,128)(2,1)}, bf16[128,1024]{1,0:T(8,128)(2,1)}, bf16[128,1024]{1,0:T(8,128)(2,1)}) custom-call(bf16[128,1024]{1,0:T(8,128)(2,1)S(1)} %shard_map.69.gates_ref, bf16[1024,4096]{1,0:T(8,128)(2,1)} %tokens_hbm.1), custom_call_target="tpu_custom_call" | custom-call | flops 1073741824 | bytes 10485760 | tf_op jit(solution)/shard_map/pallas_call | solution.py:102
  34.3 0.0 copy-start
  34.3 4.4 %collective-permute-start.4 = (bf16[128,1024]{1,0:T(8,128)(2,1)}, bf16[128,1024]{1,0:T(8,128)(2,1)S(1)}, u32[]{:S(2)}, u32[]{:S(2)}) collective-permute-start(bf16[128,1024]{1,0:T(8,128)(2,1)} %get-tuple-element.39), channel_id=1, source_target_pairs={{3,0},{0,1},{1,2},{2,3},{7,4},{4,5},{5,6},{6,7},{11,8},{8,9},{9,10... | collective-permute-start | bytes 786440 | tf_op jit(solution)/shard_map/ppermute | solution.py:18
  38.7 3.7 %collective-permute-start.5 = (bf16[128,1024]{1,0:T(8,128)(2,1)}, bf16[128,1024]{1,0:T(8,128)(2,1)S(1)}, u32[]{:S(2)}, u32[]{:S(2)}) collective-permute-start(bf16[128,1024]{1,0:T(8,128)(2,1)} %get-tuple-element.40), channel_id=1, source_target_pairs={{1,0},{2,1},{3,2},{0,3},{5,4},{6,5},{7,6},{4,7},{9,8},{10,9},{11,1... | collective-permute-start | bytes 786440 | tf_op jit(solution)/shard_map/ppermute | solution.py:18
  42.4 0.0 collective-permute-done.3
  42.4 7.3 %collective-permute-start.6 = (bf16[128,1024]{1,0:T(8,128)(2,1)}, bf16[128,1024]{1,0:T(8,128)(2,1)S(1)}, u32[]{:S(2)}, u32[]{:S(2)}) collective-permute-start(bf16[128,1024]{1,0:T(8,128)(2,1)} %get-tuple-element.41), channel_id=1, source_target_pairs={{2,0},{3,1},{0,2},{1,3},{6,4},{7,5},{4,6},{5,7},{10,8},{11,9},{8,1... | collective-permute-start | bytes 786440 | tf_op jit(solution)/shard_map/ppermute | solution.py:18
  49.7 0.0 collective-permute-done.2
  49.8 0.0 collective-permute-done.1
  49.8 0.0 all-to-all-done.1
  49.8 42.5 %conditional.1 = (bf16[32,1024]{1,0:T(8,128)(2,1)S(1)}) conditional(s32[]{:T(128)} %convert_element_type.3, () %tuple.16, (bf16[32,128,128]{2,1,0:T(8,128)(2,1)S(1)}, bf16[128,1024]{1,0:T(8,128)(2,1)S(1)}, bf16[128,1024]{1,0:T(8,128)(2,1)S(1)}, bf16[128,1024]{1,0:T(8,128)(2,1)S(1)}, bf16[128,1024]{1,0:T(8,128)(2,1)S(1)}) %tuple.18), branch_computations={%region_0.0_spmd, %region_1.0_spmd} | conditional | flops 1075314688 | bytes 12582960 | solution.py:181
  49.8 0.1 pad_maximum_fusion.mine_ref
  49.9 1.9 %collective-permute-start = (bf16[4,128,1024]{2,1,0:T(8,128)(2,1)S(1)}, bf16[4,128,1024]{2,1,0:T(8,128)(2,1)S(1)}, u32[]{:S(2)}, u32[]{:S(2)}) collective-permute-start(bf16[4,128,1024]{2,1,0:T(8,128)(2,1)S(1)} %pad_maximum_fusion.mine_ref), channel_id=1, source_target_pairs={{4,0},{0,4},{5,1},{1,5},{6,2},{2,6},{7,3},{3,7},{12,8},{8,12},{13,... | collective-permute-start | bytes 3145736 | tf_op jit(solution)/shard_map/cond/branch_1_fun/ppermute | solution.py:18
  51.8 2.6 %collective-permute-done.other_ref = bf16[4,128,1024]{2,1,0:T(8,128)(2,1)S(1)} collective-permute-done((bf16[4,128,1024]{2,1,0:T(8,128)(2,1)S(1)}, bf16[4,128,1024]{2,1,0:T(8,128)(2,1)S(1)}, u32[]{:S(2)}, u32[]{:S(2)}) %collective-permute-start) | collective-permute-done | bytes 1048608 | tf_op jit(solution)/shard_map/cond/branch_1_fun/ppermute | solution.py:18
  54.5 1.3 %branch_1_fun.2 = bf16[512,1024]{1,0:T(8,128)(2,1)S(1)} custom-call(bf16[4,8,128,128]{3,2,1,0:T(8,128)(2,1)S(1)} %bitcast.10, bf16[4,128,1024]{2,1,0:T(8,128)(2,1)S(1)} %pad_maximum_fusion.mine_ref, bf16[4,128,1024]{2,1,0:T(8,128)(2,1)S(1)} %collective-permute-done.other_ref), custom_call_target="tpu_custom_call" | custom-call | flops 1073741824 | bytes 4194304 | tf_op jit(solution)/shard_map/cond/branch_1_fun/pallas_call | solution.py:150
  55.7 36.3 %all_to_all.9.pieces_ref = bf16[16,32,1024]{2,1,0:T(8,128)(2,1)S(1)} all-to-all(bf16[16,32,1024]{2,1,0:T(8,128)(2,1)S(1)} %bitcast.8), channel_id=1, replica_groups=mesh['zl'=2,'y'=8,'x'=4,'c'=2,'mp'=4] {'zl','y'}, dimensions={0} | all-to-all | bytes 2097152 | tf_op jit(solution)/shard_map/cond/branch_1_fun/all_to_all | solution.py:199
  92.1 0.1 branch_1_fun.3
  92.2 0.0 copy-start.1
  92.2 0.0 collective-permute-done.4.right_ref
  92.2 0.0 collective-permute-done.5.left_ref
  92.3 0.0 collective-permute-done.6.far_ref
  92.3 0.0 copy-done
  92.3 0.9 shard_map.71
  93.2 0.0 copy-done.1
Async XLA Ops:
  2.6 47.1 %all-to-all-start.1 = ((bf16[32,128,128]{2,1,0:T(8,128)(2,1)}), bf16[32,128,128]{2,1,0:T(8,128)(2,1)S(1)}, u32[]{:S(2)}, u32[]{:S(2)}) async-start(bf16[32,128,128]{2,1,0:T(8,128)(2,1)} %bitcast.9), calls=%async_computation.1 | async-start | bytes 2097152 | tf_op jit(solution)/shard_map/all_to_all | solution.py:188
  17.3 25.1 %collective-permute-start.3 = (bf16[128,1024]{1,0:T(8,128)(2,1)S(1)}, bf16[128,1024]{1,0:T(8,128)(2,1)S(1)}, u32[]{:S(2)}, u32[]{:S(2)}) collective-permute-start(bf16[128,1024]{1,0:T(8,128)(2,1)S(1)} %shard_map.69.gates_ref), channel_id=1, source_target_pairs={{16,0},{24,8},{0,16},{8,24},{17,1},{25,9},{1,17},{9,25},{18,2},{26... | collective-permute-start | bytes 786440 | tf_op jit(solution)/shard_map/ppermute | solution.py:18
  22.5 27.2 %collective-permute-start.2 = (bf16[128,1024]{1,0:T(8,128)(2,1)S(1)}, bf16[128,1024]{1,0:T(8,128)(2,1)S(1)}, u32[]{:S(2)}, u32[]{:S(2)}) collective-permute-start(bf16[128,1024]{1,0:T(8,128)(2,1)S(1)} %shard_map.69.gates_ref), channel_id=1, source_target_pairs={{24,0},{0,8},{8,16},{16,24},{25,1},{1,9},{9,17},{17,25},{26,2},{2,... | collective-permute-start | bytes 786440 | tf_op jit(solution)/shard_map/ppermute | solution.py:18
  25.0 24.7 %collective-permute-start.1 = (bf16[128,1024]{1,0:T(8,128)(2,1)S(1)}, bf16[128,1024]{1,0:T(8,128)(2,1)S(1)}, u32[]{:S(2)}, u32[]{:S(2)}) collective-permute-start(bf16[128,1024]{1,0:T(8,128)(2,1)S(1)} %shard_map.69.gates_ref), channel_id=1, source_target_pairs={{8,0},{16,8},{24,16},{0,24},{9,1},{17,9},{25,17},{1,25},{10,2},{18... | collective-permute-start | bytes 786440 | tf_op jit(solution)/shard_map/ppermute | solution.py:18
  34.3 58.0 %copy-start = (f32[128,1024]{1,0:T(8,128)S(1)}, f32[128,1024]{1,0:T(8,128)}, u32[]{:S(2)}) copy-start(f32[128,1024]{1,0:T(8,128)} %get-tuple-element.43.own_ref) | copy-start | bytes 1572868
  34.3 57.9 %collective-permute-start.4 = (bf16[128,1024]{1,0:T(8,128)(2,1)}, bf16[128,1024]{1,0:T(8,128)(2,1)S(1)}, u32[]{:S(2)}, u32[]{:S(2)}) collective-permute-start(bf16[128,1024]{1,0:T(8,128)(2,1)} %get-tuple-element.39), channel_id=1, source_target_pairs={{3,0},{0,1},{1,2},{2,3},{7,4},{4,5},{5,6},{6,7},{11,8},{8,9},{9,10... | collective-permute-start | bytes 786440 | tf_op jit(solution)/shard_map/ppermute | solution.py:18
  38.7 53.5 %collective-permute-start.5 = (bf16[128,1024]{1,0:T(8,128)(2,1)}, bf16[128,1024]{1,0:T(8,128)(2,1)S(1)}, u32[]{:S(2)}, u32[]{:S(2)}) collective-permute-start(bf16[128,1024]{1,0:T(8,128)(2,1)} %get-tuple-element.40), channel_id=1, source_target_pairs={{1,0},{2,1},{3,2},{0,3},{5,4},{6,5},{7,6},{4,7},{9,8},{10,9},{11,1... | collective-permute-start | bytes 786440 | tf_op jit(solution)/shard_map/ppermute | solution.py:18
  42.4 49.8 %collective-permute-start.6 = (bf16[128,1024]{1,0:T(8,128)(2,1)}, bf16[128,1024]{1,0:T(8,128)(2,1)S(1)}, u32[]{:S(2)}, u32[]{:S(2)}) collective-permute-start(bf16[128,1024]{1,0:T(8,128)(2,1)} %get-tuple-element.41), channel_id=1, source_target_pairs={{2,0},{3,1},{0,2},{1,3},{6,4},{7,5},{4,6},{5,7},{10,8},{11,9},{8,1... | collective-permute-start | bytes 786440 | tf_op jit(solution)/shard_map/ppermute | solution.py:18
  49.9 4.6 %collective-permute-start = (bf16[4,128,1024]{2,1,0:T(8,128)(2,1)S(1)}, bf16[4,128,1024]{2,1,0:T(8,128)(2,1)S(1)}, u32[]{:S(2)}, u32[]{:S(2)}) collective-permute-start(bf16[4,128,1024]{2,1,0:T(8,128)(2,1)S(1)} %pad_maximum_fusion.mine_ref), channel_id=1, source_target_pairs={{4,0},{0,4},{5,1},{1,5},{6,2},{2,6},{7,3},{3,7},{12,8},{8,12},{13,... | collective-permute-start | bytes 3145736 | tf_op jit(solution)/shard_map/cond/branch_1_fun/ppermute | solution.py:18
  92.2 1.0 %copy-start.1 = (bf16[32,1024]{1,0:T(8,128)(2,1)}, bf16[32,1024]{1,0:T(8,128)(2,1)S(1)}, u32[]{:S(2)}) copy-start(bf16[32,1024]{1,0:T(8,128)(2,1)S(1)} %get-tuple-element.47) | copy-start | bytes 196612

commit v8 on v7

--- a/solution.py
+++ b/solution.py
@@ -131,8 +131,7 @@
 def partial_kernel(rows_ref, mine_ref, other_ref, out_ref, rows):
     x, c = lax.axis_index("x"), lax.axis_index("c")
     for k in range(8):
-        turn = ((0,) + TURNS)[k % 4]
-        source = jnp.bitwise_and(x + turn, 3) * 2 + (c if k < 4 else 1 - c)
+        source = jnp.bitwise_xor(x, k % 4) * 2 + (c if k < 4 else 1 - c)
         for m in range(4):
             rows[m * 128 : (m + 1) * 128, k * 128 : (k + 1) * 128] = rows_ref[m, source]
     for t in range(2):
@@ -188,18 +187,20 @@
     rows = lax.all_to_all(rows, ("mp", "x", "c"), 0, 0, tiled=True).reshape(4, 8, 128, 128)
 
     gates = gate_gradient(gate_pre, up_value, grad_hidden)
-    mine = [shift(gates, "x", 4, k) for k in TURNS]
+    near = lax.ppermute(gates, "x", [(i, i ^ 1) for i in range(4)])
     own, *shares = weight_shares(gates, tokens)
-    *mine, own = lax.optimization_barrier((*mine, own))
+    near, own = lax.optimization_barrier((near, own))
+    pair = jnp.stack([gates, near])
+    other_pair = lax.ppermute(pair, "x", [(i, i ^ 2) for i in range(4)])
     away = [shift(share, "mp", 4, -k) for k, share in zip(TURNS, shares)]
 
-    def exchange(rows, *mine):
-        mine = jnp.stack(mine)
+    def exchange(rows, *pairs):
+        mine = jnp.concatenate(pairs)
         partial_sums = partial_product(rows, mine, shift(mine, "c", 2, 1))
         pieces = lax.all_to_all(partial_sums.reshape(16, 32, 1024), ("zl", "y"), 0, 0, tiled=True)
         return sum_pieces(pieces)
 
-    grad_tokens = always(exchange, rows, gates, *mine)
+    grad_tokens = always(exchange, rows, pair, other_pair)
     grad_tokens, own, *away = lax.optimization_barrier((grad_tokens, own, *away))
     return (grad_tokens.T, add_shares(own, away, norm_factor))
 

time: 93.7 us -> 97.1 us (1.036)
  waiting for transfers between devices: 2.64 us -> 10.1 us
  starting transfers between devices: 42.7 us -> 39.2 us
  blocking collectives: 36.3 us -> 34.2 us
  Pallas kernels: 10.5 us -> 12.2 us
    ppermute x7 -> x4, starting transfers between devices: 29.6 us -> 17 us  [shift(): lax.ppermute(array, axis, [((i + by) % size, i) for i in range(size)])]
    ppermute x0 -> x2, starting transfers between devices: none -> 9.02 us  [the longest x1 5.19 us: body(): other_pair = lax.ppermute(pair, 'x', [(i, i ^ 2) for i in range(4)])]
    ppermute x0 -> x2, waiting for transfers between devices: none -> 7.44 us  [the longest x1 7.43 us: body(): near = lax.ppermute(gates, 'x', [(i, i ^ 1) for i in range(4)])]
    all_to_all x1, blocking collectives: 36.3 us -> 34.2 us  [exchange(): lax.all_to_all(partial_sums.reshape(16, 32, 1024), ('zl', 'y'), 0, 0, til...]
    ppermute x7 -> x4, waiting for transfers between devices: 2.64 us -> 2.63 us  [shift(): lax.ppermute(array, axis, [((i + by) % size, i) for i in range(size)])]
  transfers between devices with their start and end apart: 8 -> 7, of which waited for: 1 -> 2; matrix products, arithmetic and copies ran while one was open for 0% -> 0% of each run, Pallas kernels for 8% -> 10%
where the time goes in v8:
time: 97.1 us; the launch traced here: 96.6 us
  starting transfers between devices  39.2 us (40%)
  blocking collectives  34.2 us (35%)
  Pallas kernels  12.2 us (13%)
  waiting for transfers between devices  10.1 us (10%)
    all_to_all x1, blocking collectives, exchange(): lax.all_to_all(partial_sums.reshape(16, 32, 1024), ('zl', 'y'), 0, 0, til...  34.2 us
    ppermute x4, starting transfers between devices, shift(): lax.ppermute(array, axis, [((i + by) % size, i) for i in range(size)])  17 us
    all_to_all x1, starting transfers between devices, body(): lax.all_to_all(rows, ('mp', 'x', 'c'), 0, 0, tiled=True)  13.2 us
    ppermute x1, waiting for transfers between devices, body(): near = lax.ppermute(gates, 'x', [(i, i ^ 1) for i in range(4)])  7.43 us
    pallas_call x1, Pallas kernels, weight_shares(): pl.pallas_call(share_kernel, in_specs=[IN_VMEM, IN_HBM], out_specs=[IN_VM...  5.65 us
    ppermute x1, starting transfers between devices, body(): other_pair = lax.ppermute(pair, 'x', [(i, i ^ 2) for i in range(4)])  5.19 us
    ppermute x1, starting transfers between devices, body(): near = lax.ppermute(gates, 'x', [(i, i ^ 1) for i in range(4)])  3.83 us
    ppermute x4, waiting for transfers between devices, shift(): lax.ppermute(array, axis, [((i + by) % size, i) for i in range(size)])  2.63 us
  transfers between devices with their start and end apart: 7, of which 2 were waited for; matrix products, arithmetic and copies ran while one was open for 0% of the time, Pallas kernels for 10%

profile of v8, /device:TPU:8, one launch (start us, length us, event | category | flops | bytes accessed | tf_op | source)
XLA Modules:
  0.0 96.6 jit_solution(17710431139065511981)
XLA Ops:
  0.6 2.0 %shard_map.68 = bf16[4,8,128,128]{3,2,1,0:T(8,128)(2,1)} custom-call(bf16[1024,128]{1,0:T(8,128)(2,1)} %weight_hbm.1), custom_call_target="tpu_custom_call" | custom-call | tf_op jit(solution)/shard_map/pallas_call | solution.py:40
  2.6 13.2 %all-to-all-start.1 = ((bf16[32,128,128]{2,1,0:T(8,128)(2,1)}), bf16[32,128,128]{2,1,0:T(8,128)(2,1)S(1)}, u32[]{:S(2)}, u32[]{:S(2)}) async-start(bf16[32,128,128]{2,1,0:T(8,128)(2,1)} %bitcast.7), calls=%async_computation.1 | async-start | bytes 2097152 | tf_op jit(solution)/shard_map/all_to_all | solution.py:187
  15.8 2.2 %shard_map.69.gates_ref = bf16[128,1024]{1,0:T(8,128)(2,1)} custom-call(bf16[1024,128]{1,0:T(8,128)(2,1)} %gate_hbm.1, bf16[1024,128]{1,0:T(8,128)(2,1)} %up_hbm.1, bf16[1024,128]{1,0:T(8,128)(2,1)} %hidden_hbm.1), custom_call_target="tpu_custom_call" | custom-call | tf_op jit(solution)/shard_map/pallas_call | solution.py:74
  18.0 0.0 copy-start.1
  18.0 3.8 %collective-permute-start.1 = (bf16[128,1024]{1,0:T(8,128)(2,1)}, bf16[128,1024]{1,0:T(8,128)(2,1)S(1)}, u32[]{:S(2)}, u32[]{:S(2)}) collective-permute-start(bf16[128,1024]{1,0:T(8,128)(2,1)} %shard_map.69.gates_ref), channel_id=1, source_target_pairs={{0,8},{8,0},{16,24},{24,16},{1,9},{9,1},{17,25},{25,17},{2,10},{10... | collective-permute-start | bytes 786440 | tf_op jit(solution)/shard_map/ppermute | solution.py:190
  21.9 5.7 %shard_map.70 = (f32[128,1024]{1,0:T(8,128)}, bf16[128,1024]{1,0:T(8,128)(2,1)}, bf16[128,1024]{1,0:T(8,128)(2,1)}, bf16[128,1024]{1,0:T(8,128)(2,1)}) custom-call(bf16[128,1024]{1,0:T(8,128)(2,1)} %shard_map.69.gates_ref, bf16[1024,4096]{1,0:T(8,128)(2,1)} %tokens_hbm.1), custom_call_target="tpu_custom_call" | custom-call | flops 1073741824 | bytes 10485760 | tf_op jit(solution)/shard_map/pallas_call | solution.py:102
  27.5 0.0 copy-start
  27.5 7.4 %collective-permute-done.1 = bf16[128,1024]{1,0:T(8,128)(2,1)S(1)} collective-permute-done((bf16[128,1024]{1,0:T(8,128)(2,1)}, bf16[128,1024]{1,0:T(8,128)(2,1)S(1)}, u32[]{:S(2)}, u32[]{:S(2)}) %collective-permute-start.1) | collective-permute-done | bytes 262176 | tf_op jit(solution)/shard_map/ppermute | solution.py:190
  35.0 0.0 copy-done.1
  35.0 0.1 pad_maximum_fusion
  35.0 5.2 %collective-permute-start.2 = (bf16[2,128,1024]{2,1,0:T(8,128)(2,1)S(1)}, bf16[2,128,1024]{2,1,0:T(8,128)(2,1)S(1)}, u32[]{:S(2)}, u32[]{:S(2)}) collective-permute-start(bf16[2,128,1024]{2,1,0:T(8,128)(2,1)S(1)} %pad_maximum_fusion), channel_id=1, source_target_pairs={{0,16},{8,24},{16,0},{24,8},{1,17},{9,25},{17,1},{25,9},{2,18},{10... | collective-permute-start | bytes 1572872 | tf_op jit(solution)/shard_map/ppermute | solution.py:194
  40.2 3.8 %collective-permute-start.3 = (bf16[128,1024]{1,0:T(8,128)(2,1)}, bf16[128,1024]{1,0:T(8,128)(2,1)S(1)}, u32[]{:S(2)}, u32[]{:S(2)}) collective-permute-start(bf16[128,1024]{1,0:T(8,128)(2,1)} %get-tuple-element.29), channel_id=1, source_target_pairs={{3,0},{0,1},{1,2},{2,3},{7,4},{4,5},{5,6},{6,7},{11,8},{8,9},{9,10... | collective-permute-start | bytes 786440 | tf_op jit(solution)/shard_map/ppermute | solution.py:18
  44.0 4.2 %collective-permute-start.4 = (bf16[128,1024]{1,0:T(8,128)(2,1)}, bf16[128,1024]{1,0:T(8,128)(2,1)S(1)}, u32[]{:S(2)}, u32[]{:S(2)}) collective-permute-start(bf16[128,1024]{1,0:T(8,128)(2,1)} %get-tuple-element.30), channel_id=1, source_target_pairs={{1,0},{2,1},{3,2},{0,3},{5,4},{6,5},{7,6},{4,7},{9,8},{10,9},{11,1... | collective-permute-start | bytes 786440 | tf_op jit(solution)/shard_map/ppermute | solution.py:18
  48.2 7.1 %collective-permute-start.5 = (bf16[128,1024]{1,0:T(8,128)(2,1)}, bf16[128,1024]{1,0:T(8,128)(2,1)S(1)}, u32[]{:S(2)}, u32[]{:S(2)}) collective-permute-start(bf16[128,1024]{1,0:T(8,128)(2,1)} %get-tuple-element.31), channel_id=1, source_target_pairs={{2,0},{3,1},{0,2},{1,3},{6,4},{7,5},{4,6},{5,7},{10,8},{11,9},{8,1... | collective-permute-start | bytes 786440 | tf_op jit(solution)/shard_map/ppermute | solution.py:18
  55.3 0.0 collective-permute-done.2
  55.3 0.0 all-to-all-done.1
  55.3 40.3 %conditional.1 = (bf16[32,1024]{1,0:T(8,128)(2,1)S(1)}) conditional(s32[]{:T(128)} %convert_element_type.3, () %tuple.16, (bf16[32,128,128]{2,1,0:T(8,128)(2,1)S(1)}, bf16[2,128,1024]{2,1,0:T(8,128)(2,1)S(1)}, bf16[2,128,1024]{2,1,0:T(8,128)(2,1)S(1)}) %tuple.18), branch_computations={%region_0.0_spmd, %region_1.0_spmd} | conditional | flops 1073741824 | bytes 12582960 | solution.py:180
  55.4 1.9 %collective-permute-start = (bf16[4,128,1024]{2,1,0:T(8,128)(2,1)S(1)}, bf16[4,128,1024]{2,1,0:T(8,128)(2,1)S(1)}, u32[]{:S(2)}, u32[]{:S(2)}) collective-permute-start(bf16[4,128,1024]{2,1,0:T(8,128)(2,1)S(1)} %constant_dynamic-update-slice_fusion.mine_ref), channel_id=1, source_target_pairs={{4,0},{0,4},{5,1},{1,5},{6,2},{2,6},{7,3},{3,7},{12,8},{8,12},{13,... | collective-permute-start | bytes 3145736 | tf_op jit(solution)/shard_map/cond/branch_1_fun/ppermute | solution.py:18
  57.3 2.6 %collective-permute-done.other_ref = bf16[4,128,1024]{2,1,0:T(8,128)(2,1)S(1)} collective-permute-done((bf16[4,128,1024]{2,1,0:T(8,128)(2,1)S(1)}, bf16[4,128,1024]{2,1,0:T(8,128)(2,1)S(1)}, u32[]{:S(2)}, u32[]{:S(2)}) %collective-permute-start) | collective-permute-done | bytes 1048608 | tf_op jit(solution)/shard_map/cond/branch_1_fun/ppermute | solution.py:18
  60.0 1.3 %branch_1_fun.2 = bf16[512,1024]{1,0:T(8,128)(2,1)S(1)} custom-call(bf16[4,8,128,128]{3,2,1,0:T(8,128)(2,1)S(1)} %bitcast.8, bf16[4,128,1024]{2,1,0:T(8,128)(2,1)S(1)} %constant_dynamic-update-slice_fusion.mine_ref, bf16[4,128,1024]{2,1,0:T(8,128)(2,1)S(1)} %collective-permute-done.other_ref), custom_call_target="tpu_custom_call" | custom-call | flops 1073741824 | bytes 4194304 | tf_op jit(solution)/shard_map/cond/branch_1_fun/pallas_call | solution.py:149
  61.2 34.2 %all_to_all.9.pieces_ref = bf16[16,32,1024]{2,1,0:T(8,128)(2,1)S(1)} all-to-all(bf16[16,32,1024]{2,1,0:T(8,128)(2,1)S(1)} %bitcast.6), channel_id=1, replica_groups=mesh['zl'=2,'y'=8,'x'=4,'c'=2,'mp'=4] {'zl','y'}, dimensions={0} | all-to-all | bytes 2097152 | tf_op jit(solution)/shard_map/cond/branch_1_fun/all_to_all | solution.py:200
  95.5 0.1 branch_1_fun.3
  95.6 0.0 copy-start.2
  95.6 0.0 collective-permute-done.3.right_ref
  95.6 0.0 collective-permute-done.4.left_ref
  95.6 0.0 collective-permute-done.5.far_ref
  95.6 0.0 copy-done
  95.6 0.9 shard_map.71
  96.6 0.0 copy-done.2
  (2 shorter events, 0.1 us)
Async XLA Ops:
  2.6 52.7 %all-to-all-start.1 = ((bf16[32,128,128]{2,1,0:T(8,128)(2,1)}), bf16[32,128,128]{2,1,0:T(8,128)(2,1)S(1)}, u32[]{:S(2)}, u32[]{:S(2)}) async-start(bf16[32,128,128]{2,1,0:T(8,128)(2,1)} %bitcast.7), calls=%async_computation.1 | async-start | bytes 2097152 | tf_op jit(solution)/shard_map/all_to_all | solution.py:187
  18.0 17.0 %copy-start.1 = (bf16[128,1024]{1,0:T(8,128)(2,1)S(1)}, bf16[128,1024]{1,0:T(8,128)(2,1)}, u32[]{:S(2)}) copy-start(bf16[128,1024]{1,0:T(8,128)(2,1)} %shard_map.69.gates_ref) | copy-start | bytes 786436
  18.0 16.9 %collective-permute-start.1 = (bf16[128,1024]{1,0:T(8,128)(2,1)}, bf16[128,1024]{1,0:T(8,128)(2,1)S(1)}, u32[]{:S(2)}, u32[]{:S(2)}) collective-permute-start(bf16[128,1024]{1,0:T(8,128)(2,1)} %shard_map.69.gates_ref), channel_id=1, source_target_pairs={{0,8},{8,0},{16,24},{24,16},{1,9},{9,1},{17,25},{25,17},{2,10},{10... | collective-permute-start | bytes 786440 | tf_op jit(solution)/shard_map/ppermute | solution.py:190
  27.5 68.1 %copy-start = (f32[128,1024]{1,0:T(8,128)S(1)}, f32[128,1024]{1,0:T(8,128)}, u32[]{:S(2)}) copy-start(f32[128,1024]{1,0:T(8,128)} %get-tuple-element.33.own_ref) | copy-start | bytes 1572868
  35.0 20.3 %collective-permute-start.2 = (bf16[2,128,1024]{2,1,0:T(8,128)(2,1)S(1)}, bf16[2,128,1024]{2,1,0:T(8,128)(2,1)S(1)}, u32[]{:S(2)}, u32[]{:S(2)}) collective-permute-start(bf16[2,128,1024]{2,1,0:T(8,128)(2,1)S(1)} %pad_maximum_fusion), channel_id=1, source_target_pairs={{0,16},{8,24},{16,0},{24,8},{1,17},{9,25},{17,1},{25,9},{2,18},{10... | collective-permute-start | bytes 1572872 | tf_op jit(solution)/shard_map/ppermute | solution.py:194
  40.2 55.4 %collective-permute-start.3 = (bf16[128,1024]{1,0:T(8,128)(2,1)}, bf16[128,1024]{1,0:T(8,128)(2,1)S(1)}, u32[]{:S(2)}, u32[]{:S(2)}) collective-permute-start(bf16[128,1024]{1,0:T(8,128)(2,1)} %get-tuple-element.29), channel_id=1, source_target_pairs={{3,0},{0,1},{1,2},{2,3},{7,4},{4,5},{5,6},{6,7},{11,8},{8,9},{9,10... | collective-permute-start | bytes 786440 | tf_op jit(solution)/shard_map/ppermute | solution.py:18
  44.0 51.6 %collective-permute-start.4 = (bf16[128,1024]{1,0:T(8,128)(2,1)}, bf16[128,1024]{1,0:T(8,128)(2,1)S(1)}, u32[]{:S(2)}, u32[]{:S(2)}) collective-permute-start(bf16[128,1024]{1,0:T(8,128)(2,1)} %get-tuple-element.30), channel_id=1, source_target_pairs={{1,0},{2,1},{3,2},{0,3},{5,4},{6,5},{7,6},{4,7},{9,8},{10,9},{11,1... | collective-permute-start | bytes 786440 | tf_op jit(solution)/shard_map/ppermute | solution.py:18
  48.2 47.4 %collective-permute-start.5 = (bf16[128,1024]{1,0:T(8,128)(2,1)}, bf16[128,1024]{1,0:T(8,128)(2,1)S(1)}, u32[]{:S(2)}, u32[]{:S(2)}) collective-permute-start(bf16[128,1024]{1,0:T(8,128)(2,1)} %get-tuple-element.31), channel_id=1, source_target_pairs={{2,0},{3,1},{0,2},{1,3},{6,4},{7,5},{4,6},{5,7},{10,8},{11,9},{8,1... | collective-permute-start | bytes 786440 | tf_op jit(solution)/shard_map/ppermute | solution.py:18
  55.4 4.6 %collective-permute-start = (bf16[4,128,1024]{2,1,0:T(8,128)(2,1)S(1)}, bf16[4,128,1024]{2,1,0:T(8,128)(2,1)S(1)}, u32[]{:S(2)}, u32[]{:S(2)}) collective-permute-start(bf16[4,128,1024]{2,1,0:T(8,128)(2,1)S(1)} %constant_dynamic-update-slice_fusion.mine_ref), channel_id=1, source_target_pairs={{4,0},{0,4},{5,1},{1,5},{6,2},{2,6},{7,3},{3,7},{12,8},{8,12},{13,... | collective-permute-start | bytes 3145736 | tf_op jit(solution)/shard_map/cond/branch_1_fun/ppermute | solution.py:18
  95.6 1.0 copy-start.2

commit v9 on v7

--- a/solution.py
+++ b/solution.py
@@ -29,7 +29,7 @@
     for k in range(8):
         for q in range(4):
             spread[k, q * 32 : (q + 1) * 32, :] = weight[(q * 8 + k) * 32 : (q * 8 + k + 1) * 32, :]
-    copies = [pltpu.make_async_copy(spread, out_hbm.at[m], sems.at[m]) for m in range(4)]
+    copies = [pltpu.make_async_copy(spread, out_hbm.at[:, m], sems.at[m]) for m in range(4)]
     for copy in copies:
         copy.start()
     for copy in copies:
@@ -46,7 +46,7 @@
             pltpu.VMEM((8, 128, 128), BF16),
             pltpu.SemaphoreType.DMA((5,)),
         ],
-        out_shape=jax.ShapeDtypeStruct((4, 8, 128, 128), BF16),
+        out_shape=jax.ShapeDtypeStruct((8, 4, 128, 128), BF16),
         compiler_params=params(58),
     )(weight)
 
@@ -133,8 +133,10 @@
     for k in range(8):
         turn = ((0,) + TURNS)[k % 4]
         source = jnp.bitwise_and(x + turn, 3) * 2 + (c if k < 4 else 1 - c)
-        for m in range(4):
-            rows[m * 128 : (m + 1) * 128, k * 128 : (k + 1) * 128] = rows_ref[m, source]
+        for q in range(16):
+            at = ((q // 4 % 2 * 4 + q % 4) * 2 + q // 8) * 32
+            piece = rows_ref[source, q // 4, q % 4 * 32 : (q % 4 + 1) * 32, :]
+            rows[at : at + 32, k * 128 : (k + 1) * 128] = piece
     for t in range(2):
         columns = pl.ds(t * 512, 512)
         total = jnp.dot(
@@ -185,7 +187,7 @@
     norm_factor = float(tokens.shape[0] * lax.axis_size("mp")) ** (-0.5)
 
     rows = spread_rows(gate_weight).reshape(32, 128, 128)
-    rows = lax.all_to_all(rows, ("mp", "x", "c"), 0, 0, tiled=True).reshape(4, 8, 128, 128)
+    rows = lax.all_to_all(rows, ("x", "c", "mp"), 0, 0, tiled=True).reshape(8, 4, 128, 128)
 
     gates = gate_gradient(gate_pre, up_value, grad_hidden)
     mine = [shift(gates, "x", 4, k) for k in TURNS]
@@ -196,7 +198,7 @@
     def exchange(rows, *mine):
         mine = jnp.stack(mine)
         partial_sums = partial_product(rows, mine, shift(mine, "c", 2, 1))
-        pieces = lax.all_to_all(partial_sums.reshape(16, 32, 1024), ("zl", "y"), 0, 0, tiled=True)
+        pieces = lax.all_to_all(partial_sums.reshape(16, 32, 1024), ("y", "zl"), 0, 0, tiled=True)
         return sum_pieces(pieces)
 
     grad_tokens = always(exchange, rows, gates, *mine)

time: 93.7 us -> 94.6 us (level)
  the two profiles are of different devices: /device:TPU:8 before, /device:TPU:2 now
where the time goes in v9:
time: 94.6 us; the launch traced here: 94.1 us
  starting transfers between devices  40.6 us (43%)
  blocking collectives  39.3 us (42%)
  Pallas kernels  10.5 us (11%)
  waiting for transfers between devices  2.64 us (3%)
    all_to_all x1, blocking collectives, exchange(): lax.all_to_all(partial_sums.reshape(16, 32, 1024), ('y', 'zl'), 0, 0, til...  39.3 us
    ppermute x7, starting transfers between devices, shift(): lax.ppermute(array, axis, [((i + by) % size, i) for i in range(size)])  27.2 us
    all_to_all x1, starting transfers between devices, body(): lax.all_to_all(rows, ('x', 'c', 'mp'), 0, 0, tiled=True)  13.5 us
    pallas_call x1, Pallas kernels, weight_shares(): pl.pallas_call(share_kernel, in_specs=[IN_VMEM, IN_HBM], out_specs=[IN_VM...  4.7 us
    ppermute x7, waiting for transfers between devices, shift(): lax.ppermute(array, axis, [((i + by) % size, i) for i in range(size)])  2.64 us
    pallas_call x1, Pallas kernels, spread_rows(): pl.pallas_call(spread_kernel, in_specs=[IN_HBM], out_specs=IN_HBM, scratc...  1.98 us
  transfers between devices with their start and end apart: 8, of which 1 were waited for; matrix products, arithmetic and copies ran while one was open for 0% of the time, Pallas kernels for 8%

profile of v9, /device:TPU:2, one launch (start us, length us, event | category | flops | bytes accessed | tf_op | source)
XLA Modules:
  0.0 94.1 jit_solution(8445885708560357756)
XLA Ops:
  0.6 2.0 %shard_map.68 = bf16[8,4,128,128]{3,2,1,0:T(8,128)(2,1)} custom-call(bf16[1024,128]{1,0:T(8,128)(2,1)} %weight_hbm.1), custom_call_target="tpu_custom_call" | custom-call | tf_op jit(solution)/shard_map/pallas_call | solution.py:40
  2.6 13.5 %all-to-all-start.1 = ((bf16[32,128,128]{2,1,0:T(8,128)(2,1)}), bf16[32,128,128]{2,1,0:T(8,128)(2,1)S(1)}, u32[]{:S(2)}, u32[]{:S(2)}) async-start(bf16[32,128,128]{2,1,0:T(8,128)(2,1)} %bitcast.9), calls=%async_computation.1 | async-start | bytes 2097152 | tf_op jit(solution)/shard_map/all_to_all | solution.py:190
  16.1 1.5 %shard_map.69.gates_ref = bf16[128,1024]{1,0:T(8,128)(2,1)S(1)} custom-call(bf16[1024,128]{1,0:T(8,128)(2,1)} %gate_hbm.1, bf16[1024,128]{1,0:T(8,128)(2,1)} %up_hbm.1, bf16[1024,128]{1,0:T(8,128)(2,1)} %hidden_hbm.1), custom_call_target="tpu_custom_call" | custom-call | tf_op jit(solution)/shard_map/pallas_call | solution.py:74
  17.6 4.0 %collective-permute-start.3 = (bf16[128,1024]{1,0:T(8,128)(2,1)S(1)}, bf16[128,1024]{1,0:T(8,128)(2,1)S(1)}, u32[]{:S(2)}, u32[]{:S(2)}) collective-permute-start(bf16[128,1024]{1,0:T(8,128)(2,1)S(1)} %shard_map.69.gates_ref), channel_id=1, source_target_pairs={{16,0},{24,8},{0,16},{8,24},{17,1},{25,9},{1,17},{9,25},{18,2},{26... | collective-permute-start | bytes 786440 | tf_op jit(solution)/shard_map/ppermute | solution.py:18
  21.7 1.9 %collective-permute-start.2 = (bf16[128,1024]{1,0:T(8,128)(2,1)S(1)}, bf16[128,1024]{1,0:T(8,128)(2,1)S(1)}, u32[]{:S(2)}, u32[]{:S(2)}) collective-permute-start(bf16[128,1024]{1,0:T(8,128)(2,1)S(1)} %shard_map.69.gates_ref), channel_id=1, source_target_pairs={{24,0},{0,8},{8,16},{16,24},{25,1},{1,9},{9,17},{17,25},{26,2},{2,... | collective-permute-start | bytes 786440 | tf_op jit(solution)/shard_map/ppermute | solution.py:18
  23.6 3.9 %collective-permute-start.1 = (bf16[128,1024]{1,0:T(8,128)(2,1)S(1)}, bf16[128,1024]{1,0:T(8,128)(2,1)S(1)}, u32[]{:S(2)}, u32[]{:S(2)}) collective-permute-start(bf16[128,1024]{1,0:T(8,128)(2,1)S(1)} %shard_map.69.gates_ref), channel_id=1, source_target_pairs={{8,0},{16,8},{24,16},{0,24},{9,1},{17,9},{25,17},{1,25},{10,2},{18... | collective-permute-start | bytes 786440 | tf_op jit(solution)/shard_map/ppermute | solution.py:18
  27.5 4.7 %shard_map.70 = (f32[128,1024]{1,0:T(8,128)}, bf16[128,1024]{1,0:T(8,128)(2,1)}, bf16[128,1024]{1,0:T(8,128)(2,1)}, bf16[128,1024]{1,0:T(8,128)(2,1)}) custom-call(bf16[128,1024]{1,0:T(8,128)(2,1)S(1)} %shard_map.69.gates_ref, bf16[1024,4096]{1,0:T(8,128)(2,1)} %tokens_hbm.1), custom_call_target="tpu_custom_call" | custom-call | flops 1073741824 | bytes 10485760 | tf_op jit(solution)/shard_map/pallas_call | solution.py:102
  32.2 0.0 copy-start
  32.2 4.4 %collective-permute-start.4 = (bf16[128,1024]{1,0:T(8,128)(2,1)}, bf16[128,1024]{1,0:T(8,128)(2,1)S(1)}, u32[]{:S(2)}, u32[]{:S(2)}) collective-permute-start(bf16[128,1024]{1,0:T(8,128)(2,1)} %get-tuple-element.39), channel_id=1, source_target_pairs={{3,0},{0,1},{1,2},{2,3},{7,4},{4,5},{5,6},{6,7},{11,8},{8,9},{9,10... | collective-permute-start | bytes 786440 | tf_op jit(solution)/shard_map/ppermute | solution.py:18
  36.7 3.7 %collective-permute-start.5 = (bf16[128,1024]{1,0:T(8,128)(2,1)}, bf16[128,1024]{1,0:T(8,128)(2,1)S(1)}, u32[]{:S(2)}, u32[]{:S(2)}) collective-permute-start(bf16[128,1024]{1,0:T(8,128)(2,1)} %get-tuple-element.40), channel_id=1, source_target_pairs={{1,0},{2,1},{3,2},{0,3},{5,4},{6,5},{7,6},{4,7},{9,8},{10,9},{11,1... | collective-permute-start | bytes 786440 | tf_op jit(solution)/shard_map/ppermute | solution.py:18
  40.3 0.0 collective-permute-done.3
  40.3 7.3 %collective-permute-start.6 = (bf16[128,1024]{1,0:T(8,128)(2,1)}, bf16[128,1024]{1,0:T(8,128)(2,1)S(1)}, u32[]{:S(2)}, u32[]{:S(2)}) collective-permute-start(bf16[128,1024]{1,0:T(8,128)(2,1)} %get-tuple-element.41), channel_id=1, source_target_pairs={{2,0},{3,1},{0,2},{1,3},{6,4},{7,5},{4,6},{5,7},{10,8},{11,9},{8,1... | collective-permute-start | bytes 786440 | tf_op jit(solution)/shard_map/ppermute | solution.py:18
  47.6 0.0 collective-permute-done.2
  47.7 0.0 collective-permute-done.1
  47.7 0.0 all-to-all-done.1
  47.7 45.4 %conditional.1 = (bf16[32,1024]{1,0:T(8,128)(2,1)S(1)}) conditional(s32[]{:T(128)} %convert_element_type.3, () %tuple.16, (bf16[32,128,128]{2,1,0:T(8,128)(2,1)S(1)}, bf16[128,1024]{1,0:T(8,128)(2,1)S(1)}, bf16[128,1024]{1,0:T(8,128)(2,1)S(1)}, bf16[128,1024]{1,0:T(8,128)(2,1)S(1)}, bf16[128,1024]{1,0:T(8,128)(2,1)S(1)}) %tuple.18), branch_computations={%region_0.0_spmd, %region_1.0_spmd} | conditional | flops 1075314688 | bytes 12582960 | solution.py:183
  47.7 0.1 pad_maximum_fusion.mine_ref
  47.8 1.9 %collective-permute-start = (bf16[4,128,1024]{2,1,0:T(8,128)(2,1)S(1)}, bf16[4,128,1024]{2,1,0:T(8,128)(2,1)S(1)}, u32[]{:S(2)}, u32[]{:S(2)}) collective-permute-start(bf16[4,128,1024]{2,1,0:T(8,128)(2,1)S(1)} %pad_maximum_fusion.mine_ref), channel_id=1, source_target_pairs={{4,0},{0,4},{5,1},{1,5},{6,2},{2,6},{7,3},{3,7},{12,8},{8,12},{13,... | collective-permute-start | bytes 3145736 | tf_op jit(solution)/shard_map/cond/branch_1_fun/ppermute | solution.py:18
  49.8 2.6 %collective-permute-done.other_ref = bf16[4,128,1024]{2,1,0:T(8,128)(2,1)S(1)} collective-permute-done((bf16[4,128,1024]{2,1,0:T(8,128)(2,1)S(1)}, bf16[4,128,1024]{2,1,0:T(8,128)(2,1)S(1)}, u32[]{:S(2)}, u32[]{:S(2)}) %collective-permute-start) | collective-permute-done | bytes 1048608 | tf_op jit(solution)/shard_map/cond/branch_1_fun/ppermute | solution.py:18
  52.4 1.3 %branch_1_fun.2 = bf16[512,1024]{1,0:T(8,128)(2,1)S(1)} custom-call(bf16[8,4,128,128]{3,2,1,0:T(8,128)(2,1)S(1)} %bitcast.10, bf16[4,128,1024]{2,1,0:T(8,128)(2,1)S(1)} %pad_maximum_fusion.mine_ref, bf16[4,128,1024]{2,1,0:T(8,128)(2,1)S(1)} %collective-permute-done.other_ref), custom_call_target="tpu_custom_call" | custom-call | flops 1073741824 | bytes 4194304 | tf_op jit(solution)/shard_map/cond/branch_1_fun/pallas_call | solution.py:152
  53.6 39.3 %all_to_all.9.pieces_ref = bf16[16,32,1024]{2,1,0:T(8,128)(2,1)S(1)} all-to-all(bf16[16,32,1024]{2,1,0:T(8,128)(2,1)S(1)} %bitcast.8), channel_id=1, replica_groups=mesh['zl'=2,'y'=8,'x'=4,'c'=2,'mp'=4] {'y','zl'}, dimensions={0} | all-to-all | bytes 2097152 | tf_op jit(solution)/shard_map/cond/branch_1_fun/all_to_all | solution.py:201
  93.0 0.1 branch_1_fun.3
  93.1 0.0 copy-start.1
  93.1 0.0 collective-permute-done.4.right_ref
  93.1 0.0 collective-permute-done.5.left_ref
  93.1 0.0 collective-permute-done.6.far_ref
  93.1 0.0 copy-done
  93.2 0.9 shard_map.71
  94.1 0.0 copy-done.1
Async XLA Ops:
  2.6 45.0 %all-to-all-start.1 = ((bf16[32,128,128]{2,1,0:T(8,128)(2,1)}), bf16[32,128,128]{2,1,0:T(8,128)(2,1)S(1)}, u32[]{:S(2)}, u32[]{:S(2)}) async-start(bf16[32,128,128]{2,1,0:T(8,128)(2,1)} %bitcast.9), calls=%async_computation.1 | async-start | bytes 2097152 | tf_op jit(solution)/shard_map/all_to_all | solution.py:190
  17.6 22.7 %collective-permute-start.3 = (bf16[128,1024]{1,0:T(8,128)(2,1)S(1)}, bf16[128,1024]{1,0:T(8,128)(2,1)S(1)}, u32[]{:S(2)}, u32[]{:S(2)}) collective-permute-start(bf16[128,1024]{1,0:T(8,128)(2,1)S(1)} %shard_map.69.gates_ref), channel_id=1, source_target_pairs={{16,0},{24,8},{0,16},{8,24},{17,1},{25,9},{1,17},{9,25},{18,2},{26... | collective-permute-start | bytes 786440 | tf_op jit(solution)/shard_map/ppermute | solution.py:18
  21.7 26.0 %collective-permute-start.2 = (bf16[128,1024]{1,0:T(8,128)(2,1)S(1)}, bf16[128,1024]{1,0:T(8,128)(2,1)S(1)}, u32[]{:S(2)}, u32[]{:S(2)}) collective-permute-start(bf16[128,1024]{1,0:T(8,128)(2,1)S(1)} %shard_map.69.gates_ref), channel_id=1, source_target_pairs={{24,0},{0,8},{8,16},{16,24},{25,1},{1,9},{9,17},{17,25},{26,2},{2,... | collective-permute-start | bytes 786440 | tf_op jit(solution)/shard_map/ppermute | solution.py:18
  23.6 24.1 %collective-permute-start.1 = (bf16[128,1024]{1,0:T(8,128)(2,1)S(1)}, bf16[128,1024]{1,0:T(8,128)(2,1)S(1)}, u32[]{:S(2)}, u32[]{:S(2)}) collective-permute-start(bf16[128,1024]{1,0:T(8,128)(2,1)S(1)} %shard_map.69.gates_ref), channel_id=1, source_target_pairs={{8,0},{16,8},{24,16},{0,24},{9,1},{17,9},{25,17},{1,25},{10,2},{18... | collective-permute-start | bytes 786440 | tf_op jit(solution)/shard_map/ppermute | solution.py:18
  32.2 60.9 %copy-start = (f32[128,1024]{1,0:T(8,128)S(1)}, f32[128,1024]{1,0:T(8,128)}, u32[]{:S(2)}) copy-start(f32[128,1024]{1,0:T(8,128)} %get-tuple-element.43.own_ref) | copy-start | bytes 1572868
  32.2 60.9 %collective-permute-start.4 = (bf16[128,1024]{1,0:T(8,128)(2,1)}, bf16[128,1024]{1,0:T(8,128)(2,1)S(1)}, u32[]{:S(2)}, u32[]{:S(2)}) collective-permute-start(bf16[128,1024]{1,0:T(8,128)(2,1)} %get-tuple-element.39), channel_id=1, source_target_pairs={{3,0},{0,1},{1,2},{2,3},{7,4},{4,5},{5,6},{6,7},{11,8},{8,9},{9,10... | collective-permute-start | bytes 786440 | tf_op jit(solution)/shard_map/ppermute | solution.py:18
  36.7 56.5 %collective-permute-start.5 = (bf16[128,1024]{1,0:T(8,128)(2,1)}, bf16[128,1024]{1,0:T(8,128)(2,1)S(1)}, u32[]{:S(2)}, u32[]{:S(2)}) collective-permute-start(bf16[128,1024]{1,0:T(8,128)(2,1)} %get-tuple-element.40), channel_id=1, source_target_pairs={{1,0},{2,1},{3,2},{0,3},{5,4},{6,5},{7,6},{4,7},{9,8},{10,9},{11,1... | collective-permute-start | bytes 786440 | tf_op jit(solution)/shard_map/ppermute | solution.py:18
  40.3 52.8 %collective-permute-start.6 = (bf16[128,1024]{1,0:T(8,128)(2,1)}, bf16[128,1024]{1,0:T(8,128)(2,1)S(1)}, u32[]{:S(2)}, u32[]{:S(2)}) collective-permute-start(bf16[128,1024]{1,0:T(8,128)(2,1)} %get-tuple-element.41), channel_id=1, source_target_pairs={{2,0},{3,1},{0,2},{1,3},{6,4},{7,5},{4,6},{5,7},{10,8},{11,9},{8,1... | collective-permute-start | bytes 786440 | tf_op jit(solution)/shard_map/ppermute | solution.py:18
  47.8 4.6 %collective-permute-start = (bf16[4,128,1024]{2,1,0:T(8,128)(2,1)S(1)}, bf16[4,128,1024]{2,1,0:T(8,128)(2,1)S(1)}, u32[]{:S(2)}, u32[]{:S(2)}) collective-permute-start(bf16[4,128,1024]{2,1,0:T(8,128)(2,1)S(1)} %pad_maximum_fusion.mine_ref), channel_id=1, source_target_pairs={{4,0},{0,4},{5,1},{1,5},{6,2},{2,6},{7,3},{3,7},{12,8},{8,12},{13,... | collective-permute-start | bytes 3145736 | tf_op jit(solution)/shard_map/cond/branch_1_fun/ppermute | solution.py:18
  93.1 1.0 %copy-start.1 = (bf16[32,1024]{1,0:T(8,128)(2,1)}, bf16[32,1024]{1,0:T(8,128)(2,1)S(1)}, u32[]{:S(2)}) copy-start(bf16[32,1024]{1,0:T(8,128)(2,1)S(1)} %get-tuple-element.47) | copy-start | bytes 196612

commit v10 on v7

--- a/solution.py
+++ b/solution.py
@@ -51,64 +51,54 @@
     )(weight)
 
 
-def gate_kernel(gate_hbm, up_hbm, hidden_hbm, out_ref, *scratch):
-    sems = scratch[3]
-    copies = []
+def gate_kernel(gate_hbm, up_hbm, hidden_hbm, tokens_hbm, gates_ref, own_ref, right_ref, left_ref, far_ref, *scratch):
+    inputs, tokens, sems = scratch[:3], scratch[3], scratch[4]
+    m = lax.axis_index("mp")
+    copies, arrivals = [], []
     for step in range(4):
         rows = pl.ds(step * 256, 256)
         for n, source in enumerate((gate_hbm, up_hbm, hidden_hbm)):
-            copy = pltpu.make_async_copy(source.at[rows], scratch[n].at[rows], sems.at[n, step])
-            copy.start()
-            copies.append(copy)
+            copies.append(
+                pltpu.make_async_copy(source.at[rows], inputs[n].at[rows], sems.at[step * 3 + n])
+            )
+    for step in range(8):
+        column = jnp.bitwise_and(m + (2, 1, 3, 0)[step // 2], 3) * 1024 + step % 2 * 512
+        arrivals.append(
+            pltpu.make_async_copy(
+                tokens_hbm.at[:, pl.ds(pl.multiple_of(column, 512), 512)],
+                tokens.at[step],
+                sems.at[12 + step],
+            )
+        )
+    for copy in copies + arrivals:
+        copy.start()
     for step in range(4):
         rows = pl.ds(step * 256, 256)
         for copy in copies[step * 3 : step * 3 + 3]:
             copy.wait()
-        gate, up, hidden = (ref[rows].astype(F32) for ref in scratch[:3])
+        gate, up, hidden = (ref[rows].astype(F32) for ref in inputs)
         sigma = jax.nn.sigmoid(gate)
         product = hidden * up * sigma * (1.0 + gate * (1.0 - sigma))
-        out_ref[:, rows] = product.T.astype(BF16)
-
-
-def gate_gradient(gate_pre, up_value, grad_hidden):
-    return pl.pallas_call(
-        gate_kernel,
-        in_specs=[IN_HBM] * 3,
-        out_specs=IN_VMEM,
-        scratch_shapes=[pltpu.VMEM((1024, 128), BF16)] * 3 + [pltpu.SemaphoreType.DMA((3, 4))],
-        out_shape=jax.ShapeDtypeStruct((128, 1024), BF16),
-        compiler_params=params(58),
-    )(gate_pre, up_value, grad_hidden)
-
-
-def share_kernel(gates_ref, tokens_hbm, own_ref, right_ref, left_ref, far_ref, tokens, sems):
-    m = lax.axis_index("mp")
-    copies = []
-    for step in range(8):
-        column = jnp.bitwise_and(m + (2, 1, 3, 0)[step // 2], 3) * 1024 + step % 2 * 512
-        copy = pltpu.make_async_copy(
-            tokens_hbm.at[:, pl.ds(pl.multiple_of(column, 512), 512)], tokens.at[step], sems.at[step]
-        )
-        copy.start()
-        copies.append(copy)
-    for step, copy in enumerate(copies):
+        gates_ref[:, rows] = product.T.astype(BF16)
+    for step, copy in enumerate(arrivals):
         copy.wait()
         out_ref = (far_ref, right_ref, left_ref, own_ref)[step // 2]
         share = jnp.dot(gates_ref[...], tokens[step], preferred_element_type=F32)
         out_ref[:, step % 2 * 512 : (step % 2 + 1) * 512] = share.astype(out_ref.dtype)
 
 
-def weight_shares(gates, tokens):
-    return pl.pallas_call(
-        share_kernel,
-        in_specs=[IN_VMEM, IN_HBM],
-        out_specs=[IN_VMEM] * 4,
-        scratch_shapes=[pltpu.VMEM((8, 1024, 512), BF16), pltpu.SemaphoreType.DMA((8,))],
-        out_shape=[jax.ShapeDtypeStruct((128, 1024), F32)]
-        + [jax.ShapeDtypeStruct((128, 1024), BF16)] * 3,
+def gates_and_shares(gate_pre, up_value, grad_hidden, tokens):
+    part = jax.ShapeDtypeStruct((128, 1024), BF16)
+    return pl.pallas_call(
+        gate_kernel,
+        in_specs=[IN_HBM] * 4,
+        out_specs=[IN_VMEM] * 5,
+        scratch_shapes=[pltpu.VMEM((1024, 128), BF16)] * 3
+        + [pltpu.VMEM((8, 1024, 512), BF16), pltpu.SemaphoreType.DMA((20,))],
+        out_shape=[part, jax.ShapeDtypeStruct((128, 1024), F32), part, part, part],
         compiler_params=params(54),
         cost_estimate=pl.CostEstimate(flops=1 << 30, bytes_accessed=10 << 20, transcendentals=0),
-    )(gates, tokens)
+    )(gate_pre, up_value, grad_hidden, tokens)
 
 
 def add_kernel(scale, own_ref, right_ref, left_ref, far_ref, out_ref):
@@ -187,21 +177,24 @@
     rows = spread_rows(gate_weight).reshape(32, 128, 128)
     rows = lax.all_to_all(rows, ("mp", "x", "c"), 0, 0, tiled=True).reshape(4, 8, 128, 128)
 
-    gates = gate_gradient(gate_pre, up_value, grad_hidden)
+    gates, own, right, left, far = gates_and_shares(gate_pre, up_value, grad_hidden, tokens)
     mine = [shift(gates, "x", 4, k) for k in TURNS]
-    own, *shares = weight_shares(gates, tokens)
-    *mine, own = lax.optimization_barrier((*mine, own))
-    away = [shift(share, "mp", 4, -k) for k, share in zip(TURNS, shares)]
-
-    def exchange(rows, *mine):
-        mine = jnp.stack(mine)
-        partial_sums = partial_product(rows, mine, shift(mine, "c", 2, 1))
+    right, left = shift(right, "mp", 4, -1), shift(left, "mp", 4, 1)
+
+    def exchange(rows, mine, other):
+        partial_sums = partial_product(rows, mine, other)
         pieces = lax.all_to_all(partial_sums.reshape(16, 32, 1024), ("zl", "y"), 0, 0, tiled=True)
         return sum_pieces(pieces)
 
-    grad_tokens = always(exchange, rows, gates, *mine)
-    grad_tokens, own, *away = lax.optimization_barrier((grad_tokens, own, *away))
-    return (grad_tokens.T, add_shares(own, away, norm_factor))
+    def cross(rows, far, mine):
+        other = shift(mine, "c", 2, 1)
+        far = shift(far, "mp", 4, 2)
+        total = always(exchange, rows, mine, other)
+        return lax.optimization_barrier((total, far))
+
+    grad_tokens, far = always(cross, rows, far, jnp.stack([gates, *mine]))
+    grad_tokens, own, right, left, far = lax.optimization_barrier((grad_tokens, own, right, left, far))
+    return (grad_tokens.T, add_shares(own, (right, left, far), norm_factor))
 
 
 def solution(mesh):

time: 93.7 us -> 101 us (1.078)
  waiting for transfers between devices: 2.64 us -> 6.65 us
  blocking collectives: 36.3 us -> 39.3 us
  starting transfers between devices: 42.7 us -> 39.7 us
  Pallas kernels: 10.5 us -> 12.3 us
  other arithmetic: 0.13 us -> 1.24 us
    ppermute x7, waiting for transfers between devices: 2.64 us -> 6.64 us  [shift(): lax.ppermute(array, axis, [((i + by) % size, i) for i in range(size)])]
    ppermute x7, starting transfers between devices: 29.6 us -> 26.6 us  [shift(): lax.ppermute(array, axis, [((i + by) % size, i) for i in range(size)])]
    all_to_all x1, blocking collectives: 36.3 us -> 39.3 us  [exchange(): lax.all_to_all(partial_sums.reshape(16, 32, 1024), ('zl', 'y'), 0, 0, til...]
    pallas_call x1, Pallas kernels: 1.26 us -> 2.49 us  [partial_product(): pl.pallas_call(partial_kernel, in_specs=[IN_VMEM] * 3, out_specs=IN_VMEM,...]
    another operation x1, other arithmetic: 0.13 us -> 1.24 us  [body(): grad_tokens, far = always(cross, rows, far, jnp.stack([gates, *mine]))]
    pallas_call x2 -> x1, Pallas kernels: 6.23 us -> 5.21 us  [gates_and_shares(): pl.pallas_call(gate_kernel, in_specs=[IN_HBM] * 4, out_specs=[IN_VMEM] *...]
  transfers between devices with their start and end apart: 8 -> 8, of which waited for: 1 -> 1; matrix products, arithmetic and copies ran while one was open for 0% -> 1% of each run, Pallas kernels for 8% -> 8%
where the time goes in v10:
time: 101 us
  starting transfers between devices  39.7 us (39%)
  blocking collectives  39.3 us (39%)
  Pallas kernels  12.3 us (12%)
  waiting for transfers between devices  6.65 us (7%)
  other arithmetic  1.24 us (1%)
    all_to_all x1, blocking collectives, exchange(): lax.all_to_all(partial_sums.reshape(16, 32, 1024), ('zl', 'y'), 0, 0, til...  39.3 us
    ppermute x7, starting transfers between devices, shift(): lax.ppermute(array, axis, [((i + by) % size, i) for i in range(size)])  26.6 us
    all_to_all x1, starting transfers between devices, body(): lax.all_to_all(rows, ('mp', 'x', 'c'), 0, 0, tiled=True)  13.2 us
    ppermute x7, waiting for transfers between devices, shift(): lax.ppermute(array, axis, [((i + by) % size, i) for i in range(size)])  6.64 us
    pallas_call x1, Pallas kernels, gates_and_shares(): pl.pallas_call(gate_kernel, in_specs=[IN_HBM] * 4, out_specs=[IN_VMEM] *...  5.21 us
    pallas_call x1, Pallas kernels, partial_product(): pl.pallas_call(partial_kernel, in_specs=[IN_VMEM] * 3, out_specs=IN_VMEM,...  2.49 us
  transfers between devices with their start and end apart: 8, of which 1 were waited for; matrix products, arithmetic and copies ran while one was open for 1% of the time, Pallas kernels for 8%

profile of v10, /device:TPU:8, one launch (start us, length us, event | category | flops | bytes accessed | tf_op | source)
XLA Modules:
  0.0 100.8 jit_solution(10671041320596753131)
XLA Ops:
  0.6 2.0 %shard_map.69 = bf16[4,8,128,128]{3,2,1,0:T(8,128)(2,1)} custom-call(bf16[1024,128]{1,0:T(8,128)(2,1)} %weight_hbm.1), custom_call_target="tpu_custom_call" | custom-call | tf_op jit(solution)/shard_map/pallas_call | solution.py:40
  2.6 13.2 %all-to-all-start.1 = ((bf16[32,128,128]{2,1,0:T(8,128)(2,1)}), bf16[32,128,128]{2,1,0:T(8,128)(2,1)S(1)}, u32[]{:S(2)}, u32[]{:S(2)}) async-start(bf16[32,128,128]{2,1,0:T(8,128)(2,1)} %bitcast.9), calls=%async_computation.1 | async-start | bytes 2097152 | tf_op jit(solution)/shard_map/all_to_all | solution.py:178
  15.8 5.2 %shard_map.68 = (bf16[128,1024]{1,0:T(8,128)(2,1)}, f32[128,1024]{1,0:T(8,128)}, bf16[128,1024]{1,0:T(8,128)(2,1)}, bf16[128,1024]{1,0:T(8,128)(2,1)}, bf16[128,1024]{1,0:T(8,128)(2,1)}) custom-call(bf16[1024,128]{1,0:T(8,128)(2,1)} %gate_hbm.1, bf16[1024,128]{1,0:T(8,128)(2,1)} %up_hbm.1, bf16[1024,128]{1,0:T(8,128)(2,1)} %hidden_hbm.1, ...), custom_call_target="tpu_custom_call" | custom-call | flops 1073741824 | bytes 10485760 | tf_op jit(solution)/shard_map/pallas_call | solution.py:92
  21.0 0.0 copy-start
  21.0 5.0 %collective-permute-start.2 = (bf16[128,1024]{1,0:T(8,128)(2,1)}, bf16[128,1024]{1,0:T(8,128)(2,1)S(1)}, u32[]{:S(2)}, u32[]{:S(2)}) collective-permute-start(bf16[128,1024]{1,0:T(8,128)(2,1)} %get-tuple-element.37), channel_id=1, source_target_pairs={{8,0},{16,8},{24,16},{0,24},{9,1},{17,9},{25,17},{1,25},{10,2},{18... | collective-permute-start | bytes 786440 | tf_op jit(solution)/shard_map/ppermute | solution.py:18
  26.1 1.9 %collective-permute-start.3 = (bf16[128,1024]{1,0:T(8,128)(2,1)}, bf16[128,1024]{1,0:T(8,128)(2,1)S(1)}, u32[]{:S(2)}, u32[]{:S(2)}) collective-permute-start(bf16[128,1024]{1,0:T(8,128)(2,1)} %get-tuple-element.37), channel_id=1, source_target_pairs={{24,0},{0,8},{8,16},{16,24},{25,1},{1,9},{9,17},{17,25},{26,2},{2,... | collective-permute-start | bytes 786440 | tf_op jit(solution)/shard_map/ppermute | solution.py:18
  28.0 4.2 %collective-permute-start.4 = (bf16[128,1024]{1,0:T(8,128)(2,1)}, bf16[128,1024]{1,0:T(8,128)(2,1)S(1)}, u32[]{:S(2)}, u32[]{:S(2)}) collective-permute-start(bf16[128,1024]{1,0:T(8,128)(2,1)} %get-tuple-element.37), channel_id=1, source_target_pairs={{16,0},{24,8},{0,16},{8,24},{17,1},{25,9},{1,17},{9,25},{18,2},{26... | collective-permute-start | bytes 786440 | tf_op jit(solution)/shard_map/ppermute | solution.py:18
  32.2 4.3 %collective-permute-start.5 = (bf16[128,1024]{1,0:T(8,128)(2,1)}, bf16[128,1024]{1,0:T(8,128)(2,1)S(1)}, u32[]{:S(2)}, u32[]{:S(2)}) collective-permute-start(bf16[128,1024]{1,0:T(8,128)(2,1)} %get-tuple-element.41), channel_id=1, source_target_pairs={{3,0},{0,1},{1,2},{2,3},{7,4},{4,5},{5,6},{6,7},{11,8},{8,9},{9,10... | collective-permute-start | bytes 786440 | tf_op jit(solution)/shard_map/ppermute | solution.py:18
  36.5 3.7 %collective-permute-start.6 = (bf16[128,1024]{1,0:T(8,128)(2,1)}, bf16[128,1024]{1,0:T(8,128)(2,1)S(1)}, u32[]{:S(2)}, u32[]{:S(2)}) collective-permute-start(bf16[128,1024]{1,0:T(8,128)(2,1)} %get-tuple-element.42), channel_id=1, source_target_pairs={{1,0},{2,1},{3,2},{0,3},{5,4},{6,5},{7,6},{4,7},{9,8},{10,9},{11,1... | collective-permute-start | bytes 786440 | tf_op jit(solution)/shard_map/ppermute | solution.py:18
  40.2 0.0 collective-permute-done.2
  40.2 6.6 %collective-permute-done.3 = bf16[128,1024]{1,0:T(8,128)(2,1)S(1)} collective-permute-done((bf16[128,1024]{1,0:T(8,128)(2,1)}, bf16[128,1024]{1,0:T(8,128)(2,1)S(1)}, u32[]{:S(2)}, u32[]{:S(2)}) %collective-permute-start.3) | collective-permute-done | bytes 262176 | tf_op jit(solution)/shard_map/ppermute | solution.py:18
  46.8 0.0 copy-start.1
  46.8 0.0 collective-permute-done.4
  46.8 0.0 copy-start.2
  46.8 0.7 copy-done.1
  47.6 0.1 copy-done.2
  47.6 1.2 %pad_maximum_fusion = bf16[4,128,1024]{2,1,0:T(8,128)(2,1)S(1)} fusion(bf16[1,128,1024]{2,1,0:T(8,128)(2,1)} %bitcast.14, bf16[1,128,1024]{2,1,0:T(8,128)(2,1)} %bitcast.13, bf16[1,128,1024]{2,1,0:T(8,128)(2,1)S(1)} %bitcast.12, bf16[1,128,1024]{2,1,0:T(8,128)(2,1)} %bitcast.11), kind=kLoop, calls=%fused_computation | loop fusion | flops 1572864 | bytes 2097152 | tf_op jit(solution)/shard_map/stack | solution.py:195
  48.9 0.0 all-to-all-done.1
  48.9 50.0 %conditional.2 = (bf16[32,1024]{1,0:T(8,128)(2,1)}, bf16[128,1024]{1,0:T(8,128)(2,1)}) conditional(s32[]{:T(128)} %convert_element_type.6, () %tuple.23, (bf16[4,128,1024]{2,1,0:T(8,128)(2,1)S(1)}, bf16[32,128,128]{2,1,0:T(8,128)(2,1)S(1)}, bf16[128,1024]{1,0:T(8,128)(2,1)}) %tuple.24), branch_computations={%region_0.0_spmd, %region_1.0_spmd} | conditional | flops 1073741824 | bytes 11534566 | solution.py:171
  48.9 1.9 %collective-permute-start = (bf16[4,128,1024]{2,1,0:T(8,128)(2,1)S(1)}, bf16[4,128,1024]{2,1,0:T(8,128)(2,1)}, u32[]{:S(2)}, u32[]{:S(2)}) collective-permute-start(bf16[4,128,1024]{2,1,0:T(8,128)(2,1)S(1)} %get-tuple-element.21), channel_id=1, source_target_pairs={{4,0},{0,4},{5,1},{1,5},{6,2},{2,6},{7,3},{3,7},{12,8},{8,12},{13,... | collective-permute-start | bytes 3145736 | tf_op jit(solution)/shard_map/cond/branch_1_fun/ppermute | solution.py:18
  50.8 5.5 %collective-permute-start.1 = (bf16[128,1024]{1,0:T(8,128)(2,1)}, bf16[128,1024]{1,0:T(8,128)(2,1)}, u32[]{:S(2)}, u32[]{:S(2)}) collective-permute-start(bf16[128,1024]{1,0:T(8,128)(2,1)} %get-tuple-element.22), channel_id=1, source_target_pairs={{2,0},{3,1},{0,2},{1,3},{6,4},{7,5},{4,6},{5,7},{10,8},{11,9},{8,1... | collective-permute-start | bytes 786440 | tf_op jit(solution)/shard_map/cond/branch_1_fun/ppermute | solution.py:18
  56.4 0.0 collective-permute-done
  56.4 42.5 %conditional = (bf16[32,1024]{1,0:T(8,128)(2,1)}) conditional(s32[]{:T(128)} %convert_element_type.4, () %tuple.15, (bf16[32,128,128]{2,1,0:T(8,128)(2,1)S(1)}, bf16[4,128,1024]{2,1,0:T(8,128)(2,1)S(1)}, bf16[4,128,1024]{2,1,0:T(8,128)(2,1)}) %tuple.16), branch_computations={%region_2.0_spmd, %region_3.0_spmd} | conditional | flops 1073741824 | bytes 6291464 | solution.py:171
  56.4 2.5 %branch_1_fun.2 = bf16[512,1024]{1,0:T(8,128)(2,1)S(1)} custom-call(bf16[4,8,128,128]{3,2,1,0:T(8,128)(2,1)S(1)} %bitcast.10, bf16[4,128,1024]{2,1,0:T(8,128)(2,1)S(1)} %get-tuple-element.18.mine_ref, bf16[4,128,1024]{2,1,0:T(8,128)(2,1)} %get-tuple-element.19.other_ref), custom_call_target="tpu_custom_call" | custom-call | flops 1073741824 | bytes 4194304 | tf_op jit(solution)/shard_map/cond/branch_1_fun/cond/branch_1_fun/pallas_call | solution.py:140
  58.9 39.3 %all_to_all.9.pieces_ref = bf16[16,32,1024]{2,1,0:T(8,128)(2,1)S(1)} all-to-all(bf16[16,32,1024]{2,1,0:T(8,128)(2,1)S(1)} %bitcast.8), channel_id=1, replica_groups=mesh['zl'=2,'y'=8,'x'=4,'c'=2,'mp'=4] {'zl','y'}, dimensions={0} | all-to-all | bytes 2097152 | tf_op jit(solution)/shard_map/cond/branch_1_fun/cond/branch_1_fun/all_to_all | solution.py:186
  98.1 0.8 branch_1_fun.3
  98.9 0.0 collective-permute-done.1
  98.9 0.0 collective-permute-done.5.right_ref
  98.9 0.0 collective-permute-done.6.left_ref
  98.9 0.0 copy-done
  98.9 1.9 %shard_map.70 = bf16[1024,128]{1,0:T(8,128)(2,1)} custom-call(f32[128,1024]{1,0:T(8,128)S(1)} %copy-done, bf16[128,1024]{1,0:T(8,128)(2,1)S(1)} %collective-permute-done.5.right_ref, bf16[128,1024]{1,0:T(8,128)(2,1)S(1)} %collective-permute-done.6.left_ref, bf16[128,1024]{1,0:T(8,128)(2,1)} %get-tuple-element.48.far_ref), custom_call_target="tpu_custom_call" | custom-call | tf_op jit(solution)/shard_map/pallas_call | solution.py:112
Async XLA Ops:
  2.6 46.3 %all-to-all-start.1 = ((bf16[32,128,128]{2,1,0:T(8,128)(2,1)}), bf16[32,128,128]{2,1,0:T(8,128)(2,1)S(1)}, u32[]{:S(2)}, u32[]{:S(2)}) async-start(bf16[32,128,128]{2,1,0:T(8,128)(2,1)} %bitcast.9), calls=%async_computation.1 | async-start | bytes 2097152 | tf_op jit(solution)/shard_map/all_to_all | solution.py:178
  21.0 77.9 %copy-start = (f32[128,1024]{1,0:T(8,128)S(1)}, f32[128,1024]{1,0:T(8,128)}, u32[]{:S(2)}) copy-start(f32[128,1024]{1,0:T(8,128)} %get-tuple-element.45.own_ref) | copy-start | bytes 1572868
  21.0 19.2 %collective-permute-start.2 = (bf16[128,1024]{1,0:T(8,128)(2,1)}, bf16[128,1024]{1,0:T(8,128)(2,1)S(1)}, u32[]{:S(2)}, u32[]{:S(2)}) collective-permute-start(bf16[128,1024]{1,0:T(8,128)(2,1)} %get-tuple-element.37), channel_id=1, source_target_pairs={{8,0},{16,8},{24,16},{0,24},{9,1},{17,9},{25,17},{1,25},{10,2},{18... | collective-permute-start | bytes 786440 | tf_op jit(solution)/shard_map/ppermute | solution.py:18
  26.1 20.8 %collective-permute-start.3 = (bf16[128,1024]{1,0:T(8,128)(2,1)}, bf16[128,1024]{1,0:T(8,128)(2,1)S(1)}, u32[]{:S(2)}, u32[]{:S(2)}) collective-permute-start(bf16[128,1024]{1,0:T(8,128)(2,1)} %get-tuple-element.37), channel_id=1, source_target_pairs={{24,0},{0,8},{8,16},{16,24},{25,1},{1,9},{9,17},{17,25},{26,2},{2,... | collective-permute-start | bytes 786440 | tf_op jit(solution)/shard_map/ppermute | solution.py:18
  28.0 18.8 %collective-permute-start.4 = (bf16[128,1024]{1,0:T(8,128)(2,1)}, bf16[128,1024]{1,0:T(8,128)(2,1)S(1)}, u32[]{:S(2)}, u32[]{:S(2)}) collective-permute-start(bf16[128,1024]{1,0:T(8,128)(2,1)} %get-tuple-element.37), channel_id=1, source_target_pairs={{16,0},{24,8},{0,16},{8,24},{17,1},{25,9},{1,17},{9,25},{18,2},{26... | collective-permute-start | bytes 786440 | tf_op jit(solution)/shard_map/ppermute | solution.py:18
  32.2 66.7 %collective-permute-start.5 = (bf16[128,1024]{1,0:T(8,128)(2,1)}, bf16[128,1024]{1,0:T(8,128)(2,1)S(1)}, u32[]{:S(2)}, u32[]{:S(2)}) collective-permute-start(bf16[128,1024]{1,0:T(8,128)(2,1)} %get-tuple-element.41), channel_id=1, source_target_pairs={{3,0},{0,1},{1,2},{2,3},{7,4},{4,5},{5,6},{6,7},{11,8},{8,9},{9,10... | collective-permute-start | bytes 786440 | tf_op jit(solution)/shard_map/ppermute | solution.py:18
  36.5 62.4 %collective-permute-start.6 = (bf16[128,1024]{1,0:T(8,128)(2,1)}, bf16[128,1024]{1,0:T(8,128)(2,1)S(1)}, u32[]{:S(2)}, u32[]{:S(2)}) collective-permute-start(bf16[128,1024]{1,0:T(8,128)(2,1)} %get-tuple-element.42), channel_id=1, source_target_pairs={{1,0},{2,1},{3,2},{0,3},{5,4},{6,5},{7,6},{4,7},{9,8},{10,9},{11,1... | collective-permute-start | bytes 786440 | tf_op jit(solution)/shard_map/ppermute | solution.py:18
  46.8 0.7 copy-start.1
  46.8 0.8 copy-start.2
  48.9 7.5 %collective-permute-start = (bf16[4,128,1024]{2,1,0:T(8,128)(2,1)S(1)}, bf16[4,128,1024]{2,1,0:T(8,128)(2,1)}, u32[]{:S(2)}, u32[]{:S(2)}) collective-permute-start(bf16[4,128,1024]{2,1,0:T(8,128)(2,1)S(1)} %get-tuple-element.21), channel_id=1, source_target_pairs={{4,0},{0,4},{5,1},{1,5},{6,2},{2,6},{7,3},{3,7},{12,8},{8,12},{13,... | collective-permute-start | bytes 3145736 | tf_op jit(solution)/shard_map/cond/branch_1_fun/ppermute | solution.py:18
  50.8 48.1 %collective-permute-start.1 = (bf16[128,1024]{1,0:T(8,128)(2,1)}, bf16[128,1024]{1,0:T(8,128)(2,1)}, u32[]{:S(2)}, u32[]{:S(2)}) collective-permute-start(bf16[128,1024]{1,0:T(8,128)(2,1)} %get-tuple-element.22), channel_id=1, source_target_pairs={{2,0},{3,1},{0,2},{1,3},{6,4},{7,5},{4,6},{5,7},{10,8},{11,9},{8,1... | collective-permute-start | bytes 786440 | tf_op jit(solution)/shard_map/cond/branch_1_fun/ppermute | solution.py:18

commit v11 on v7

--- a/solution.py
+++ b/solution.py
@@ -111,9 +111,9 @@
     )(gates, tokens)
 
 
-def add_kernel(scale, own_ref, right_ref, left_ref, far_ref, out_ref):
+def add_kernel(scale, own_ref, first_ref, second_ref, third_ref, out_ref):
     total = own_ref[...]
-    for ref in (right_ref, left_ref, far_ref):
+    for ref in (first_ref, second_ref, third_ref):
         total += ref[...].astype(F32)
     out_ref[...] = (total * scale).T.astype(BF16)
 
@@ -191,7 +191,9 @@
     mine = [shift(gates, "x", 4, k) for k in TURNS]
     own, *shares = weight_shares(gates, tokens)
     *mine, own = lax.optimization_barrier((*mine, own))
-    away = [shift(share, "mp", 4, -k) for k, share in zip(TURNS, shares)]
+    right, left, far = shares
+    far = shift(far, "mp", 4, 2)
+    away = far, shift(right, "mp", 4, -1), shift(left, "mp", 4, 1)
 
     def exchange(rows, *mine):
         mine = jnp.stack(mine)

time: 93.7 us -> 102 us (1.089)
  the two profiles are of different devices: /device:TPU:8 before, /device:TPU:138 now
where the time goes in v11:
time: 102 us; the launch traced here: 101 us
  starting transfers between devices  52.8 us (52%)
  blocking collectives  34.5 us (34%)
  Pallas kernels  10.5 us (10%)
  waiting for transfers between devices  2.28 us (2%)
    ppermute x7, starting transfers between devices, shift(): lax.ppermute(array, axis, [((i + by) % size, i) for i in range(size)])  41.2 us
    all_to_all x1, blocking collectives, exchange(): lax.all_to_all(partial_sums.reshape(16, 32, 1024), ('zl', 'y'), 0, 0, til...  34.5 us
    all_to_all x1, starting transfers between devices, body(): lax.all_to_all(rows, ('mp', 'x', 'c'), 0, 0, tiled=True)  11.6 us
    pallas_call x1, Pallas kernels, weight_shares(): pl.pallas_call(share_kernel, in_specs=[IN_VMEM, IN_HBM], out_specs=[IN_VM...  4.7 us
    ppermute x7, waiting for transfers between devices, shift(): lax.ppermute(array, axis, [((i + by) % size, i) for i in range(size)])  2.28 us
  transfers between devices with their start and end apart: 8, of which 1 were waited for; matrix products, arithmetic and copies ran while one was open for 0% of the time, Pallas kernels for 8%

profile of v11, /device:TPU:138, one launch (start us, length us, event | category | flops | bytes accessed | tf_op | source)
XLA Modules:
  0.0 101.1 jit_solution(3214107436720125343)
XLA Ops:
  0.6 2.0 %shard_map.68 = bf16[4,8,128,128]{3,2,1,0:T(8,128)(2,1)} custom-call(bf16[1024,128]{1,0:T(8,128)(2,1)} %weight_hbm.1), custom_call_target="tpu_custom_call" | custom-call | tf_op jit(solution)/shard_map/pallas_call | solution.py:40
  2.6 11.6 %all-to-all-start.1 = ((bf16[32,128,128]{2,1,0:T(8,128)(2,1)}), bf16[32,128,128]{2,1,0:T(8,128)(2,1)S(1)}, u32[]{:S(2)}, u32[]{:S(2)}) async-start(bf16[32,128,128]{2,1,0:T(8,128)(2,1)} %bitcast.9), calls=%async_computation.1 | async-start | bytes 2097152 | tf_op jit(solution)/shard_map/all_to_all | solution.py:188
  14.3 1.5 %shard_map.69.gates_ref = bf16[128,1024]{1,0:T(8,128)(2,1)S(1)} custom-call(bf16[1024,128]{1,0:T(8,128)(2,1)} %gate_hbm.1, bf16[1024,128]{1,0:T(8,128)(2,1)} %up_hbm.1, bf16[1024,128]{1,0:T(8,128)(2,1)} %hidden_hbm.1), custom_call_target="tpu_custom_call" | custom-call | tf_op jit(solution)/shard_map/pallas_call | solution.py:74
  15.8 4.0 %collective-permute-start.3 = (bf16[128,1024]{1,0:T(8,128)(2,1)S(1)}, bf16[128,1024]{1,0:T(8,128)(2,1)S(1)}, u32[]{:S(2)}, u32[]{:S(2)}) collective-permute-start(bf16[128,1024]{1,0:T(8,128)(2,1)S(1)} %shard_map.69.gates_ref), channel_id=1, source_target_pairs={{16,0},{24,8},{0,16},{8,24},{17,1},{25,9},{1,17},{9,25},{18,2},{26... | collective-permute-start | bytes 786440 | tf_op jit(solution)/shard_map/ppermute | solution.py:18
  19.8 1.9 %collective-permute-start.2 = (bf16[128,1024]{1,0:T(8,128)(2,1)S(1)}, bf16[128,1024]{1,0:T(8,128)(2,1)S(1)}, u32[]{:S(2)}, u32[]{:S(2)}) collective-permute-start(bf16[128,1024]{1,0:T(8,128)(2,1)S(1)} %shard_map.69.gates_ref), channel_id=1, source_target_pairs={{24,0},{0,8},{8,16},{16,24},{25,1},{1,9},{9,17},{17,25},{26,2},{2,... | collective-permute-start | bytes 786440 | tf_op jit(solution)/shard_map/ppermute | solution.py:18
  21.7 3.9 %collective-permute-start.1 = (bf16[128,1024]{1,0:T(8,128)(2,1)S(1)}, bf16[128,1024]{1,0:T(8,128)(2,1)S(1)}, u32[]{:S(2)}, u32[]{:S(2)}) collective-permute-start(bf16[128,1024]{1,0:T(8,128)(2,1)S(1)} %shard_map.69.gates_ref), channel_id=1, source_target_pairs={{8,0},{16,8},{24,16},{0,24},{9,1},{17,9},{25,17},{1,25},{10,2},{18... | collective-permute-start | bytes 786440 | tf_op jit(solution)/shard_map/ppermute | solution.py:18
  25.7 4.7 %shard_map.70 = (f32[128,1024]{1,0:T(8,128)}, bf16[128,1024]{1,0:T(8,128)(2,1)}, bf16[128,1024]{1,0:T(8,128)(2,1)}, bf16[128,1024]{1,0:T(8,128)(2,1)}) custom-call(bf16[128,1024]{1,0:T(8,128)(2,1)S(1)} %shard_map.69.gates_ref, bf16[1024,4096]{1,0:T(8,128)(2,1)} %tokens_hbm.1), custom_call_target="tpu_custom_call" | custom-call | flops 1073741824 | bytes 10485760 | tf_op jit(solution)/shard_map/pallas_call | solution.py:102
  30.4 0.0 copy-start
  30.4 5.7 %collective-permute-start.4 = (bf16[128,1024]{1,0:T(8,128)(2,1)}, bf16[128,1024]{1,0:T(8,128)(2,1)S(1)}, u32[]{:S(2)}, u32[]{:S(2)}) collective-permute-start(bf16[128,1024]{1,0:T(8,128)(2,1)} %get-tuple-element.39), channel_id=1, source_target_pairs={{2,0},{3,1},{0,2},{1,3},{6,4},{7,5},{4,6},{5,7},{10,8},{11,9},{8,1... | collective-permute-start | bytes 786440 | tf_op jit(solution)/shard_map/ppermute | solution.py:18
  36.1 2.4 %collective-permute-start.5 = (bf16[128,1024]{1,0:T(8,128)(2,1)}, bf16[128,1024]{1,0:T(8,128)(2,1)S(1)}, u32[]{:S(2)}, u32[]{:S(2)}) collective-permute-start(bf16[128,1024]{1,0:T(8,128)(2,1)} %get-tuple-element.40), channel_id=1, source_target_pairs={{3,0},{0,1},{1,2},{2,3},{7,4},{4,5},{5,6},{6,7},{11,8},{8,9},{9,10... | collective-permute-start | bytes 786440 | tf_op jit(solution)/shard_map/ppermute | solution.py:18
  38.5 0.0 collective-permute-done.3
  38.5 4.4 %collective-permute-start.6 = (bf16[128,1024]{1,0:T(8,128)(2,1)}, bf16[128,1024]{1,0:T(8,128)(2,1)S(1)}, u32[]{:S(2)}, u32[]{:S(2)}) collective-permute-start(bf16[128,1024]{1,0:T(8,128)(2,1)} %get-tuple-element.41), channel_id=1, source_target_pairs={{1,0},{2,1},{3,2},{0,3},{5,4},{6,5},{7,6},{4,7},{9,8},{10,9},{11,1... | collective-permute-start | bytes 786440 | tf_op jit(solution)/shard_map/ppermute | solution.py:18
  42.8 0.0 collective-permute-done.2
  42.9 0.0 collective-permute-done.1
  42.9 0.0 all-to-all-done.1
  42.9 57.2 %conditional.1 = (bf16[32,1024]{1,0:T(8,128)(2,1)S(1)}) conditional(s32[]{:T(128)} %convert_element_type.3, () %tuple.16, (bf16[32,128,128]{2,1,0:T(8,128)(2,1)S(1)}, bf16[128,1024]{1,0:T(8,128)(2,1)S(1)}, bf16[128,1024]{1,0:T(8,128)(2,1)S(1)}, bf16[128,1024]{1,0:T(8,128)(2,1)S(1)}, bf16[128,1024]{1,0:T(8,128)(2,1)S(1)}) %tuple.18), branch_computations={%region_0.0_spmd, %region_1.0_spmd} | conditional | flops 1075314688 | bytes 12582960 | solution.py:181
  42.9 0.1 pad_maximum_fusion.mine_ref
  43.0 18.9 %collective-permute-start = (bf16[4,128,1024]{2,1,0:T(8,128)(2,1)S(1)}, bf16[4,128,1024]{2,1,0:T(8,128)(2,1)S(1)}, u32[]{:S(2)}, u32[]{:S(2)}) collective-permute-start(bf16[4,128,1024]{2,1,0:T(8,128)(2,1)S(1)} %pad_maximum_fusion.mine_ref), channel_id=1, source_target_pairs={{4,0},{0,4},{5,1},{1,5},{6,2},{2,6},{7,3},{3,7},{12,8},{8,12},{13,... | collective-permute-start | bytes 3145736 | tf_op jit(solution)/shard_map/cond/branch_1_fun/ppermute | solution.py:18
  62.0 2.3 %collective-permute-done.other_ref = bf16[4,128,1024]{2,1,0:T(8,128)(2,1)S(1)} collective-permute-done((bf16[4,128,1024]{2,1,0:T(8,128)(2,1)S(1)}, bf16[4,128,1024]{2,1,0:T(8,128)(2,1)S(1)}, u32[]{:S(2)}, u32[]{:S(2)}) %collective-permute-start) | collective-permute-done | bytes 1048608 | tf_op jit(solution)/shard_map/cond/branch_1_fun/ppermute | solution.py:18
  64.2 1.3 %branch_1_fun.2 = bf16[512,1024]{1,0:T(8,128)(2,1)S(1)} custom-call(bf16[4,8,128,128]{3,2,1,0:T(8,128)(2,1)S(1)} %bitcast.10, bf16[4,128,1024]{2,1,0:T(8,128)(2,1)S(1)} %pad_maximum_fusion.mine_ref, bf16[4,128,1024]{2,1,0:T(8,128)(2,1)S(1)} %collective-permute-done.other_ref), custom_call_target="tpu_custom_call" | custom-call | flops 1073741824 | bytes 4194304 | tf_op jit(solution)/shard_map/cond/branch_1_fun/pallas_call | solution.py:150
  65.5 34.5 %all_to_all.9.pieces_ref = bf16[16,32,1024]{2,1,0:T(8,128)(2,1)S(1)} all-to-all(bf16[16,32,1024]{2,1,0:T(8,128)(2,1)S(1)} %bitcast.8), channel_id=1, replica_groups=mesh['zl'=2,'y'=8,'x'=4,'c'=2,'mp'=4] {'zl','y'}, dimensions={0} | all-to-all | bytes 2097152 | tf_op jit(solution)/shard_map/cond/branch_1_fun/all_to_all | solution.py:201
  100.0 0.1 branch_1_fun.3
  100.1 0.0 copy-start.1
  100.1 0.0 collective-permute-done.4.first_ref
  100.1 0.0 collective-permute-done.5.second_ref
  100.2 0.0 collective-permute-done.6.third_ref
  100.2 0.0 copy-done
  100.2 0.9 shard_map.71
  101.1 0.0 copy-done.1
Async XLA Ops:
  2.6 40.2 %all-to-all-start.1 = ((bf16[32,128,128]{2,1,0:T(8,128)(2,1)}), bf16[32,128,128]{2,1,0:T(8,128)(2,1)S(1)}, u32[]{:S(2)}, u32[]{:S(2)}) async-start(bf16[32,128,128]{2,1,0:T(8,128)(2,1)} %bitcast.9), calls=%async_computation.1 | async-start | bytes 2097152 | tf_op jit(solution)/shard_map/all_to_all | solution.py:188
  15.8 22.7 %collective-permute-start.3 = (bf16[128,1024]{1,0:T(8,128)(2,1)S(1)}, bf16[128,1024]{1,0:T(8,128)(2,1)S(1)}, u32[]{:S(2)}, u32[]{:S(2)}) collective-permute-start(bf16[128,1024]{1,0:T(8,128)(2,1)S(1)} %shard_map.69.gates_ref), channel_id=1, source_target_pairs={{16,0},{24,8},{0,16},{8,24},{17,1},{25,9},{1,17},{9,25},{18,2},{26... | collective-permute-start | bytes 786440 | tf_op jit(solution)/shard_map/ppermute | solution.py:18
  19.8 23.1 %collective-permute-start.2 = (bf16[128,1024]{1,0:T(8,128)(2,1)S(1)}, bf16[128,1024]{1,0:T(8,128)(2,1)S(1)}, u32[]{:S(2)}, u32[]{:S(2)}) collective-permute-start(bf16[128,1024]{1,0:T(8,128)(2,1)S(1)} %shard_map.69.gates_ref), channel_id=1, source_target_pairs={{24,0},{0,8},{8,16},{16,24},{25,1},{1,9},{9,17},{17,25},{26,2},{2,... | collective-permute-start | bytes 786440 | tf_op jit(solution)/shard_map/ppermute | solution.py:18
  21.7 21.1 %collective-permute-start.1 = (bf16[128,1024]{1,0:T(8,128)(2,1)S(1)}, bf16[128,1024]{1,0:T(8,128)(2,1)S(1)}, u32[]{:S(2)}, u32[]{:S(2)}) collective-permute-start(bf16[128,1024]{1,0:T(8,128)(2,1)S(1)} %shard_map.69.gates_ref), channel_id=1, source_target_pairs={{8,0},{16,8},{24,16},{0,24},{9,1},{17,9},{25,17},{1,25},{10,2},{18... | collective-permute-start | bytes 786440 | tf_op jit(solution)/shard_map/ppermute | solution.py:18
  30.4 69.8 %copy-start = (f32[128,1024]{1,0:T(8,128)S(1)}, f32[128,1024]{1,0:T(8,128)}, u32[]{:S(2)}) copy-start(f32[128,1024]{1,0:T(8,128)} %get-tuple-element.43.own_ref) | copy-start | bytes 1572868
  30.4 69.8 %collective-permute-start.4 = (bf16[128,1024]{1,0:T(8,128)(2,1)}, bf16[128,1024]{1,0:T(8,128)(2,1)S(1)}, u32[]{:S(2)}, u32[]{:S(2)}) collective-permute-start(bf16[128,1024]{1,0:T(8,128)(2,1)} %get-tuple-element.39), channel_id=1, source_target_pairs={{2,0},{3,1},{0,2},{1,3},{6,4},{7,5},{4,6},{5,7},{10,8},{11,9},{8,1... | collective-permute-start | bytes 786440 | tf_op jit(solution)/shard_map/ppermute | solution.py:18
  36.1 64.1 %collective-permute-start.5 = (bf16[128,1024]{1,0:T(8,128)(2,1)}, bf16[128,1024]{1,0:T(8,128)(2,1)S(1)}, u32[]{:S(2)}, u32[]{:S(2)}) collective-permute-start(bf16[128,1024]{1,0:T(8,128)(2,1)} %get-tuple-element.40), channel_id=1, source_target_pairs={{3,0},{0,1},{1,2},{2,3},{7,4},{4,5},{5,6},{6,7},{11,8},{8,9},{9,10... | collective-permute-start | bytes 786440 | tf_op jit(solution)/shard_map/ppermute | solution.py:18
  38.5 61.7 %collective-permute-start.6 = (bf16[128,1024]{1,0:T(8,128)(2,1)}, bf16[128,1024]{1,0:T(8,128)(2,1)S(1)}, u32[]{:S(2)}, u32[]{:S(2)}) collective-permute-start(bf16[128,1024]{1,0:T(8,128)(2,1)} %get-tuple-element.41), channel_id=1, source_target_pairs={{1,0},{2,1},{3,2},{0,3},{5,4},{6,5},{7,6},{4,7},{9,8},{10,9},{11,1... | collective-permute-start | bytes 786440 | tf_op jit(solution)/shard_map/ppermute | solution.py:18
  43.0 21.2 %collective-permute-start = (bf16[4,128,1024]{2,1,0:T(8,128)(2,1)S(1)}, bf16[4,128,1024]{2,1,0:T(8,128)(2,1)S(1)}, u32[]{:S(2)}, u32[]{:S(2)}) collective-permute-start(bf16[4,128,1024]{2,1,0:T(8,128)(2,1)S(1)} %pad_maximum_fusion.mine_ref), channel_id=1, source_target_pairs={{4,0},{0,4},{5,1},{1,5},{6,2},{2,6},{7,3},{3,7},{12,8},{8,12},{13,... | collective-permute-start | bytes 3145736 | tf_op jit(solution)/shard_map/cond/branch_1_fun/ppermute | solution.py:18
  100.1 1.0 copy-start.1

commit v12 on v7

--- a/solution.py
+++ b/solution.py
@@ -191,17 +191,18 @@
     mine = [shift(gates, "x", 4, k) for k in TURNS]
     own, *shares = weight_shares(gates, tokens)
     *mine, own = lax.optimization_barrier((*mine, own))
-    away = [shift(share, "mp", 4, -k) for k, share in zip(TURNS, shares)]
-
-    def exchange(rows, *mine):
+    right, left, far = shares
+    right, far = shift(right, "mp", 4, -1), shift(far, "mp", 4, 2)
+
+    def exchange(rows, left, *mine):
         mine = jnp.stack(mine)
         partial_sums = partial_product(rows, mine, shift(mine, "c", 2, 1))
         pieces = lax.all_to_all(partial_sums.reshape(16, 32, 1024), ("zl", "y"), 0, 0, tiled=True)
-        return sum_pieces(pieces)
-
-    grad_tokens = always(exchange, rows, gates, *mine)
-    grad_tokens, own, *away = lax.optimization_barrier((grad_tokens, own, *away))
-    return (grad_tokens.T, add_shares(own, away, norm_factor))
+        return sum_pieces(pieces), shift(left, "mp", 4, 1)
+
+    grad_tokens, left = always(exchange, rows, left, gates, *mine)
+    grad_tokens, own, right, left, far = lax.optimization_barrier((grad_tokens, own, right, left, far))
+    return (grad_tokens.T, add_shares(own, (right, left, far), norm_factor))
 
 
 def solution(mesh):

time: 93.7 us -> 92.9 us (level)
  blocking collectives: 36.3 us -> 0 us
  waiting for transfers between devices: 2.64 us -> 27.5 us
  starting transfers between devices: 42.7 us -> 51.4 us
  Pallas kernels: 10.5 us -> 12.5 us
    all_to_all x1 -> x0, blocking collectives: 36.3 us -> none  [exchange(): lax.all_to_all(partial_sums.reshape(16, 32, 1024), ('zl', 'y'), 0, 0, til...]
    all_to_all x0 -> x1, waiting for transfers between devices: none -> 23.1 us  [exchange(): lax.all_to_all(partial_sums.reshape(16, 32, 1024), ('zl', 'y'), 0, 0, til...]
    all_to_all x0 -> x1, starting transfers between devices: none -> 11.8 us  [exchange(): lax.all_to_all(partial_sums.reshape(16, 32, 1024), ('zl', 'y'), 0, 0, til...]
    ppermute x7, starting transfers between devices: 29.6 us -> 26.4 us  [shift(): lax.ppermute(array, axis, [((i + by) % size, i) for i in range(size)])]
    ppermute x7, waiting for transfers between devices: 2.64 us -> 4.48 us  [shift(): lax.ppermute(array, axis, [((i + by) % size, i) for i in range(size)])]
    pallas_call x1, Pallas kernels: 1.26 us -> 2.25 us  [partial_product(): pl.pallas_call(partial_kernel, in_specs=[IN_VMEM] * 3, out_specs=IN_VMEM,...]
    pallas_call x1, Pallas kernels: 0.91 us -> 1.85 us  [add_shares(): pl.pallas_call(functools.partial(add_kernel, scale), in_specs=[IN_VMEM] *...]
  transfers between devices with their start and end apart: 8 -> 9, of which waited for: 1 -> 3; matrix products, arithmetic and copies ran while one was open for 0% -> 0% of each run, Pallas kernels for 8% -> 9%
where the time goes in v12:
time: 92.9 us; the launch traced here: 92.3 us
  starting transfers between devices  51.4 us (55%)
  waiting for transfers between devices  27.5 us (30%)
  Pallas kernels  12.5 us (13%)
    ppermute x7, starting transfers between devices, shift(): lax.ppermute(array, axis, [((i + by) % size, i) for i in range(size)])  26.4 us
    all_to_all x1, waiting for transfers between devices, exchange(): lax.all_to_all(partial_sums.reshape(16, 32, 1024), ('zl', 'y'), 0, 0, til...  23.1 us
    all_to_all x1, starting transfers between devices, body(): lax.all_to_all(rows, ('mp', 'x', 'c'), 0, 0, tiled=True)  13.2 us
    all_to_all x1, starting transfers between devices, exchange(): lax.all_to_all(partial_sums.reshape(16, 32, 1024), ('zl', 'y'), 0, 0, til...  11.8 us
    pallas_call x1, Pallas kernels, weight_shares(): pl.pallas_call(share_kernel, in_specs=[IN_VMEM, IN_HBM], out_specs=[IN_VM...  4.7 us
    ppermute x7, waiting for transfers between devices, shift(): lax.ppermute(array, axis, [((i + by) % size, i) for i in range(size)])  4.48 us
    pallas_call x1, Pallas kernels, partial_product(): pl.pallas_call(partial_kernel, in_specs=[IN_VMEM] * 3, out_specs=IN_VMEM,...  2.25 us
    pallas_call x1, Pallas kernels, spread_rows(): pl.pallas_call(spread_kernel, in_specs=[IN_HBM], out_specs=IN_HBM, scratc...  1.99 us
  transfers between devices with their start and end apart: 9, of which 3 were waited for; matrix products, arithmetic and copies ran while one was open for 0% of the time, Pallas kernels for 9%

profile of v12, /device:TPU:8, one launch (start us, length us, event | category | flops | bytes accessed | tf_op | source)
XLA Modules:
  0.0 92.3 jit_solution(17171805816778107878)
XLA Ops:
  0.6 2.0 %shard_map.68 = bf16[4,8,128,128]{3,2,1,0:T(8,128)(2,1)} custom-call(bf16[1024,128]{1,0:T(8,128)(2,1)} %weight_hbm.1), custom_call_target="tpu_custom_call" | custom-call | tf_op jit(solution)/shard_map/pallas_call | solution.py:40
  2.6 13.2 %all-to-all-start.1 = ((bf16[32,128,128]{2,1,0:T(8,128)(2,1)}), bf16[32,128,128]{2,1,0:T(8,128)(2,1)S(1)}, u32[]{:S(2)}, u32[]{:S(2)}) async-start(bf16[32,128,128]{2,1,0:T(8,128)(2,1)} %bitcast.8), calls=%async_computation.1 | async-start | bytes 2097152 | tf_op jit(solution)/shard_map/all_to_all | solution.py:188
  15.8 1.5 %shard_map.69.gates_ref = bf16[128,1024]{1,0:T(8,128)(2,1)S(1)} custom-call(bf16[1024,128]{1,0:T(8,128)(2,1)} %gate_hbm.1, bf16[1024,128]{1,0:T(8,128)(2,1)} %up_hbm.1, bf16[1024,128]{1,0:T(8,128)(2,1)} %hidden_hbm.1), custom_call_target="tpu_custom_call" | custom-call | tf_op jit(solution)/shard_map/pallas_call | solution.py:74
  17.3 4.9 %collective-permute-start.2 = (bf16[128,1024]{1,0:T(8,128)(2,1)S(1)}, bf16[128,1024]{1,0:T(8,128)(2,1)S(1)}, u32[]{:S(2)}, u32[]{:S(2)}) collective-permute-start(bf16[128,1024]{1,0:T(8,128)(2,1)S(1)} %shard_map.69.gates_ref), channel_id=1, source_target_pairs={{8,0},{16,8},{24,16},{0,24},{9,1},{17,9},{25,17},{1,25},{10,2},{18... | collective-permute-start | bytes 786440 | tf_op jit(solution)/shard_map/ppermute | solution.py:18
  22.3 1.9 %collective-permute-start.3 = (bf16[128,1024]{1,0:T(8,128)(2,1)S(1)}, bf16[128,1024]{1,0:T(8,128)(2,1)S(1)}, u32[]{:S(2)}, u32[]{:S(2)}) collective-permute-start(bf16[128,1024]{1,0:T(8,128)(2,1)S(1)} %shard_map.69.gates_ref), channel_id=1, source_target_pairs={{24,0},{0,8},{8,16},{16,24},{25,1},{1,9},{9,17},{17,25},{26,2},{2,... | collective-permute-start | bytes 786440 | tf_op jit(solution)/shard_map/ppermute | solution.py:18
  24.2 4.2 %collective-permute-start.4 = (bf16[128,1024]{1,0:T(8,128)(2,1)S(1)}, bf16[128,1024]{1,0:T(8,128)(2,1)S(1)}, u32[]{:S(2)}, u32[]{:S(2)}) collective-permute-start(bf16[128,1024]{1,0:T(8,128)(2,1)S(1)} %shard_map.69.gates_ref), channel_id=1, source_target_pairs={{16,0},{24,8},{0,16},{8,24},{17,1},{25,9},{1,17},{9,25},{18,2},{26... | collective-permute-start | bytes 786440 | tf_op jit(solution)/shard_map/ppermute | solution.py:18
  28.4 4.7 %shard_map.70 = (f32[128,1024]{1,0:T(8,128)}, bf16[128,1024]{1,0:T(8,128)(2,1)}, bf16[128,1024]{1,0:T(8,128)(2,1)S(1)}, bf16[128,1024]{1,0:T(8,128)(2,1)}) custom-call(bf16[128,1024]{1,0:T(8,128)(2,1)S(1)} %shard_map.69.gates_ref, bf16[1024,4096]{1,0:T(8,128)(2,1)} %tokens_hbm.1), custom_call_target="tpu_custom_call" | custom-call | flops 1073741824 | bytes 10485760 | tf_op jit(solution)/shard_map/pallas_call | solution.py:102
  33.1 0.0 copy-start
  33.1 4.4 %collective-permute-start.5 = (bf16[128,1024]{1,0:T(8,128)(2,1)}, bf16[128,1024]{1,0:T(8,128)(2,1)S(1)}, u32[]{:S(2)}, u32[]{:S(2)}) collective-permute-start(bf16[128,1024]{1,0:T(8,128)(2,1)} %get-tuple-element.43), channel_id=1, source_target_pairs={{3,0},{0,1},{1,2},{2,3},{7,4},{4,5},{5,6},{6,7},{11,8},{8,9},{9,10... | collective-permute-start | bytes 786440 | tf_op jit(solution)/shard_map/ppermute | solution.py:18
  37.5 5.5 %collective-permute-start.6 = (bf16[128,1024]{1,0:T(8,128)(2,1)}, bf16[128,1024]{1,0:T(8,128)(2,1)S(1)}, u32[]{:S(2)}, u32[]{:S(2)}) collective-permute-start(bf16[128,1024]{1,0:T(8,128)(2,1)} %get-tuple-element.45), channel_id=1, source_target_pairs={{2,0},{3,1},{0,2},{1,3},{6,4},{7,5},{4,6},{5,7},{10,8},{11,9},{8,1... | collective-permute-start | bytes 786440 | tf_op jit(solution)/shard_map/ppermute | solution.py:18
  43.1 0.0 collective-permute-done.2
  43.1 1.8 %collective-permute-done.3 = bf16[128,1024]{1,0:T(8,128)(2,1)S(1)} collective-permute-done((bf16[128,1024]{1,0:T(8,128)(2,1)S(1)}, bf16[128,1024]{1,0:T(8,128)(2,1)S(1)}, u32[]{:S(2)}, u32[]{:S(2)}) %collective-permute-start.3) | collective-permute-done | bytes 262176 | tf_op jit(solution)/shard_map/ppermute | solution.py:18
  44.9 0.0 collective-permute-done.4
  45.0 0.0 all-to-all-done.1
  45.0 45.4 %conditional.1 = (bf16[32,1024]{1,0:T(8,128)(2,1)S(1)}, bf16[128,1024]{1,0:T(8,128)(2,1)}) conditional(s32[]{:T(128)} %convert_element_type.3, () %tuple.18, (bf16[32,128,128]{2,1,0:T(8,128)(2,1)S(1)}, bf16[128,1024]{1,0:T(8,128)(2,1)S(1)}, bf16[128,1024]{1,0:T(8,128)(2,1)S(1)}, bf16[128,1024]{1,0:T(8,128)(2,1)S(1)}, bf16[128,1024]{1,0:T(8,128)(2,1)S(1)}, ...), branch_computations={%region_0.0_spmd, %region_1.0_spmd} | conditional | flops 1075314688 | bytes 14680192 | solution.py:181
  45.0 0.1 pad_maximum_fusion.mine_ref
  45.1 1.9 %collective-permute-start = (bf16[4,128,1024]{2,1,0:T(8,128)(2,1)S(1)}, bf16[4,128,1024]{2,1,0:T(8,128)(2,1)S(1)}, u32[]{:S(2)}, u32[]{:S(2)}) collective-permute-start(bf16[4,128,1024]{2,1,0:T(8,128)(2,1)S(1)} %pad_maximum_fusion.mine_ref), channel_id=1, source_target_pairs={{4,0},{0,4},{5,1},{1,5},{6,2},{2,6},{7,3},{3,7},{12,8},{8,12},{13,... | collective-permute-start | bytes 3145736 | tf_op jit(solution)/shard_map/cond/branch_1_fun/ppermute | solution.py:18
  47.0 2.6 %collective-permute-done.other_ref = bf16[4,128,1024]{2,1,0:T(8,128)(2,1)S(1)} collective-permute-done((bf16[4,128,1024]{2,1,0:T(8,128)(2,1)S(1)}, bf16[4,128,1024]{2,1,0:T(8,128)(2,1)S(1)}, u32[]{:S(2)}, u32[]{:S(2)}) %collective-permute-start) | collective-permute-done | bytes 1048608 | tf_op jit(solution)/shard_map/cond/branch_1_fun/ppermute | solution.py:18
  49.6 2.2 %branch_1_fun.2 = bf16[512,1024]{1,0:T(8,128)(2,1)} custom-call(bf16[4,8,128,128]{3,2,1,0:T(8,128)(2,1)S(1)} %bitcast.9, bf16[4,128,1024]{2,1,0:T(8,128)(2,1)S(1)} %pad_maximum_fusion.mine_ref, bf16[4,128,1024]{2,1,0:T(8,128)(2,1)S(1)} %collective-permute-done.other_ref), custom_call_target="tpu_custom_call" | custom-call | flops 1073741824 | bytes 4194304 | tf_op jit(solution)/shard_map/cond/branch_1_fun/pallas_call | solution.py:150
  51.9 11.8 %all-to-all-start = ((bf16[16,32,1024]{2,1,0:T(8,128)(2,1)}), bf16[16,32,1024]{2,1,0:T(8,128)(2,1)S(1)}, u32[]{:S(2)}, u32[]{:S(2)}) async-start(bf16[16,32,1024]{2,1,0:T(8,128)(2,1)} %bitcast.5), calls=%async_computation | async-start | bytes 2097152 | tf_op jit(solution)/shard_map/cond/branch_1_fun/all_to_all | solution.py:200
  63.7 3.5 %collective-permute-start.1 = (bf16[128,1024]{1,0:T(8,128)(2,1)S(1)}, bf16[128,1024]{1,0:T(8,128)(2,1)}, u32[]{:S(2)}, u32[]{:S(2)}) collective-permute-start(bf16[128,1024]{1,0:T(8,128)(2,1)S(1)} %get-tuple-element.18), channel_id=1, source_target_pairs={{1,0},{2,1},{3,2},{0,3},{5,4},{6,5},{7,6},{4,7},{9,8},{10,9},{11,1... | collective-permute-start | bytes 786440 | tf_op jit(solution)/shard_map/cond/branch_1_fun/ppermute | solution.py:18
  67.2 23.1 %all-to-all-done.pieces_ref = bf16[16,32,1024]{2,1,0:T(8,128)(2,1)S(1)} async-done(((bf16[16,32,1024]{2,1,0:T(8,128)(2,1)}), bf16[16,32,1024]{2,1,0:T(8,128)(2,1)S(1)}, u32[]{:S(2)}, u32[]{:S(2)}) %all-to-all-start) | async-done | bytes 1048608 | tf_op jit(solution)/shard_map/cond/branch_1_fun/all_to_all | solution.py:200
  90.2 0.1 branch_1_fun.3
  90.4 0.0 collective-permute-done.1
  90.4 0.0 copy-start.1
  90.4 0.0 collective-permute-done.5.right_ref
  90.4 0.0 collective-permute-done.6.far_ref
  90.4 0.0 copy-done
  90.4 1.9 %shard_map.71 = bf16[1024,128]{1,0:T(8,128)(2,1)} custom-call(f32[128,1024]{1,0:T(8,128)S(1)} %copy-done, bf16[128,1024]{1,0:T(8,128)(2,1)S(1)} %collective-permute-done.5.right_ref, bf16[128,1024]{1,0:T(8,128)(2,1)} %get-tuple-element.49.left_ref, bf16[128,1024]{1,0:T(8,128)(2,1)S(1)} %collective-permute-done.6.far_ref), custom_call_target="tpu_custom_call" | custom-call | tf_op jit(solution)/shard_map/pallas_call | solution.py:122
  92.3 0.0 copy-done.1
Async XLA Ops:
  2.6 42.3 %all-to-all-start.1 = ((bf16[32,128,128]{2,1,0:T(8,128)(2,1)}), bf16[32,128,128]{2,1,0:T(8,128)(2,1)S(1)}, u32[]{:S(2)}, u32[]{:S(2)}) async-start(bf16[32,128,128]{2,1,0:T(8,128)(2,1)} %bitcast.8), calls=%async_computation.1 | async-start | bytes 2097152 | tf_op jit(solution)/shard_map/all_to_all | solution.py:188
  17.3 25.8 %collective-permute-start.2 = (bf16[128,1024]{1,0:T(8,128)(2,1)S(1)}, bf16[128,1024]{1,0:T(8,128)(2,1)S(1)}, u32[]{:S(2)}, u32[]{:S(2)}) collective-permute-start(bf16[128,1024]{1,0:T(8,128)(2,1)S(1)} %shard_map.69.gates_ref), channel_id=1, source_target_pairs={{8,0},{16,8},{24,16},{0,24},{9,1},{17,9},{25,17},{1,25},{10,2},{18... | collective-permute-start | bytes 786440 | tf_op jit(solution)/shard_map/ppermute | solution.py:18
  22.3 22.7 %collective-permute-start.3 = (bf16[128,1024]{1,0:T(8,128)(2,1)S(1)}, bf16[128,1024]{1,0:T(8,128)(2,1)S(1)}, u32[]{:S(2)}, u32[]{:S(2)}) collective-permute-start(bf16[128,1024]{1,0:T(8,128)(2,1)S(1)} %shard_map.69.gates_ref), channel_id=1, source_target_pairs={{24,0},{0,8},{8,16},{16,24},{25,1},{1,9},{9,17},{17,25},{26,2},{2,... | collective-permute-start | bytes 786440 | tf_op jit(solution)/shard_map/ppermute | solution.py:18
  24.2 20.8 %collective-permute-start.4 = (bf16[128,1024]{1,0:T(8,128)(2,1)S(1)}, bf16[128,1024]{1,0:T(8,128)(2,1)S(1)}, u32[]{:S(2)}, u32[]{:S(2)}) collective-permute-start(bf16[128,1024]{1,0:T(8,128)(2,1)S(1)} %shard_map.69.gates_ref), channel_id=1, source_target_pairs={{16,0},{24,8},{0,16},{8,24},{17,1},{25,9},{1,17},{9,25},{18,2},{26... | collective-permute-start | bytes 786440 | tf_op jit(solution)/shard_map/ppermute | solution.py:18
  33.1 57.3 %copy-start = (f32[128,1024]{1,0:T(8,128)S(1)}, f32[128,1024]{1,0:T(8,128)}, u32[]{:S(2)}) copy-start(f32[128,1024]{1,0:T(8,128)} %get-tuple-element.47.own_ref) | copy-start | bytes 1572868
  33.1 57.3 %collective-permute-start.5 = (bf16[128,1024]{1,0:T(8,128)(2,1)}, bf16[128,1024]{1,0:T(8,128)(2,1)S(1)}, u32[]{:S(2)}, u32[]{:S(2)}) collective-permute-start(bf16[128,1024]{1,0:T(8,128)(2,1)} %get-tuple-element.43), channel_id=1, source_target_pairs={{3,0},{0,1},{1,2},{2,3},{7,4},{4,5},{5,6},{6,7},{11,8},{8,9},{9,10... | collective-permute-start | bytes 786440 | tf_op jit(solution)/shard_map/ppermute | solution.py:18
  37.5 52.9 %collective-permute-start.6 = (bf16[128,1024]{1,0:T(8,128)(2,1)}, bf16[128,1024]{1,0:T(8,128)(2,1)S(1)}, u32[]{:S(2)}, u32[]{:S(2)}) collective-permute-start(bf16[128,1024]{1,0:T(8,128)(2,1)} %get-tuple-element.45), channel_id=1, source_target_pairs={{2,0},{3,1},{0,2},{1,3},{6,4},{7,5},{4,6},{5,7},{10,8},{11,9},{8,1... | collective-permute-start | bytes 786440 | tf_op jit(solution)/shard_map/ppermute | solution.py:18
  45.1 4.6 %collective-permute-start = (bf16[4,128,1024]{2,1,0:T(8,128)(2,1)S(1)}, bf16[4,128,1024]{2,1,0:T(8,128)(2,1)S(1)}, u32[]{:S(2)}, u32[]{:S(2)}) collective-permute-start(bf16[4,128,1024]{2,1,0:T(8,128)(2,1)S(1)} %pad_maximum_fusion.mine_ref), channel_id=1, source_target_pairs={{4,0},{0,4},{5,1},{1,5},{6,2},{2,6},{7,3},{3,7},{12,8},{8,12},{13,... | collective-permute-start | bytes 3145736 | tf_op jit(solution)/shard_map/cond/branch_1_fun/ppermute | solution.py:18
  51.9 38.3 %all-to-all-start = ((bf16[16,32,1024]{2,1,0:T(8,128)(2,1)}), bf16[16,32,1024]{2,1,0:T(8,128)(2,1)S(1)}, u32[]{:S(2)}, u32[]{:S(2)}) async-start(bf16[16,32,1024]{2,1,0:T(8,128)(2,1)} %bitcast.5), calls=%async_computation | async-start | bytes 2097152 | tf_op jit(solution)/shard_map/cond/branch_1_fun/all_to_all | solution.py:200
  63.7 26.7 %collective-permute-start.1 = (bf16[128,1024]{1,0:T(8,128)(2,1)S(1)}, bf16[128,1024]{1,0:T(8,128)(2,1)}, u32[]{:S(2)}, u32[]{:S(2)}) collective-permute-start(bf16[128,1024]{1,0:T(8,128)(2,1)S(1)} %get-tuple-element.18), channel_id=1, source_target_pairs={{1,0},{2,1},{3,2},{0,3},{5,4},{6,5},{7,6},{4,7},{9,8},{10,9},{11,1... | collective-permute-start | bytes 786440 | tf_op jit(solution)/shard_map/cond/branch_1_fun/ppermute | solution.py:18
  90.4 1.9 %copy-start.1 = (bf16[32,1024]{1,0:T(8,128)(2,1)}, bf16[32,1024]{1,0:T(8,128)(2,1)S(1)}, u32[]{:S(2)}) copy-start(bf16[32,1024]{1,0:T(8,128)(2,1)S(1)} %get-tuple-element.46) | copy-start | bytes 196612

commit v13 on v12

--- a/solution.py
+++ b/solution.py
@@ -111,9 +111,23 @@
     )(gates, tokens)
 
 
-def add_kernel(scale, own_ref, right_ref, left_ref, far_ref, out_ref):
+def join_kernel(own_ref, share_ref, out_ref):
+    out_ref[...] = own_ref[...] + share_ref[...].astype(F32)
+
+
+def join_shares(own, share):
+    return pl.pallas_call(
+        join_kernel,
+        in_specs=[IN_VMEM] * 2,
+        out_specs=IN_VMEM,
+        out_shape=jax.ShapeDtypeStruct((128, 1024), F32),
+        compiler_params=params(),
+    )(own, share)
+
+
+def add_kernel(scale, own_ref, right_ref, far_ref, out_ref):
     total = own_ref[...]
-    for ref in (right_ref, left_ref, far_ref):
+    for ref in (right_ref, far_ref):
         total += ref[...].astype(F32)
     out_ref[...] = (total * scale).T.astype(BF16)
 
@@ -121,37 +135,47 @@
 def add_shares(own, away, scale):
     return pl.pallas_call(
         functools.partial(add_kernel, scale),
-        in_specs=[IN_VMEM] * 4,
+        in_specs=[IN_VMEM] * 3,
         out_specs=IN_VMEM,
         out_shape=jax.ShapeDtypeStruct((1024, 128), BF16),
         compiler_params=params(),
     )(own, *away)
 
 
-def partial_kernel(rows_ref, mine_ref, other_ref, out_ref, rows):
+def partial_kernel(rows_ref, mine_ref, other_ref, out_hbm, rows, total_ref, sems):
+    copies = []
     x, c = lax.axis_index("x"), lax.axis_index("c")
     for k in range(8):
         turn = ((0,) + TURNS)[k % 4]
         source = jnp.bitwise_and(x + turn, 3) * 2 + (c if k < 4 else 1 - c)
         for m in range(4):
             rows[m * 128 : (m + 1) * 128, k * 128 : (k + 1) * 128] = rows_ref[m, source]
-    for t in range(2):
-        columns = pl.ds(t * 512, 512)
+    for t in range(4):
+        columns = pl.ds(t * 256, 256)
         total = jnp.dot(
-            rows[:, :512], mine_ref[:, :, columns].reshape(512, 512), preferred_element_type=F32
+            rows[:, :512], mine_ref[:, :, columns].reshape(512, 256), preferred_element_type=F32
         )
         total += jnp.dot(
-            rows[:, 512:], other_ref[:, :, columns].reshape(512, 512), preferred_element_type=F32
+            rows[:, 512:], other_ref[:, :, columns].reshape(512, 256), preferred_element_type=F32
         )
-        out_ref[:, columns] = total.astype(BF16)
+        total_ref[:, columns] = total.astype(BF16)
+        copy = pltpu.make_async_copy(total_ref.at[:, columns], out_hbm.at[:, columns], sems.at[t])
+        copy.start()
+        copies.append(copy)
+    for copy in copies:
+        copy.wait()
 
 
 def partial_product(rows, mine, other):
     return pl.pallas_call(
         partial_kernel,
         in_specs=[IN_VMEM] * 3,
-        out_specs=IN_VMEM,
-        scratch_shapes=[pltpu.VMEM((512, 1024), BF16)],
+        out_specs=IN_HBM,
+        scratch_shapes=[
+            pltpu.VMEM((512, 1024), BF16),
+            pltpu.VMEM((512, 1024), BF16),
+            pltpu.SemaphoreType.DMA((4,)),
+        ],
         out_shape=jax.ShapeDtypeStruct((512, 1024), BF16),
         compiler_params=params(),
         cost_estimate=pl.CostEstimate(flops=1 << 30, bytes_accessed=4 << 20, transcendentals=0),
@@ -194,15 +218,15 @@
     right, left, far = shares
     right, far = shift(right, "mp", 4, -1), shift(far, "mp", 4, 2)
 
-    def exchange(rows, left, *mine):
+    def exchange(rows, own, left, *mine):
         mine = jnp.stack(mine)
         partial_sums = partial_product(rows, mine, shift(mine, "c", 2, 1))
         pieces = lax.all_to_all(partial_sums.reshape(16, 32, 1024), ("zl", "y"), 0, 0, tiled=True)
-        return sum_pieces(pieces), shift(left, "mp", 4, 1)
-
-    grad_tokens, left = always(exchange, rows, left, gates, *mine)
-    grad_tokens, own, right, left, far = lax.optimization_barrier((grad_tokens, own, right, left, far))
-    return (grad_tokens.T, add_shares(own, (right, left, far), norm_factor))
+        return sum_pieces(pieces), join_shares(own, shift(left, "mp", 4, 1))
+
+    grad_tokens, own = always(exchange, rows, own, left, gates, *mine)
+    grad_tokens, own, right, far = lax.optimization_barrier((grad_tokens, own, right, far))
+    return (grad_tokens.T, add_shares(own, (right, far), norm_factor))
 
 
 def solution(mesh):

time: 92.9 us -> 93 us (level)
  starting transfers between devices: 51.4 us -> 52.8 us
  Pallas kernels: 12.5 us -> 11.2 us
    ppermute x7, waiting for transfers between devices: 4.48 us -> 14.8 us  [shift(): lax.ppermute(array, axis, [((i + by) % size, i) for i in range(size)])]
    all_to_all x1, waiting for transfers between devices: 23.1 us -> 12.8 us  [exchange(): lax.all_to_all(partial_sums.reshape(16, 32, 1024), ('zl', 'y'), 0, 0, til...]
    all_to_all x1, starting transfers between devices: 11.8 us -> 13 us  [exchange(): lax.all_to_all(partial_sums.reshape(16, 32, 1024), ('zl', 'y'), 0, 0, til...]
    pallas_call x1, Pallas kernels: 1.85 us -> 0.87 us  [add_shares(): pl.pallas_call(functools.partial(add_kernel, scale), in_specs=[IN_VMEM] *...]
    pallas_call x1 -> x2, Pallas kernels: 2.25 us -> 2.27 us  [the longest x1 2.22 us: partial_product(): pl.pallas_call(partial_kernel, in_specs=[IN_VMEM] * 3, out_specs=IN_HBM,...]
  transfers between devices with their start and end apart: 9 -> 9, of which waited for: 3 -> 4; matrix products, arithmetic and copies ran while one was open for 0% -> 0% of each run, Pallas kernels for 9% -> 9%
where the time goes in v13:
time: 93 us; the launch traced here: 92.5 us
  starting transfers between devices  52.8 us (57%)
  waiting for transfers between devices  27.6 us (30%)
  Pallas kernels  11.2 us (12%)
    ppermute x7, starting transfers between devices, shift(): lax.ppermute(array, axis, [((i + by) % size, i) for i in range(size)])  26.6 us
    ppermute x7, waiting for transfers between devices, shift(): lax.ppermute(array, axis, [((i + by) % size, i) for i in range(size)])  14.8 us
    all_to_all x1, starting transfers between devices, body(): lax.all_to_all(rows, ('mp', 'x', 'c'), 0, 0, tiled=True)  13.2 us
    all_to_all x1, starting transfers between devices, exchange(): lax.all_to_all(partial_sums.reshape(16, 32, 1024), ('zl', 'y'), 0, 0, til...  13 us
    all_to_all x1, waiting for transfers between devices, exchange(): lax.all_to_all(partial_sums.reshape(16, 32, 1024), ('zl', 'y'), 0, 0, til...  12.8 us
    pallas_call x1, Pallas kernels, weight_shares(): pl.pallas_call(share_kernel, in_specs=[IN_VMEM, IN_HBM], out_specs=[IN_VM...  4.38 us
    pallas_call x1, Pallas kernels, partial_product(): pl.pallas_call(partial_kernel, in_specs=[IN_VMEM] * 3, out_specs=IN_HBM,...  2.22 us
    pallas_call x1, Pallas kernels, spread_rows(): pl.pallas_call(spread_kernel, in_specs=[IN_HBM], out_specs=IN_HBM, scratc...  1.99 us
  transfers between devices with their start and end apart: 9, of which 4 were waited for; matrix products, arithmetic and copies ran while one was open for 0% of the time, Pallas kernels for 9%

profile of v13, /device:TPU:8, one launch (start us, length us, event | category | flops | bytes accessed | tf_op | source)
XLA Modules:
  0.0 92.5 jit_solution(9526167356462664292)
XLA Ops:
  0.6 2.0 %shard_map.68 = bf16[4,8,128,128]{3,2,1,0:T(8,128)(2,1)} custom-call(bf16[1024,128]{1,0:T(8,128)(2,1)} %weight_hbm.1), custom_call_target="tpu_custom_call" | custom-call | tf_op jit(solution)/shard_map/pallas_call | solution.py:40
  2.6 13.2 %all-to-all-start.1 = ((bf16[32,128,128]{2,1,0:T(8,128)(2,1)}), bf16[32,128,128]{2,1,0:T(8,128)(2,1)S(1)}, u32[]{:S(2)}, u32[]{:S(2)}) async-start(bf16[32,128,128]{2,1,0:T(8,128)(2,1)} %bitcast.8), calls=%async_computation.1 | async-start | bytes 2097152 | tf_op jit(solution)/shard_map/all_to_all | solution.py:212
  15.8 1.5 %shard_map.69.gates_ref = bf16[128,1024]{1,0:T(8,128)(2,1)S(1)} custom-call(bf16[1024,128]{1,0:T(8,128)(2,1)} %gate_hbm.1, bf16[1024,128]{1,0:T(8,128)(2,1)} %up_hbm.1, bf16[1024,128]{1,0:T(8,128)(2,1)} %hidden_hbm.1), custom_call_target="tpu_custom_call" | custom-call | tf_op jit(solution)/shard_map/pallas_call | solution.py:74
  17.3 4.9 %collective-permute-start.2 = (bf16[128,1024]{1,0:T(8,128)(2,1)S(1)}, bf16[128,1024]{1,0:T(8,128)(2,1)S(1)}, u32[]{:S(2)}, u32[]{:S(2)}) collective-permute-start(bf16[128,1024]{1,0:T(8,128)(2,1)S(1)} %shard_map.69.gates_ref), channel_id=1, source_target_pairs={{8,0},{16,8},{24,16},{0,24},{9,1},{17,9},{25,17},{1,25},{10,2},{18... | collective-permute-start | bytes 786440 | tf_op jit(solution)/shard_map/ppermute | solution.py:18
  22.3 1.9 %collective-permute-start.3 = (bf16[128,1024]{1,0:T(8,128)(2,1)S(1)}, bf16[128,1024]{1,0:T(8,128)(2,1)S(1)}, u32[]{:S(2)}, u32[]{:S(2)}) collective-permute-start(bf16[128,1024]{1,0:T(8,128)(2,1)S(1)} %shard_map.69.gates_ref), channel_id=1, source_target_pairs={{24,0},{0,8},{8,16},{16,24},{25,1},{1,9},{9,17},{17,25},{26,2},{2,... | collective-permute-start | bytes 786440 | tf_op jit(solution)/shard_map/ppermute | solution.py:18
  24.2 4.2 %collective-permute-start.4 = (bf16[128,1024]{1,0:T(8,128)(2,1)S(1)}, bf16[128,1024]{1,0:T(8,128)(2,1)S(1)}, u32[]{:S(2)}, u32[]{:S(2)}) collective-permute-start(bf16[128,1024]{1,0:T(8,128)(2,1)S(1)} %shard_map.69.gates_ref), channel_id=1, source_target_pairs={{16,0},{24,8},{0,16},{8,24},{17,1},{25,9},{1,17},{9,25},{18,2},{26... | collective-permute-start | bytes 786440 | tf_op jit(solution)/shard_map/ppermute | solution.py:18
  28.4 4.4 %shard_map.70 = (f32[128,1024]{1,0:T(8,128)S(1)}, bf16[128,1024]{1,0:T(8,128)(2,1)}, bf16[128,1024]{1,0:T(8,128)(2,1)S(1)}, bf16[128,1024]{1,0:T(8,128)(2,1)}) custom-call(bf16[128,1024]{1,0:T(8,128)(2,1)S(1)} %shard_map.69.gates_ref, bf16[1024,4096]{1,0:T(8,128)(2,1)} %tokens_hbm.1), custom_call_target="tpu_custom_call" | custom-call | flops 1073741824 | bytes 10485760 | tf_op jit(solution)/shard_map/pallas_call | solution.py:102
  32.8 4.3 %collective-permute-start.5 = (bf16[128,1024]{1,0:T(8,128)(2,1)}, bf16[128,1024]{1,0:T(8,128)(2,1)S(1)}, u32[]{:S(2)}, u32[]{:S(2)}) collective-permute-start(bf16[128,1024]{1,0:T(8,128)(2,1)} %get-tuple-element.46), channel_id=1, source_target_pairs={{3,0},{0,1},{1,2},{2,3},{7,4},{4,5},{5,6},{6,7},{11,8},{8,9},{9,10... | collective-permute-start | bytes 786440 | tf_op jit(solution)/shard_map/ppermute | solution.py:18
  37.1 5.6 %collective-permute-start.6 = (bf16[128,1024]{1,0:T(8,128)(2,1)}, bf16[128,1024]{1,0:T(8,128)(2,1)S(1)}, u32[]{:S(2)}, u32[]{:S(2)}) collective-permute-start(bf16[128,1024]{1,0:T(8,128)(2,1)} %get-tuple-element.47), channel_id=1, source_target_pairs={{2,0},{3,1},{0,2},{1,3},{6,4},{7,5},{4,6},{5,7},{10,8},{11,9},{8,1... | collective-permute-start | bytes 786440 | tf_op jit(solution)/shard_map/ppermute | solution.py:18
  42.6 0.0 collective-permute-done.2
  42.6 2.3 %collective-permute-done.3 = bf16[128,1024]{1,0:T(8,128)(2,1)S(1)} collective-permute-done((bf16[128,1024]{1,0:T(8,128)(2,1)S(1)}, bf16[128,1024]{1,0:T(8,128)(2,1)S(1)}, u32[]{:S(2)}, u32[]{:S(2)}) %collective-permute-start.3) | collective-permute-done | bytes 262176 | tf_op jit(solution)/shard_map/ppermute | solution.py:18
  44.9 0.0 collective-permute-done.4
  45.0 0.0 all-to-all-done.1
  45.0 46.6 %conditional.1 = (bf16[32,1024]{1,0:T(8,128)(2,1)S(1)}, f32[128,1024]{1,0:T(8,128)S(1)}) conditional(s32[]{:T(128)} %convert_element_type.3, () %tuple.18, (bf16[32,128,128]{2,1,0:T(8,128)(2,1)S(1)}, bf16[128,1024]{1,0:T(8,128)(2,1)S(1)}, bf16[128,1024]{1,0:T(8,128)(2,1)S(1)}, bf16[128,1024]{1,0:T(8,128)(2,1)S(1)}, bf16[128,1024]{1,0:T(8,128)(2,1)S(1)}, ...), branch_computations={%region_0.0_spmd, %region_1.0_spmd} | conditional | flops 1075314688 | bytes 14680192 | solution.py:205
  45.0 0.1 pad_maximum_fusion.mine_ref
  45.1 1.9 %collective-permute-start = (bf16[4,128,1024]{2,1,0:T(8,128)(2,1)S(1)}, bf16[4,128,1024]{2,1,0:T(8,128)(2,1)S(1)}, u32[]{:S(2)}, u32[]{:S(2)}) collective-permute-start(bf16[4,128,1024]{2,1,0:T(8,128)(2,1)S(1)} %pad_maximum_fusion.mine_ref), channel_id=1, source_target_pairs={{4,0},{0,4},{5,1},{1,5},{6,2},{2,6},{7,3},{3,7},{12,8},{8,12},{13,... | collective-permute-start | bytes 3145736 | tf_op jit(solution)/shard_map/cond/branch_1_fun/ppermute | solution.py:18
  47.0 2.6 %collective-permute-done.other_ref = bf16[4,128,1024]{2,1,0:T(8,128)(2,1)S(1)} collective-permute-done((bf16[4,128,1024]{2,1,0:T(8,128)(2,1)S(1)}, bf16[4,128,1024]{2,1,0:T(8,128)(2,1)S(1)}, u32[]{:S(2)}, u32[]{:S(2)}) %collective-permute-start) | collective-permute-done | bytes 1048608 | tf_op jit(solution)/shard_map/cond/branch_1_fun/ppermute | solution.py:18
  49.6 2.2 %branch_1_fun.3 = bf16[512,1024]{1,0:T(8,128)(2,1)} custom-call(bf16[4,8,128,128]{3,2,1,0:T(8,128)(2,1)S(1)} %bitcast.9, bf16[4,128,1024]{2,1,0:T(8,128)(2,1)S(1)} %pad_maximum_fusion.mine_ref, bf16[4,128,1024]{2,1,0:T(8,128)(2,1)S(1)} %collective-permute-done.other_ref), custom_call_target="tpu_custom_call" | custom-call | flops 1073741824 | bytes 4194304 | tf_op jit(solution)/shard_map/cond/branch_1_fun/pallas_call | solution.py:170
  51.9 13.0 %all-to-all-start = ((bf16[16,32,1024]{2,1,0:T(8,128)(2,1)}), bf16[16,32,1024]{2,1,0:T(8,128)(2,1)S(1)}, u32[]{:S(2)}, u32[]{:S(2)}) async-start(bf16[16,32,1024]{2,1,0:T(8,128)(2,1)} %bitcast.5), calls=%async_computation | async-start | bytes 2097152 | tf_op jit(solution)/shard_map/cond/branch_1_fun/all_to_all | solution.py:224
  64.9 3.8 %collective-permute-start.1 = (bf16[128,1024]{1,0:T(8,128)(2,1)S(1)}, bf16[128,1024]{1,0:T(8,128)(2,1)S(1)}, u32[]{:S(2)}, u32[]{:S(2)}) collective-permute-start(bf16[128,1024]{1,0:T(8,128)(2,1)S(1)} %get-tuple-element.21), channel_id=1, source_target_pairs={{1,0},{2,1},{3,2},{0,3},{5,4},{6,5},{7,6},{4,7},{9,8},{10,9},{11,1... | collective-permute-start | bytes 786440 | tf_op jit(solution)/shard_map/cond/branch_1_fun/ppermute | solution.py:18
  68.7 9.8 %collective-permute-done.1.share_ref = bf16[128,1024]{1,0:T(8,128)(2,1)S(1)} collective-permute-done((bf16[128,1024]{1,0:T(8,128)(2,1)S(1)}, bf16[128,1024]{1,0:T(8,128)(2,1)S(1)}, u32[]{:S(2)}, u32[]{:S(2)}) %collective-permute-start.1) | collective-permute-done | bytes 262176 | tf_op jit(solution)/shard_map/cond/branch_1_fun/ppermute | solution.py:18
  78.6 12.8 %all-to-all-done.pieces_ref = bf16[16,32,1024]{2,1,0:T(8,128)(2,1)S(1)} async-done(((bf16[16,32,1024]{2,1,0:T(8,128)(2,1)}), bf16[16,32,1024]{2,1,0:T(8,128)(2,1)S(1)}, u32[]{:S(2)}, u32[]{:S(2)}) %all-to-all-start) | async-done | bytes 1048608 | tf_op jit(solution)/shard_map/cond/branch_1_fun/all_to_all | solution.py:224
  91.4 0.1 branch_1_fun.4
  91.6 0.0 copy-start
  91.6 0.0 collective-permute-done.5.right_ref
  91.6 0.0 collective-permute-done.6.far_ref
  91.6 0.9 shard_map.71
  92.5 0.0 copy-done
  (1 shorter events, 0.0 us)
Async XLA Ops:
  2.6 42.3 %all-to-all-start.1 = ((bf16[32,128,128]{2,1,0:T(8,128)(2,1)}), bf16[32,128,128]{2,1,0:T(8,128)(2,1)S(1)}, u32[]{:S(2)}, u32[]{:S(2)}) async-start(bf16[32,128,128]{2,1,0:T(8,128)(2,1)} %bitcast.8), calls=%async_computation.1 | async-start | bytes 2097152 | tf_op jit(solution)/shard_map/all_to_all | solution.py:212
  17.3 25.3 %collective-permute-start.2 = (bf16[128,1024]{1,0:T(8,128)(2,1)S(1)}, bf16[128,1024]{1,0:T(8,128)(2,1)S(1)}, u32[]{:S(2)}, u32[]{:S(2)}) collective-permute-start(bf16[128,1024]{1,0:T(8,128)(2,1)S(1)} %shard_map.69.gates_ref), channel_id=1, source_target_pairs={{8,0},{16,8},{24,16},{0,24},{9,1},{17,9},{25,17},{1,25},{10,2},{18... | collective-permute-start | bytes 786440 | tf_op jit(solution)/shard_map/ppermute | solution.py:18
  22.3 22.7 %collective-permute-start.3 = (bf16[128,1024]{1,0:T(8,128)(2,1)S(1)}, bf16[128,1024]{1,0:T(8,128)(2,1)S(1)}, u32[]{:S(2)}, u32[]{:S(2)}) collective-permute-start(bf16[128,1024]{1,0:T(8,128)(2,1)S(1)} %shard_map.69.gates_ref), channel_id=1, source_target_pairs={{24,0},{0,8},{8,16},{16,24},{25,1},{1,9},{9,17},{17,25},{26,2},{2,... | collective-permute-start | bytes 786440 | tf_op jit(solution)/shard_map/ppermute | solution.py:18
  24.2 20.8 %collective-permute-start.4 = (bf16[128,1024]{1,0:T(8,128)(2,1)S(1)}, bf16[128,1024]{1,0:T(8,128)(2,1)S(1)}, u32[]{:S(2)}, u32[]{:S(2)}) collective-permute-start(bf16[128,1024]{1,0:T(8,128)(2,1)S(1)} %shard_map.69.gates_ref), channel_id=1, source_target_pairs={{16,0},{24,8},{0,16},{8,24},{17,1},{25,9},{1,17},{9,25},{18,2},{26... | collective-permute-start | bytes 786440 | tf_op jit(solution)/shard_map/ppermute | solution.py:18
  32.8 58.8 %collective-permute-start.5 = (bf16[128,1024]{1,0:T(8,128)(2,1)}, bf16[128,1024]{1,0:T(8,128)(2,1)S(1)}, u32[]{:S(2)}, u32[]{:S(2)}) collective-permute-start(bf16[128,1024]{1,0:T(8,128)(2,1)} %get-tuple-element.46), channel_id=1, source_target_pairs={{3,0},{0,1},{1,2},{2,3},{7,4},{4,5},{5,6},{6,7},{11,8},{8,9},{9,10... | collective-permute-start | bytes 786440 | tf_op jit(solution)/shard_map/ppermute | solution.py:18
  37.1 54.5 %collective-permute-start.6 = (bf16[128,1024]{1,0:T(8,128)(2,1)}, bf16[128,1024]{1,0:T(8,128)(2,1)S(1)}, u32[]{:S(2)}, u32[]{:S(2)}) collective-permute-start(bf16[128,1024]{1,0:T(8,128)(2,1)} %get-tuple-element.47), channel_id=1, source_target_pairs={{2,0},{3,1},{0,2},{1,3},{6,4},{7,5},{4,6},{5,7},{10,8},{11,9},{8,1... | collective-permute-start | bytes 786440 | tf_op jit(solution)/shard_map/ppermute | solution.py:18
  45.1 4.6 %collective-permute-start = (bf16[4,128,1024]{2,1,0:T(8,128)(2,1)S(1)}, bf16[4,128,1024]{2,1,0:T(8,128)(2,1)S(1)}, u32[]{:S(2)}, u32[]{:S(2)}) collective-permute-start(bf16[4,128,1024]{2,1,0:T(8,128)(2,1)S(1)} %pad_maximum_fusion.mine_ref), channel_id=1, source_target_pairs={{4,0},{0,4},{5,1},{1,5},{6,2},{2,6},{7,3},{3,7},{12,8},{8,12},{13,... | collective-permute-start | bytes 3145736 | tf_op jit(solution)/shard_map/cond/branch_1_fun/ppermute | solution.py:18
  51.9 39.5 %all-to-all-start = ((bf16[16,32,1024]{2,1,0:T(8,128)(2,1)}), bf16[16,32,1024]{2,1,0:T(8,128)(2,1)S(1)}, u32[]{:S(2)}, u32[]{:S(2)}) async-start(bf16[16,32,1024]{2,1,0:T(8,128)(2,1)} %bitcast.5), calls=%async_computation | async-start | bytes 2097152 | tf_op jit(solution)/shard_map/cond/branch_1_fun/all_to_all | solution.py:224
  64.9 13.7 %collective-permute-start.1 = (bf16[128,1024]{1,0:T(8,128)(2,1)S(1)}, bf16[128,1024]{1,0:T(8,128)(2,1)S(1)}, u32[]{:S(2)}, u32[]{:S(2)}) collective-permute-start(bf16[128,1024]{1,0:T(8,128)(2,1)S(1)} %get-tuple-element.21), channel_id=1, source_target_pairs={{1,0},{2,1},{3,2},{0,3},{5,4},{6,5},{7,6},{4,7},{9,8},{10,9},{11,1... | collective-permute-start | bytes 786440 | tf_op jit(solution)/shard_map/cond/branch_1_fun/ppermute | solution.py:18
  91.6 0.9 copy-start

commit v14 on v12

--- a/solution.py
+++ b/solution.py
@@ -7,7 +7,7 @@
 from jax.experimental.pallas import tpu as pltpu
 from jax.sharding import Mesh, PartitionSpec as P
 
-TURNS = (1, 3, 2)
+TURNS = (2, 1, 3)
 AXES = ("zl", "y", "x", "c", "mp")
 BF16, F32 = jnp.bfloat16, jnp.float32
 IN_HBM = pl.BlockSpec(memory_space=pltpu.HBM)

time: 92.9 us -> 95.6 us (1.029)
  starting transfers between devices: 51.4 us -> 55.1 us
  waiting for transfers between devices: 27.5 us -> 26.5 us
    all_to_all x1, starting transfers between devices: 11.8 us -> 16.3 us  [exchange(): lax.all_to_all(partial_sums.reshape(16, 32, 1024), ('zl', 'y'), 0, 0, til...]
    ppermute x7, waiting for transfers between devices: 4.48 us -> 2.58 us  [shift(): lax.ppermute(array, axis, [((i + by) % size, i) for i in range(size)])]
where the time goes in v14:
time: 95.6 us; the launch traced here: 95 us
  starting transfers between devices  55.1 us (58%)
  waiting for transfers between devices  26.5 us (28%)
  Pallas kernels  12.5 us (13%)
    ppermute x7, starting transfers between devices, shift(): lax.ppermute(array, axis, [((i + by) % size, i) for i in range(size)])  25.6 us
    all_to_all x1, waiting for transfers between devices, exchange(): lax.all_to_all(partial_sums.reshape(16, 32, 1024), ('zl', 'y'), 0, 0, til...  23.9 us
    all_to_all x1, starting transfers between devices, exchange(): lax.all_to_all(partial_sums.reshape(16, 32, 1024), ('zl', 'y'), 0, 0, til...  16.3 us
    all_to_all x1, starting transfers between devices, body(): lax.all_to_all(rows, ('mp', 'x', 'c'), 0, 0, tiled=True)  13.2 us
    pallas_call x1, Pallas kernels, weight_shares(): pl.pallas_call(share_kernel, in_specs=[IN_VMEM, IN_HBM], out_specs=[IN_VM...  4.7 us
    ppermute x7, waiting for transfers between devices, shift(): lax.ppermute(array, axis, [((i + by) % size, i) for i in range(size)])  2.58 us
    pallas_call x1, Pallas kernels, partial_product(): pl.pallas_call(partial_kernel, in_specs=[IN_VMEM] * 3, out_specs=IN_VMEM,...  2.25 us
    pallas_call x1, Pallas kernels, spread_rows(): pl.pallas_call(spread_kernel, in_specs=[IN_HBM], out_specs=IN_HBM, scratc...  1.99 us
  transfers between devices with their start and end apart: 9, of which 3 were waited for; matrix products, arithmetic and copies ran while one was open for 0% of the time, Pallas kernels for 9%

profile of v14, /device:TPU:8, one launch (start us, length us, event | category | flops | bytes accessed | tf_op | source)
XLA Modules:
  0.0 95.0 jit_solution(17767551762399198014)
XLA Ops:
  0.6 2.0 %shard_map.68 = bf16[4,8,128,128]{3,2,1,0:T(8,128)(2,1)} custom-call(bf16[1024,128]{1,0:T(8,128)(2,1)} %weight_hbm.1), custom_call_target="tpu_custom_call" | custom-call | tf_op jit(solution)/shard_map/pallas_call | solution.py:40
  2.6 13.2 %all-to-all-start.1 = ((bf16[32,128,128]{2,1,0:T(8,128)(2,1)}), bf16[32,128,128]{2,1,0:T(8,128)(2,1)S(1)}, u32[]{:S(2)}, u32[]{:S(2)}) async-start(bf16[32,128,128]{2,1,0:T(8,128)(2,1)} %bitcast.8), calls=%async_computation.1 | async-start | bytes 2097152 | tf_op jit(solution)/shard_map/all_to_all | solution.py:188
  15.8 1.5 %shard_map.69.gates_ref = bf16[128,1024]{1,0:T(8,128)(2,1)S(1)} custom-call(bf16[1024,128]{1,0:T(8,128)(2,1)} %gate_hbm.1, bf16[1024,128]{1,0:T(8,128)(2,1)} %up_hbm.1, bf16[1024,128]{1,0:T(8,128)(2,1)} %hidden_hbm.1), custom_call_target="tpu_custom_call" | custom-call | tf_op jit(solution)/shard_map/pallas_call | solution.py:74
  17.3 5.2 %collective-permute-start.2 = (bf16[128,1024]{1,0:T(8,128)(2,1)S(1)}, bf16[128,1024]{1,0:T(8,128)(2,1)S(1)}, u32[]{:S(2)}, u32[]{:S(2)}) collective-permute-start(bf16[128,1024]{1,0:T(8,128)(2,1)S(1)} %shard_map.69.gates_ref), channel_id=1, source_target_pairs={{16,0},{24,8},{0,16},{8,24},{17,1},{25,9},{1,17},{9,25},{18,2},{26... | collective-permute-start | bytes 786440 | tf_op jit(solution)/shard_map/ppermute | solution.py:18
  22.5 3.1 %collective-permute-start.3 = (bf16[128,1024]{1,0:T(8,128)(2,1)S(1)}, bf16[128,1024]{1,0:T(8,128)(2,1)S(1)}, u32[]{:S(2)}, u32[]{:S(2)}) collective-permute-start(bf16[128,1024]{1,0:T(8,128)(2,1)S(1)} %shard_map.69.gates_ref), channel_id=1, source_target_pairs={{8,0},{16,8},{24,16},{0,24},{9,1},{17,9},{25,17},{1,25},{10,2},{18... | collective-permute-start | bytes 786440 | tf_op jit(solution)/shard_map/ppermute | solution.py:18
  25.6 2.8 %collective-permute-start.4 = (bf16[128,1024]{1,0:T(8,128)(2,1)S(1)}, bf16[128,1024]{1,0:T(8,128)(2,1)S(1)}, u32[]{:S(2)}, u32[]{:S(2)}) collective-permute-start(bf16[128,1024]{1,0:T(8,128)(2,1)S(1)} %shard_map.69.gates_ref), channel_id=1, source_target_pairs={{24,0},{0,8},{8,16},{16,24},{25,1},{1,9},{9,17},{17,25},{26,2},{2,... | collective-permute-start | bytes 786440 | tf_op jit(solution)/shard_map/ppermute | solution.py:18
  28.4 4.7 %shard_map.70 = (f32[128,1024]{1,0:T(8,128)}, bf16[128,1024]{1,0:T(8,128)(2,1)}, bf16[128,1024]{1,0:T(8,128)(2,1)S(1)}, bf16[128,1024]{1,0:T(8,128)(2,1)}) custom-call(bf16[128,1024]{1,0:T(8,128)(2,1)S(1)} %shard_map.69.gates_ref, bf16[1024,4096]{1,0:T(8,128)(2,1)} %tokens_hbm.1), custom_call_target="tpu_custom_call" | custom-call | flops 1073741824 | bytes 10485760 | tf_op jit(solution)/shard_map/pallas_call | solution.py:102
  33.1 0.0 copy-start
  33.1 4.4 %collective-permute-start.5 = (bf16[128,1024]{1,0:T(8,128)(2,1)}, bf16[128,1024]{1,0:T(8,128)(2,1)S(1)}, u32[]{:S(2)}, u32[]{:S(2)}) collective-permute-start(bf16[128,1024]{1,0:T(8,128)(2,1)} %get-tuple-element.43), channel_id=1, source_target_pairs={{3,0},{0,1},{1,2},{2,3},{7,4},{4,5},{5,6},{6,7},{11,8},{8,9},{9,10... | collective-permute-start | bytes 786440 | tf_op jit(solution)/shard_map/ppermute | solution.py:18
  37.5 5.5 %collective-permute-start.6 = (bf16[128,1024]{1,0:T(8,128)(2,1)}, bf16[128,1024]{1,0:T(8,128)(2,1)S(1)}, u32[]{:S(2)}, u32[]{:S(2)}) collective-permute-start(bf16[128,1024]{1,0:T(8,128)(2,1)} %get-tuple-element.45), channel_id=1, source_target_pairs={{2,0},{3,1},{0,2},{1,3},{6,4},{7,5},{4,6},{5,7},{10,8},{11,9},{8,1... | collective-permute-start | bytes 786440 | tf_op jit(solution)/shard_map/ppermute | solution.py:18
  43.1 0.0 collective-permute-done.2
  43.1 0.0 collective-permute-done.3
  43.1 0.1 collective-permute-done.4
  43.2 0.0 all-to-all-done.1
  43.2 49.9 %conditional.1 = (bf16[32,1024]{1,0:T(8,128)(2,1)S(1)}, bf16[128,1024]{1,0:T(8,128)(2,1)}) conditional(s32[]{:T(128)} %convert_element_type.3, () %tuple.18, (bf16[32,128,128]{2,1,0:T(8,128)(2,1)S(1)}, bf16[128,1024]{1,0:T(8,128)(2,1)S(1)}, bf16[128,1024]{1,0:T(8,128)(2,1)S(1)}, bf16[128,1024]{1,0:T(8,128)(2,1)S(1)}, bf16[128,1024]{1,0:T(8,128)(2,1)S(1)}, ...), branch_computations={%region_0.0_spmd, %region_1.0_spmd} | conditional | flops 1075314688 | bytes 14680192 | solution.py:181
  43.2 0.1 pad_maximum_fusion.mine_ref
  43.3 2.0 %collective-permute-start = (bf16[4,128,1024]{2,1,0:T(8,128)(2,1)S(1)}, bf16[4,128,1024]{2,1,0:T(8,128)(2,1)S(1)}, u32[]{:S(2)}, u32[]{:S(2)}) collective-permute-start(bf16[4,128,1024]{2,1,0:T(8,128)(2,1)S(1)} %pad_maximum_fusion.mine_ref), channel_id=1, source_target_pairs={{4,0},{0,4},{5,1},{1,5},{6,2},{2,6},{7,3},{3,7},{12,8},{8,12},{13,... | collective-permute-start | bytes 3145736 | tf_op jit(solution)/shard_map/cond/branch_1_fun/ppermute | solution.py:18
  45.3 2.5 %collective-permute-done.other_ref = bf16[4,128,1024]{2,1,0:T(8,128)(2,1)S(1)} collective-permute-done((bf16[4,128,1024]{2,1,0:T(8,128)(2,1)S(1)}, bf16[4,128,1024]{2,1,0:T(8,128)(2,1)S(1)}, u32[]{:S(2)}, u32[]{:S(2)}) %collective-permute-start) | collective-permute-done | bytes 1048608 | tf_op jit(solution)/shard_map/cond/branch_1_fun/ppermute | solution.py:18
  47.9 2.2 %branch_1_fun.2 = bf16[512,1024]{1,0:T(8,128)(2,1)} custom-call(bf16[4,8,128,128]{3,2,1,0:T(8,128)(2,1)S(1)} %bitcast.9, bf16[4,128,1024]{2,1,0:T(8,128)(2,1)S(1)} %pad_maximum_fusion.mine_ref, bf16[4,128,1024]{2,1,0:T(8,128)(2,1)S(1)} %collective-permute-done.other_ref), custom_call_target="tpu_custom_call" | custom-call | flops 1073741824 | bytes 4194304 | tf_op jit(solution)/shard_map/cond/branch_1_fun/pallas_call | solution.py:150
  50.1 16.3 %all-to-all-start = ((bf16[16,32,1024]{2,1,0:T(8,128)(2,1)}), bf16[16,32,1024]{2,1,0:T(8,128)(2,1)S(1)}, u32[]{:S(2)}, u32[]{:S(2)}) async-start(bf16[16,32,1024]{2,1,0:T(8,128)(2,1)} %bitcast.5), calls=%async_computation | async-start | bytes 2097152 | tf_op jit(solution)/shard_map/cond/branch_1_fun/all_to_all | solution.py:200
  66.4 2.6 %collective-permute-start.1 = (bf16[128,1024]{1,0:T(8,128)(2,1)S(1)}, bf16[128,1024]{1,0:T(8,128)(2,1)}, u32[]{:S(2)}, u32[]{:S(2)}) collective-permute-start(bf16[128,1024]{1,0:T(8,128)(2,1)S(1)} %get-tuple-element.18), channel_id=1, source_target_pairs={{1,0},{2,1},{3,2},{0,3},{5,4},{6,5},{7,6},{4,7},{9,8},{10,9},{11,1... | collective-permute-start | bytes 786440 | tf_op jit(solution)/shard_map/cond/branch_1_fun/ppermute | solution.py:18
  69.0 23.9 %all-to-all-done.pieces_ref = bf16[16,32,1024]{2,1,0:T(8,128)(2,1)S(1)} async-done(((bf16[16,32,1024]{2,1,0:T(8,128)(2,1)}), bf16[16,32,1024]{2,1,0:T(8,128)(2,1)S(1)}, u32[]{:S(2)}, u32[]{:S(2)}) %all-to-all-start) | async-done | bytes 1048608 | tf_op jit(solution)/shard_map/cond/branch_1_fun/all_to_all | solution.py:200
  92.9 0.1 branch_1_fun.3
  93.1 0.0 collective-permute-done.1
  93.1 0.0 copy-start.1
  93.1 0.0 collective-permute-done.5.right_ref
  93.1 0.0 collective-permute-done.6.far_ref
  93.1 0.0 copy-done
  93.1 1.9 %shard_map.71 = bf16[1024,128]{1,0:T(8,128)(2,1)} custom-call(f32[128,1024]{1,0:T(8,128)S(1)} %copy-done, bf16[128,1024]{1,0:T(8,128)(2,1)S(1)} %collective-permute-done.5.right_ref, bf16[128,1024]{1,0:T(8,128)(2,1)} %get-tuple-element.49.left_ref, bf16[128,1024]{1,0:T(8,128)(2,1)S(1)} %collective-permute-done.6.far_ref), custom_call_target="tpu_custom_call" | custom-call | tf_op jit(solution)/shard_map/pallas_call | solution.py:122
  95.0 0.0 copy-done.1
Async XLA Ops:
  2.6 40.5 %all-to-all-start.1 = ((bf16[32,128,128]{2,1,0:T(8,128)(2,1)}), bf16[32,128,128]{2,1,0:T(8,128)(2,1)S(1)}, u32[]{:S(2)}, u32[]{:S(2)}) async-start(bf16[32,128,128]{2,1,0:T(8,128)(2,1)} %bitcast.8), calls=%async_computation.1 | async-start | bytes 2097152 | tf_op jit(solution)/shard_map/all_to_all | solution.py:188
  17.3 25.8 %collective-permute-start.2 = (bf16[128,1024]{1,0:T(8,128)(2,1)S(1)}, bf16[128,1024]{1,0:T(8,128)(2,1)S(1)}, u32[]{:S(2)}, u32[]{:S(2)}) collective-permute-start(bf16[128,1024]{1,0:T(8,128)(2,1)S(1)} %shard_map.69.gates_ref), channel_id=1, source_target_pairs={{16,0},{24,8},{0,16},{8,24},{17,1},{25,9},{1,17},{9,25},{18,2},{26... | collective-permute-start | bytes 786440 | tf_op jit(solution)/shard_map/ppermute | solution.py:18
  22.5 20.6 %collective-permute-start.3 = (bf16[128,1024]{1,0:T(8,128)(2,1)S(1)}, bf16[128,1024]{1,0:T(8,128)(2,1)S(1)}, u32[]{:S(2)}, u32[]{:S(2)}) collective-permute-start(bf16[128,1024]{1,0:T(8,128)(2,1)S(1)} %shard_map.69.gates_ref), channel_id=1, source_target_pairs={{8,0},{16,8},{24,16},{0,24},{9,1},{17,9},{25,17},{1,25},{10,2},{18... | collective-permute-start | bytes 786440 | tf_op jit(solution)/shard_map/ppermute | solution.py:18
  25.6 17.5 %collective-permute-start.4 = (bf16[128,1024]{1,0:T(8,128)(2,1)S(1)}, bf16[128,1024]{1,0:T(8,128)(2,1)S(1)}, u32[]{:S(2)}, u32[]{:S(2)}) collective-permute-start(bf16[128,1024]{1,0:T(8,128)(2,1)S(1)} %shard_map.69.gates_ref), channel_id=1, source_target_pairs={{24,0},{0,8},{8,16},{16,24},{25,1},{1,9},{9,17},{17,25},{26,2},{2,... | collective-permute-start | bytes 786440 | tf_op jit(solution)/shard_map/ppermute | solution.py:18
  33.1 60.0 %copy-start = (f32[128,1024]{1,0:T(8,128)S(1)}, f32[128,1024]{1,0:T(8,128)}, u32[]{:S(2)}) copy-start(f32[128,1024]{1,0:T(8,128)} %get-tuple-element.47.own_ref) | copy-start | bytes 1572868
  33.1 60.0 %collective-permute-start.5 = (bf16[128,1024]{1,0:T(8,128)(2,1)}, bf16[128,1024]{1,0:T(8,128)(2,1)S(1)}, u32[]{:S(2)}, u32[]{:S(2)}) collective-permute-start(bf16[128,1024]{1,0:T(8,128)(2,1)} %get-tuple-element.43), channel_id=1, source_target_pairs={{3,0},{0,1},{1,2},{2,3},{7,4},{4,5},{5,6},{6,7},{11,8},{8,9},{9,10... | collective-permute-start | bytes 786440 | tf_op jit(solution)/shard_map/ppermute | solution.py:18
  37.5 55.6 %collective-permute-start.6 = (bf16[128,1024]{1,0:T(8,128)(2,1)}, bf16[128,1024]{1,0:T(8,128)(2,1)S(1)}, u32[]{:S(2)}, u32[]{:S(2)}) collective-permute-start(bf16[128,1024]{1,0:T(8,128)(2,1)} %get-tuple-element.45), channel_id=1, source_target_pairs={{2,0},{3,1},{0,2},{1,3},{6,4},{7,5},{4,6},{5,7},{10,8},{11,9},{8,1... | collective-permute-start | bytes 786440 | tf_op jit(solution)/shard_map/ppermute | solution.py:18
  43.3 4.6 %collective-permute-start = (bf16[4,128,1024]{2,1,0:T(8,128)(2,1)S(1)}, bf16[4,128,1024]{2,1,0:T(8,128)(2,1)S(1)}, u32[]{:S(2)}, u32[]{:S(2)}) collective-permute-start(bf16[4,128,1024]{2,1,0:T(8,128)(2,1)S(1)} %pad_maximum_fusion.mine_ref), channel_id=1, source_target_pairs={{4,0},{0,4},{5,1},{1,5},{6,2},{2,6},{7,3},{3,7},{12,8},{8,12},{13,... | collective-permute-start | bytes 3145736 | tf_op jit(solution)/shard_map/cond/branch_1_fun/ppermute | solution.py:18
  50.1 42.8 %all-to-all-start = ((bf16[16,32,1024]{2,1,0:T(8,128)(2,1)}), bf16[16,32,1024]{2,1,0:T(8,128)(2,1)S(1)}, u32[]{:S(2)}, u32[]{:S(2)}) async-start(bf16[16,32,1024]{2,1,0:T(8,128)(2,1)} %bitcast.5), calls=%async_computation | async-start | bytes 2097152 | tf_op jit(solution)/shard_map/cond/branch_1_fun/all_to_all | solution.py:200
  66.4 26.7 %collective-permute-start.1 = (bf16[128,1024]{1,0:T(8,128)(2,1)S(1)}, bf16[128,1024]{1,0:T(8,128)(2,1)}, u32[]{:S(2)}, u32[]{:S(2)}) collective-permute-start(bf16[128,1024]{1,0:T(8,128)(2,1)S(1)} %get-tuple-element.18), channel_id=1, source_target_pairs={{1,0},{2,1},{3,2},{0,3},{5,4},{6,5},{7,6},{4,7},{9,8},{10,9},{11,1... | collective-permute-start | bytes 786440 | tf_op jit(solution)/shard_map/cond/branch_1_fun/ppermute | solution.py:18
  93.1 1.9 %copy-start.1 = (bf16[32,1024]{1,0:T(8,128)(2,1)}, bf16[32,1024]{1,0:T(8,128)(2,1)S(1)}, u32[]{:S(2)}) copy-start(bf16[32,1024]{1,0:T(8,128)(2,1)S(1)} %get-tuple-element.46) | copy-start | bytes 196612
